TPU v7x, 32 devices: a whole 2x2x4 slice. The times are simulated.
32 devices in a mesh: dp: 8 (over y, x, core), seq: 4 (over z).
Axes of the slice: x: 2, y: 2, z: 4, core: 2. Of those that a mesh axis runs over, the one named last changes fastest.
Arguments:
- latents: bfloat16 [2, 16, 256, 768], P(None, 'dp', 'seq'), may hold values from -6 to 6
- conditions: bfloat16 [2, 16, 768], P(None, 'dp'), may hold values from -6 to 6
- modulator: bfloat16 [768, 4608], P('dp', 'seq'), may hold values from -0.21875 to 0.21875
- modbias: bfloat16 [4608], P('seq'), may hold values from -3 to 3
- qkvweight: bfloat16 [768, 2304], P('dp', 'seq'), may hold values from -0.21875 to 0.21875
- querybias: bfloat16 [768], P('seq'), may hold values from -3 to 3
- valuebias: bfloat16 [768], P('seq'), may hold values from -3 to 3
- projection: bfloat16 [768, 768], P('dp', 'seq'), may hold values from -0.875 to 0.875
- projbias: bfloat16 [768], P('seq'), may hold values from -3 to 3
- expand: bfloat16 [768, 3072], P('dp', 'seq'), may hold values from -0.21875 to 0.21875
- expandbias: bfloat16 [3072], P('seq'), may hold values from -3 to 3
- contract: bfloat16 [3072, 768], P('dp', 'seq'), may hold values from -0.109375 to 0.109375
- contractbias: bfloat16 [768], P('seq'), may hold values from -3 to 3
- cotangent: bfloat16 [2, 16, 256, 768], P(None, 'dp', 'seq'), may hold values from -6 to 6
Outputs:
- result: bfloat16 [2, 16, 256, 768], P(None, 'dp', 'seq')
- latents_grad: bfloat16 [2, 16, 256, 768], P(None, 'dp', 'seq')
- conditions_grad: float32 [2, 16, 768], P(None, 'dp')
- modulator_grad: float32 [768, 4608], P('dp', 'seq')
- modbias_grad: float32 [4608], P('seq')
- qkvweight_grad: float32 [768, 2304], P('dp', 'seq')
- querybias_grad: float32 [768], P('seq')
- valuebias_grad: float32 [768], P('seq')
- projection_grad: float32 [768, 768], P('dp', 'seq')
- projbias_grad: float32 [768], P('seq')
- expand_grad: float32 [768, 3072], P('dp', 'seq')
- expandbias_grad: float32 [3072], P('seq')
- contract_grad: float32 [3072, 768], P('dp', 'seq')
- contractbias_grad: float32 [768], P('seq')
All inputs are finite; a program needn't handle non-finite values.
Results may differ from a plain program's by a relative error of at most 0.04.
Values may be sent and summed in bfloat16 or wider, within the bound.
No kernel may reach another device: no remote copies, remote signals or barrier semaphores. Data moves between devices by JAX's collectives and lax.ppermute only.
A program may use at most 128 MiB of HBM per device.

v0:
```python
import functools

import jax
import jax.numpy as jnp
from jax import lax
from jax.experimental import pallas as pl
from jax.experimental.pallas import tpu as pltpu
from jax.sharding import PartitionSpec as P

H = 12
EPSILON = 1e-06
BF = jnp.bfloat16
F32 = jnp.float32


def bits_of(count):
    bits = count.bit_length() - 1
    assert 1 << bits == count
    return bits


def swap(values, axis, bit):
    count = lax.axis_size(axis)
    return lax.ppermute(values, axis, [(i, i ^ (1 << bit)) for i in range(count)])


def own_bit(axis, bit):
    return (lax.axis_index(axis) >> bit) & 1


def halve(values, axis, bit):
    index = own_bit(axis, bit)
    sent = lax.dynamic_index_in_dim(values, 1 - index, 0, keepdims=False)
    kept = lax.dynamic_index_in_dim(values, index, 0, keepdims=False)
    other = swap(sent.astype(BF), axis, bit)
    return kept.astype(F32) + other.astype(F32)


def scatter_seq(values):
    count = bits_of(lax.axis_size("seq"))
    shape = values.shape[1:]
    values = values.reshape((2,) * count + shape)
    values = values.transpose(list(range(count - 1, -1, -1)) + list(range(count, count + len(shape))))
    for bit in range(count):
        values = halve(values, "seq", bit)
    return values


class Layout:
    def __init__(self, n_dp, rows, width):
        self.direct = rows % 16 == 0 and n_dp == 8
        self.blocks = n_dp if self.direct else 1
        self.rows = rows if self.direct else width


def mask_of(place, order):
    return sum(((place >> j) & 1) << bit for j, bit in enumerate(order))


def gather_dp(units):
    part = units[None]
    order = list(range(bits_of(lax.axis_size("dp"))))[::-1]
    for bit in order:
        part = jnp.concatenate([part, swap(part, "dp", bit)], axis=0)
    count = part.shape[0]
    place = [0] * count
    for index in range(count):
        place[mask_of(index, order)] = index
    wanted = jnp.asarray(place)[jnp.arange(count) ^ lax.axis_index("dp")]
    return jnp.take(part, wanted, axis=0)


def scatter_dp(values):
    count = bits_of(values.shape[0])
    values = jnp.take(values, jnp.arange(1 << count) ^ lax.axis_index("dp"), axis=0)
    values = values.reshape((2,) * count + values.shape[1:]).astype(F32)
    for bit in range(count - 1, -1, -1):
        values = values[0] + swap(values[1].astype(BF), "dp", bit).astype(F32)
    return values


def gather_square(units):
    middle = units.shape[0] // 2
    over_x, over_y = swap(units, "dp", 1), swap(units, "dp", 2)
    low = swap(over_x[:middle], "dp", 2)
    high = swap(over_y[middle:], "dp", 1)
    near = [(units, 0, 0), (over_x, 2, 0), (over_y, 4, 0), (low, 6, 0), (high, 6, middle)]
    far = [(swap(part, "dp", 0), mask | 1, first) for part, mask, first in near]
    return [entry for pair in zip(near, far) for entry in pair]


def scatter_square(kept, sent):
    other = swap(sent, "dp", 0)
    middle = kept.shape[1] // 2
    both = lambda place, units: kept[place, units].astype(F32) + other[place, units].astype(F32)
    low, high, every = slice(0, middle), slice(middle, None), slice(0, None)
    low_in = swap(both(3, low).astype(BF), "dp", 2)
    high_in = swap(both(3, high).astype(BF), "dp", 1)
    to_x = jnp.concatenate([both(1, low) + low_in.astype(F32), both(1, high)]).astype(BF)
    to_y = jnp.concatenate([both(2, low), both(2, high) + high_in.astype(F32)]).astype(BF)
    return (kept, other, swap(to_x, "dp", 1), swap(to_y, "dp", 2))


def swap_seq(values):
    count = lax.axis_size("seq")
    return [
        lax.ppermute(values[mask - 1] if isinstance(values, list) else values, "seq",
                     [(i, i ^ mask) for i in range(count)])
        for mask in range(1, count)
    ]


def dot(a, b):
    return jnp.dot(a, b, preferred_element_type=F32)


def dot_back(a, b):
    return lax.dot_general(a, b, (((1,), (1,)), ((), ())), preferred_element_type=F32)


def dot_outer(a, b):
    return lax.dot_general(a, b, (((0,), (0,)), ((), ())), preferred_element_type=F32)


def normalize(values):
    center = values - jnp.mean(values, axis=-1, keepdims=True)
    inverse = lax.rsqrt(jnp.mean(center * center, axis=-1, keepdims=True) + EPSILON)
    return (center * inverse, inverse)


def norm_back(grad_normed, normed, inverse):
    first = jnp.mean(grad_normed, axis=-1, keepdims=True)
    second = jnp.mean(grad_normed * normed, axis=-1, keepdims=True)
    return inverse * (grad_normed - first - normed * second)


def total(values):
    return jnp.sum(values.astype(F32), axis=0, keepdims=True)


def loads(pieces, refs, me, target, span, sems):
    copies = []
    for ref, (mask, first) in zip(refs, pieces):
        low, high = max(span[0], first), min(span[1], first + ref.shape[0])
        if low < high:
            view = target(me ^ mask, low - span[0], high - span[0])
            copies.append(
                pltpu.make_async_copy(ref.at[low - first : high - first], view, sems.at[len(copies)])
            )
    return copies


def start(copies):
    for copy in copies:
        copy.start()


def finish(copies):
    for copy in copies:
        copy.wait()


def by_unit(scratch):
    return lambda block, low, high: scratch.at[low:high, block]


def by_block(scratch):
    return lambda block, low, high: scratch.at[block, low:high]


def matrix_of(scratch, unit):
    block = scratch[unit]
    return block.reshape(block.shape[0] * block.shape[1], block.shape[2])


def stores(scratch, outs, me, units, sems, base):
    copies = []
    blocks = scratch.shape[0]
    for mask in range(blocks):
        out = outs[mask & 1] if blocks > 1 else outs[0]
        place = mask >> 1
        copies.append(
            pltpu.make_async_copy(
                scratch.at[me ^ mask], out.at[place, units[0] : units[1]], sems.at[base + len(copies)]
            )
        )
    return copies


def lanes(shape):
    return lax.broadcasted_iota(jnp.int32, shape, 1)


def attend_kernel(spec, me_ref, tokens_ref, mod_ref, qkv_off_ref, proj_off_ref, *rest):
    width, pieces, factor, pairs = spec
    refs, rest = rest[: len(pieces)], rest[len(pieces) :]
    hidden_ref, qkv_ref, att_ref, branch_ref, middle_ref, weights, sems = rest
    me = me_ref[0]
    copies = loads(pieces, refs, me, by_unit(weights), (0, 4), sems)
    start(copies)
    tokens = tokens_ref[...].astype(F32)
    part = lambda i: mod_ref[:, i * width : (i + 1) * width]
    normed, _ = normalize(tokens)
    hidden = (normed * (1.0 + part(1)) + part(0)).astype(BF)
    hidden_ref[...] = hidden
    finish(copies)
    for unit in range(3):
        offset = qkv_off_ref[:, unit * width : (unit + 1) * width]
        qkv_ref[unit] = (dot(hidden, matrix_of(weights, unit)) + offset).astype(BF)
    for pair in range(pairs):
        cols = slice(pair * 128, (pair + 1) * 128)
        q, k, v = qkv_ref[0, :, cols], qkv_ref[1, :, cols], qkv_ref[2, :, cols]
        first = lanes(k.shape) < 64
        mixed = []
        for which in range(2):
            masked = jnp.where(first if which == 0 else ~first, k, jnp.zeros_like(k))
            scores = dot_back(q, masked) * factor
            expo = jnp.exp(scores - jnp.max(scores, axis=-1, keepdims=True))
            probs = expo * (1.0 / jnp.sum(expo, axis=-1, keepdims=True))
            mixed.append(dot(probs.astype(BF), v))
        att_ref[:, cols] = jnp.where(first, mixed[0], mixed[1]).astype(BF)
    branch = dot(att_ref[...], matrix_of(weights, 3)) + proj_off_ref[...]
    branch_ref[...] = branch
    middle_ref[...] = tokens + part(2) * branch


GELU_C = 0.7978845608028654
GELU_A = 0.044715


def mlp_kernel(spec, me_ref, middle_ref, mod_ref, cot_ref, up_off_ref, down_off_ref, *rest):
    width, wide, pieces = spec
    refs, rest = rest[: len(pieces)], rest[len(pieces) :]
    outs, rest = rest[: len(rest) - 14], rest[len(rest) - 14 :]
    (
        result_ref, dbefore_ref, gate_ref, up_bias_ref, down_bias_ref,
        up, down, up_grad, down_grad, active, slope, up_sems, down_sems, out_sems,
    ) = rest
    me = me_ref[0]
    up_copies = loads(pieces, refs, me, by_unit(up), (0, wide), up_sems)
    down_copies = loads(pieces, refs, me, by_block(down), (wide, 2 * wide), down_sems)
    start(up_copies)
    start(down_copies)
    part = lambda i: mod_ref[:, i * width : (i + 1) * width]
    middle = middle_ref[...]
    cot = cot_ref[...].astype(F32)
    normed, _ = normalize(middle)
    hidden = (normed * (1.0 + part(4)) + part(3)).astype(BF)
    gate = part(5)
    dbranch = (gate * cot).astype(BF)
    down_bias_ref[...] = total(dbranch)
    finish(up_copies)
    for unit in range(wide):
        before = dot(hidden, matrix_of(up, unit)) + up_off_ref[:, unit * width : (unit + 1) * width]
        square = before * before
        bent = jnp.tanh(GELU_C * before * (1.0 + GELU_A * square))
        active[unit] = (0.5 * before * (1.0 + bent)).astype(BF)
        slope[unit] = 0.5 * (1.0 + bent) + (0.5 * GELU_C) * before * (1.0 - bent * bent) * (
            1.0 + (3.0 * GELU_A) * square
        )
    finish(down_copies)
    down_rows = down[...].reshape(wide * width, width)
    grads = down_grad.shape
    span = grads[0] // wide if grads[0] > 1 else 0
    branch = down_off_ref[...]
    for unit in range(wide):
        branch = branch + dot(active[unit], down_rows[unit * width : (unit + 1) * width])
        grad = dot_outer(active[unit], dbranch).astype(BF)
        if span:
            down_grad[unit * span : (unit + 1) * span] = grad.reshape((span,) + grads[1:])
        else:
            down_grad[0, unit] = grad
    down_stores = stores(down_grad, outs, me, (wide, 2 * wide), out_sems, 0)
    start(down_stores)
    result_ref[...] = (middle + gate * branch).astype(BF)
    gate_ref[...] = total(cot * branch)
    for unit in range(wide):
        dactive = dot_back(dbranch, down_rows[unit * width : (unit + 1) * width])
        dbefore = (dactive * slope[unit]).astype(BF)
        dbefore_ref[unit] = dbefore
        up_bias_ref[:, unit * width : (unit + 1) * width] = total(dbefore)
        grad = dot_outer(hidden, dbefore).astype(BF)
        up_grad[:, unit] = grad.reshape(up_grad.shape[0], up_grad.shape[2], width)
    up_stores = stores(up_grad, outs, me, (0, wide), out_sems, up_grad.shape[0])
    start(up_stores)
    finish(down_stores)
    finish(up_stores)


def attend_back_kernel(spec, me_ref, middle_ref, mod_ref, cot_ref, dbefore_ref, branch_ref, att_ref,
                       hidden_ref, qkv_ref, *rest):
    width, wide, up_pieces, pieces, factor, pairs = spec
    up_refs, rest = rest[: len(up_pieces)], rest[len(up_pieces) :]
    refs, rest = rest[: len(pieces)], rest[len(pieces) :]
    outs, rest = rest[: len(rest) - 10], rest[len(rest) - 10 :]
    dmiddle_ref, dqkv_ref, sums_ref, bias_ref, up, proj, grads, up_sems, proj_sems, out_sems = rest
    me = me_ref[0]
    up_copies = loads(up_pieces, up_refs, me, by_unit(up), (0, wide), up_sems)
    proj_copies = loads(pieces, refs, me, by_unit(proj), (3, 4), proj_sems)
    start(up_copies)
    start(proj_copies)
    part = lambda i: mod_ref[:, i * width : (i + 1) * width]
    normed, inverse = normalize(middle_ref[...])
    finish(up_copies)
    dhidden = dot_back(dbefore_ref[0], matrix_of(up, 0))
    for unit in range(1, wide):
        dhidden = dhidden + dot_back(dbefore_ref[unit], matrix_of(up, unit))
    dmiddle = cot_ref[...].astype(F32) + norm_back(dhidden * (1.0 + part(4)), normed, inverse)
    dmiddle_ref[...] = dmiddle
    dbranch = (part(2) * dmiddle).astype(BF)
    sums_ref[:, :width] = total(dmiddle * branch_ref[...])
    sums_ref[:, width : 2 * width] = total(dhidden)
    sums_ref[:, 2 * width : 3 * width] = total(dhidden * normed)
    bias_ref[:, 2 * width : 3 * width] = total(dbranch)
    finish(proj_copies)
    datt = dot_back(dbranch, matrix_of(proj, 0)).astype(BF)
    for pair in range(pairs):
        cols = slice(pair * 128, (pair + 1) * 128)
        q, k, v = qkv_ref[0, :, cols], qkv_ref[1, :, cols], qkv_ref[2, :, cols]
        da = datt[:, cols]
        first = lanes(k.shape) < 64
        zero = jnp.zeros_like(k)
        grad_q, grad_k, grad_v = [], [], []
        for which in range(2):
            own = first if which == 0 else ~first
            scores = dot_back(q, jnp.where(own, k, zero)) * factor
            expo = jnp.exp(scores - jnp.max(scores, axis=-1, keepdims=True))
            probs = expo * (1.0 / jnp.sum(expo, axis=-1, keepdims=True))
            dprobs = dot_back(da, jnp.where(own, v, zero))
            rowsum = jnp.sum(dprobs * probs, axis=-1, keepdims=True)
            dscores = (probs * (dprobs - rowsum)).astype(BF)
            grad_q.append(dot(dscores, k))
            grad_k.append(dot_outer(dscores, q))
            grad_v.append(dot_outer(probs.astype(BF), da))
        dqkv_ref[0, :, cols] = (jnp.where(first, grad_q[0], grad_q[1]) * factor).astype(BF)
        dqkv_ref[1, :, cols] = (jnp.where(first, grad_k[0], grad_k[1]) * factor).astype(BF)
        dqkv_ref[2, :, cols] = jnp.where(first, grad_v[0], grad_v[1]).astype(BF)
    bias_ref[:, :width] = total(dqkv_ref[0])
    bias_ref[:, width : 2 * width] = total(dqkv_ref[2])
    shape = (grads.shape[0], grads.shape[2], width)
    for unit in range(3):
        grads[:, unit] = dot_outer(hidden_ref[...], dqkv_ref[unit]).astype(BF).reshape(shape)
    grads[:, 3] = dot_outer(att_ref[...], dbranch).astype(BF).reshape(shape)
    out_copies = stores(grads, outs, me, (0, 4), out_sems, 0)
    start(out_copies)
    finish(out_copies)


def input_back_kernel(spec, me_ref, tokens_ref, mod_ref, dmiddle_ref, dqkv_ref, *rest):
    width, pieces = spec
    refs, rest = rest[: len(pieces)], rest[len(pieces) :]
    dtokens_ref, sums_ref, weights, sems = rest
    copies = loads(pieces, refs, me_ref[0], by_unit(weights), (0, 3), sems)
    start(copies)
    normed, inverse = normalize(tokens_ref[...].astype(F32))
    finish(copies)
    dhidden = dot_back(dqkv_ref[0], matrix_of(weights, 0))
    for unit in range(1, 3):
        dhidden = dhidden + dot_back(dqkv_ref[unit], matrix_of(weights, unit))
    sums_ref[:, :width] = total(dhidden)
    sums_ref[:, width : 2 * width] = total(dhidden * normed)
    scale = 1.0 + mod_ref[:, width : 2 * width]
    dtokens_ref[...] = (dmiddle_ref[...] + norm_back(dhidden * scale, normed, inverse)).astype(BF)


def chunks(width, chunk, wide):
    table = []
    for seq in range(width // chunk):
        entry = []
        for j in range(3):
            index = 3 * seq + j
            per = width // chunk
            entry.append((index // per, index % per * chunk, j * chunk, chunk))
        entry.append((3, seq * chunk, 3 * chunk, chunk))
        table.append(entry)
    return table


def pick(refs, me, seq):
    value = refs[0][...]
    for mask in range(1, len(refs)):
        value = jnp.where((me ^ seq) == mask, refs[mask][...], value)
    return value


def spread1_kernel(spec, me_ref, *refs):
    width, chunk, rows, n_seq = spec
    blocks, (units_ref, qkv_off_ref, proj_off_ref, up_off_ref, down_off_ref) = refs[:n_seq], refs[n_seq:]
    me = me_ref[0]
    qkv_off_ref[...] = jnp.zeros_like(qkv_off_ref)
    for seq, entry in enumerate(chunks(width, chunk, 0)):
        value = pick(blocks, me, seq)
        for unit, there, here, columns in entry:
            units_ref[unit, :, there : there + columns] = value[:rows, here : here + columns]
        tail = value[rows:].astype(F32)
        for index, ref in enumerate((qkv_off_ref, qkv_off_ref, proj_off_ref, down_off_ref)):
            at = seq * chunk + (2 * width if index == 1 else 0)
            ref[:, at : at + chunk] = tail[0:1, index * chunk : (index + 1) * chunk]
        up_off_ref[:, seq * width : (seq + 1) * width] = tail[1:2]


def spread2_kernel(spec, me_ref, *refs):
    width, chunk, wide, n_seq = spec
    blocks, units_ref = refs[:n_seq], refs[n_seq]
    me = me_ref[0]
    for seq in range(n_seq):
        value = pick(blocks, me, seq)
        units_ref[seq] = value[0]
        for unit in range(wide):
            units_ref[wide + unit, :, seq * chunk : (seq + 1) * chunk] = value[
                1, :, unit * chunk : (unit + 1) * chunk
            ]


def summed(refs, unit):
    kept, other, over_x, over_y = refs
    value = kept[0, unit].astype(F32) + other[0, unit].astype(F32)
    return value + (over_x[unit].astype(F32) + over_y[unit].astype(F32))


def send_blocks(scratch, outs, me, sems):
    copies = [
        pltpu.make_async_copy(scratch.at[me ^ mask], out, sems.at[mask]) for mask, out in enumerate(outs)
    ]
    start(copies)
    finish(copies)


def collect1_kernel(spec, me_ref, *refs):
    width, chunk, wide, n_seq = spec
    ins, outs, (scratch, sems) = refs[:4], refs[4 : 4 + n_seq], refs[4 + n_seq :]
    table = chunks(width, chunk, wide)
    for unit in range(4):
        value = summed(ins, unit).astype(BF)
        for seq, entry in enumerate(table):
            for source, there, here, columns in entry:
                if source == unit:
                    scratch[seq, :, here : here + columns] = value[:, there : there + columns]
    send_blocks(scratch, outs, me_ref[0], sems)


def collect2_kernel(spec, me_ref, *refs):
    width, chunk, wide, n_seq = spec
    ins, outs, (scratch, sems) = refs[:4], refs[4 : 4 + n_seq], refs[4 + n_seq :]
    for unit in range(wide):
        scratch[unit, 0] = summed(ins, unit).astype(BF)
        value = summed(ins, wide + unit).astype(BF)
        for seq in range(n_seq):
            scratch[seq, 1, :, unit * chunk : (unit + 1) * chunk] = value[:, seq * chunk : (seq + 1) * chunk]
    send_blocks(scratch, outs, me_ref[0], sems)


def final1_kernel(spec, me_ref, *refs):
    width, chunk, wide, n_seq = spec
    value = refs[0][...].astype(F32)
    for ref in refs[1:n_seq]:
        value = value + ref[...].astype(F32)
    qkv_ref, proj_ref = refs[n_seq:]
    qkv_ref[...] = value[:, : 3 * chunk]
    proj_ref[...] = value[:, 3 * chunk :]


def final2_kernel(spec, me_ref, *refs):
    width, chunk, wide, n_seq = spec
    up_ref, down_ref = refs[n_seq:]
    rows = up_ref.shape[0]
    for index in range(2):
        value = refs[0][index].astype(F32)
        for ref in refs[1:n_seq]:
            value = value + ref[index].astype(F32)
        if index == 0:
            up_ref[...] = value
        else:
            for unit in range(wide):
                down_ref[unit * rows : (unit + 1) * rows] = value[:, unit * chunk : (unit + 1) * chunk]


def call(body, spec, me, inputs, pieces, outs, far_outs, scratch, name):
    vmem = pl.BlockSpec(memory_space=pltpu.VMEM)
    far = pl.BlockSpec(memory_space=pl.ANY)
    return pl.pallas_call(
        functools.partial(body, spec),
        out_shape=far_outs + outs,
        in_specs=[pl.BlockSpec(memory_space=pltpu.SMEM)] + [vmem] * len(inputs) + [far] * len(pieces),
        out_specs=[far] * len(far_outs) + [vmem] * len(outs),
        scratch_shapes=scratch,
        compiler_params=pltpu.CompilerParams(vmem_limit_bytes=52 * 1024 * 1024),
        cost_estimate=pl.CostEstimate(flops=0, bytes_accessed=0, transcendentals=0),
        name=name,
    )(me, *inputs, *pieces)


def local(
    latents,
    conditions,
    modulator,
    modbias,
    qkvweight,
    querybias,
    valuebias,
    projection,
    projbias,
    expand,
    expandbias,
    contract,
    contractbias,
    cotangent,
):
    n_dp, n_seq = lax.axis_size("dp"), lax.axis_size("seq")
    micro, lats, tok, width = latents.shape
    held = micro * lats
    assert held == n_seq
    length = n_seq * tok
    rows = width // n_dp
    chunk = width // n_seq
    wide = contract.shape[0] // rows
    head = width // H
    assert 2 * head == 128
    factor = head ** (-0.5)
    layout = Layout(n_dp, rows, width)

    shaped = jax.ShapeDtypeStruct
    dma = pltpu.SemaphoreType.DMA
    here = lax.axis_index("seq").reshape(1).astype(jnp.int32)
    spec_seq = (width, chunk, wide, n_seq)
    offsets_low = jnp.concatenate([querybias, valuebias, projbias, contractbias, expandbias])
    tail = jnp.pad(offsets_low.reshape(-1, width), ((0, 14), (0, 0)))
    shards1 = jnp.concatenate([jnp.concatenate([qkvweight, projection], axis=1), tail])
    down_shard = contract.reshape(wide, rows, chunk)
    shards2 = jnp.stack([expand, jnp.concatenate([down_shard[i] for i in range(wide)], axis=1)])
    blocks1 = [shards1] + swap_seq(shards1)
    blocks2 = [shards2] + swap_seq(shards2)
    offset_shapes = [shaped((1, n), F32) for n in (3 * width, width, wide * width, width)]
    if layout.direct:
        me = lax.axis_index("dp").reshape(1).astype(jnp.int32)
        u1, offsets, proj_offset, up_offset, down_offset = call(
            spread1_kernel, (width, chunk, rows, n_seq), here, blocks1, [],
            [shaped((4, rows, width), BF)] + offset_shapes, [], [], "spread1",
        )
        (u2,) = call(
            spread2_kernel, spec_seq, here, blocks2, [],
            [shaped((2 * wide, rows, width), BF)], [], [], "spread2",
        )
        w1, w2 = gather_square(u1), gather_square(u2)
    else:
        me = jnp.zeros((1,), jnp.int32)
        order = jnp.arange(n_seq) ^ lax.axis_index("seq")
        b1 = jnp.take(jnp.stack(blocks1), order, axis=0)
        b2 = jnp.take(jnp.stack(blocks2), order, axis=0)
        u_qkv = b1[:, :rows, : 3 * chunk].transpose(1, 0, 2).reshape(rows, 3, width).transpose(1, 0, 2)
        u_proj = b1[:, :rows, 3 * chunk :].transpose(1, 0, 2).reshape(1, rows, width)
        u_up = b2[:, 0].transpose(1, 0, 2).reshape(rows, wide, width).transpose(1, 0, 2)
        u_down = b2[:, 1].reshape(n_seq, rows, wide, chunk).transpose(2, 1, 0, 3).reshape(wide, rows, width)
        natural = lambda v: gather_dp(v).transpose(1, 0, 2, 3).reshape(v.shape[0], width, width)
        w1 = [(natural(jnp.concatenate([u_qkv, u_proj])), 0, 0)]
        w2 = [(natural(u_up), 0, 0), (gather_dp(u_down).reshape(wide, width, width), 0, wide)]
        four = b1[:, rows].reshape(n_seq, 4, chunk).transpose(1, 0, 2).reshape(4, 1, width).astype(F32)
        offsets = jnp.concatenate([four[0], jnp.zeros_like(four[0]), four[1]], axis=1)
        proj_offset, down_offset = four[2], four[3]
        up_offset = b1[:, rows + 1].reshape(1, -1).astype(F32)
    arrays1, spec1 = [w[0] for w in w1], tuple(w[1:] for w in w1)
    arrays2, spec2 = [w[0] for w in w2], tuple(w[1:] for w in w2)

    def to_latents(values):
        values = values.reshape(held, tok, width)
        return lax.all_to_all(values, "seq", 0, 0, tiled=True).reshape(length, width)

    def to_tokens(*values):
        values = jnp.stack([v.reshape(n_seq, tok, width) for v in values], axis=1)
        values = lax.all_to_all(values, "seq", 0, 0, tiled=True)
        return [values[:, i].reshape(micro, lats, tok, width) for i in range(values.shape[1])]

    tokens = to_latents(latents)
    cot = to_latents(cotangent)

    cond_float = conditions.reshape(held, width).astype(F32)
    cond_act = jax.nn.silu(cond_float).astype(BF)
    cond_rows = lax.all_to_all(
        cond_act.reshape(held, n_dp, rows), "dp", 1, 0, tiled=True
    ).reshape(n_dp * held, rows)
    part = jnp.dot(cond_rows, modulator, preferred_element_type=F32)
    part = part + jnp.where(lax.axis_index("dp") == 0, modbias.astype(F32), 0.0)
    part = lax.all_to_all(part, ("dp", "seq"), 0, 0, tiled=True)
    mod = jnp.sum(part.reshape(n_dp, n_seq, -1), axis=0)
    mod = mod.reshape(1, -1)

    pairs = H // 2
    blocks, block_rows = layout.blocks, layout.rows
    places = max(blocks // 2, 1)
    n_far = min(blocks, 2)
    n1, n2 = len(w1), len(w2)
    hidden1, qkv, attended, branch1, middle = call(
        attend_kernel,
        (width, spec1, factor, pairs),
        me,
        [tokens, mod, offsets, proj_offset],
        arrays1,
        [
            shaped((length, width), BF),
            shaped((3, length, width), BF),
            shaped((length, width), BF),
            shaped((length, width), F32),
            shaped((length, width), F32),
        ],
        [],
        [pltpu.VMEM((4, blocks, block_rows, width), BF), dma((n1,))],
        "attention",
    )
    *grads2, result, dbefore, dgate2, up_bias, down_bias = call(
        mlp_kernel,
        (width, wide, spec2),
        me,
        [middle, mod, cot, up_offset, down_offset],
        arrays2,
        [
            shaped((length, width), BF),
            shaped((wide, length, width), BF),
            shaped((1, width), F32),
            shaped((1, wide * width), F32),
            shaped((1, width), F32),
        ],
        [shaped((places, 2 * wide, block_rows, width), BF)] * n_far,
        [
            pltpu.VMEM((wide, blocks, block_rows, width), BF),
            pltpu.VMEM((blocks, wide, block_rows, width), BF),
            pltpu.VMEM((blocks, wide, block_rows, width), BF),
            pltpu.VMEM((blocks, wide, block_rows, width), BF),
            pltpu.VMEM((wide, length, width), BF),
            pltpu.VMEM((wide, length, width), F32),
            dma((n2,)),
            dma((n2,)),
            dma((2 * blocks,)),
        ],
        "mlp",
    )
    *grads1, dmiddle, dqkv, sums1, bias1 = call(
        attend_back_kernel,
        (width, wide, spec2, spec1, factor, pairs),
        me,
        [middle, mod, cot, dbefore, branch1, attended, hidden1, qkv],
        arrays2 + arrays1,
        [
            shaped((length, width), F32),
            shaped((3, length, width), BF),
            shaped((1, 3 * width), F32),
            shaped((1, 3 * width), F32),
        ],
        [shaped((places, 4, block_rows, width), BF)] * n_far,
        [
            pltpu.VMEM((wide, blocks, block_rows, width), BF),
            pltpu.VMEM((1, blocks, block_rows, width), BF),
            pltpu.VMEM((blocks, 4, block_rows, width), BF),
            dma((n2,)),
            dma((n1,)),
            dma((blocks,)),
        ],
        "attention_back",
    )
    dtokens, sums0 = call(
        input_back_kernel,
        (width, spec1),
        me,
        [tokens, mod, dmiddle, dqkv],
        arrays1,
        [shaped((length, width), BF), shaped((1, 2 * width), F32)],
        [],
        [pltpu.VMEM((3, blocks, block_rows, width), BF), dma((n1,))],
        "input_back",
    )
    result, token_grad = to_tokens(result, dtokens)

    dmod = jnp.concatenate([sums0, sums1, dgate2], axis=1)
    offset_grads = (
        bias1[:, :width], bias1[:, width : 2 * width], bias1[:, 2 * width :], up_bias, down_bias
    )
    offset_grads = jnp.concatenate([g.reshape(n_seq, -1) for g in offset_grads], axis=1)
    small = jnp.concatenate([dmod.reshape(n_seq, -1), offset_grads], axis=1).astype(BF)
    small = jnp.broadcast_to(small[None], (n_dp,) + small.shape).reshape(n_dp * n_seq, -1)
    small = lax.all_to_all(small, ("dp", "seq"), 0, 0, tiled=True)
    cols = modulator.shape[1]
    dmod_all = small[:, :cols]
    offset_sums = jnp.sum(small[:, cols:].astype(F32), axis=0)
    grad_mod = jnp.einsum("ld,ln->dn", cond_rows, dmod_all, preferred_element_type=F32)
    grad_mod_offset = jnp.sum(dmod_all.astype(F32), axis=0)
    dcond_rows = jnp.einsum("ln,dn->ld", dmod_all, modulator, preferred_element_type=F32)
    dcond = jnp.broadcast_to(
        dcond_rows.reshape(n_dp, 1, held, rows), (n_dp, n_seq, held, rows)
    ).reshape(n_dp * n_seq, held, rows)
    dcond = lax.all_to_all(dcond, ("dp", "seq"), 0, 0, tiled=True)
    dcond = jnp.sum(dcond.reshape(n_dp, n_seq, held, rows), axis=1)
    dcond = dcond.transpose(1, 0, 2).reshape(held, width)
    dconds = jax.vjp(jax.nn.silu, cond_float)[1](dcond)[0].reshape(micro, lats, width)

    if layout.direct:
        blocks2 = call(
            collect2_kernel, spec_seq, here, list(scatter_square(*grads2)), [], [],
            [shaped((2, rows, width), BF)] * n_seq,
            [pltpu.VMEM((n_seq, 2, rows, width), BF), dma((n_seq,))], "collect2",
        )
        blocks1 = call(
            collect1_kernel, spec_seq, here, list(scatter_square(*grads1)), [], [],
            [shaped((rows, width), BF)] * n_seq,
            [pltpu.VMEM((n_seq, rows, width), BF), dma((n_seq,))], "collect1",
        )
        up_out, down_out = call(
            final2_kernel, spec_seq, here, [blocks2[0]] + swap_seq(list(blocks2[1:])), [],
            [shaped((rows, width), F32), shaped((wide * rows, chunk), F32)], [], [], "final2",
        )
        qkv_out, proj_out = call(
            final1_kernel, spec_seq, here, [blocks1[0]] + swap_seq(list(blocks1[1:])), [],
            [shaped((rows, 3 * chunk), F32), shaped((rows, chunk), F32)], [], [], "final1",
        )
    else:
        unit_rows = lambda v: v.reshape(-1, n_dp, rows, width).transpose(1, 0, 2, 3)
        s1 = scatter_dp(unit_rows(grads1[0][0]))
        s_up = scatter_dp(unit_rows(grads2[0][0, :wide]))
        s_down = scatter_dp(grads2[0][0, wide:].reshape(n_dp, wide, rows, width))
        t1 = s1[:3].transpose(1, 0, 2).reshape(rows, n_seq, 3 * chunk)
        t1 = jnp.concatenate([t1, s1[3].reshape(rows, n_seq, chunk)], axis=2).transpose(1, 0, 2)
        t2 = s_up.transpose(1, 0, 2).reshape(rows, n_seq, -1).transpose(1, 0, 2)
        t3 = s_down.reshape(wide * rows, n_seq, chunk).transpose(1, 0, 2)
        r1, up_out, down_out = scatter_seq(t1), scatter_seq(t2), scatter_seq(t3)
        qkv_out, proj_out = r1[:, : 3 * chunk], r1[:, 3 * chunk :]
    sizes = [b.shape[0] for b in (querybias, valuebias, projbias, expandbias, contractbias)]
    starts = [sum(sizes[:i]) for i in range(len(sizes))]
    sums = [offset_sums[a : a + n] for a, n in zip(starts, sizes)]
    return (
        result,
        token_grad,
        dconds,
        grad_mod,
        grad_mod_offset,
        qkv_out,
        sums[0],
        sums[1],
        proj_out,
        sums[2],
        up_out,
        sums[3],
        down_out,
        sums[4],
    )


def solution(mesh):
    placed = (
        P(None, "dp", "seq", None),
        P(None, "dp", None),
        P("dp", "seq"),
        P("seq"),
        P("dp", "seq"),
        P("seq"),
        P("seq"),
        P("dp", "seq"),
        P("seq"),
        P("dp", "seq"),
        P("seq"),
        P("dp", "seq"),
        P("seq"),
        P(None, "dp", "seq", None),
    )
    return jax.shard_map(
        local,
        mesh=mesh,
        in_specs=placed,
        out_specs=(
            P(None, "dp", "seq", None),
            P(None, "dp", "seq", None),
            P(None, "dp", None),
            P("dp", "seq"),
            P("seq"),
            P("dp", "seq"),
            P("seq"),
            P("seq"),
            P("dp", "seq"),
            P("seq"),
            P("dp", "seq"),
            P("seq"),
            P("dp", "seq"),
            P("seq"),
        ),
        check_vma=False,
    )
```

profile of v0, /device:TPU:0, one launch (start us, length us, event | category | flops | bytes accessed | tf_op | source)
XLA Modules:
  0.0 315.3 jit_solution(17101532483569668856)
XLA Ops:
  2.6 3.1 collective-permute-start.12
  5.6 2.6 collective-permute-start.13
  9.4 3.5 %collective-permute-start.1 = (bf16[112,768]{1,0:T(8,128)(2,1)S(1)}, bf16[112,768]{1,0:T(8,128)(2,1)S(1)}, u32[]{:S(2)}, u32[]{:S(2)}) collective-permute-start(bf16[112,768]{1,0:T(8,128)(2,1)S(1)} %fusion.14.refs_0_), channel_id=1, source_target_pairs={{0,2},{1,3},{2,0},{3,1},{4,6},{5,7},{6,4},{7,5},{8,10},{9,11},{10,... | collective-permute-start | bytes 516104 | tf_op jit(solution)/shard_map/ppermute | solution.py:107
  12.9 6.1 %collective-permute-done.12.refs_1_ = bf16[2,96,768]{2,1,0:T(8,128)(2,1)S(1)} collective-permute-done((bf16[2,96,768]{2,1,0:T(8,128)(2,1)S(1)}, bf16[2,96,768]{2,1,0:T(8,128)(2,1)S(1)}, u32[]{:S(2)}, u32[]{:S(2)}) %collective-permute-start.12) | collective-permute-done | bytes 294944 | tf_op jit(solution)/shard_map/ppermute | solution.py:107
  19.0 4.6 %collective-permute-start.2 = (bf16[112,768]{1,0:T(8,128)(2,1)S(1)}, bf16[112,768]{1,0:T(8,128)(2,1)S(1)}, u32[]{:S(2)}, u32[]{:S(2)}) collective-permute-start(bf16[112,768]{1,0:T(8,128)(2,1)S(1)} %fusion.14.refs_0_), channel_id=1, source_target_pairs={{0,3},{1,2},{2,1},{3,0},{4,7},{5,6},{6,5},{7,4},{8,11},{9,10},{10,... | collective-permute-start | bytes 516104 | tf_op jit(solution)/shard_map/ppermute | solution.py:107
  23.6 5.5 %collective-permute-done.13.refs_2_ = bf16[2,96,768]{2,1,0:T(8,128)(2,1)S(1)} collective-permute-done((bf16[2,96,768]{2,1,0:T(8,128)(2,1)S(1)}, bf16[2,96,768]{2,1,0:T(8,128)(2,1)S(1)}, u32[]{:S(2)}, u32[]{:S(2)}) %collective-permute-start.13) | collective-permute-done | bytes 294944 | tf_op jit(solution)/shard_map/ppermute | solution.py:107
  30.6 1.5 collective-permute-start.16
  32.1 1.5 collective-permute-start.18
  33.6 12.9 %collective-permute-done.1.refs_2_ = bf16[112,768]{1,0:T(8,128)(2,1)S(1)} collective-permute-done((bf16[112,768]{1,0:T(8,128)(2,1)S(1)}, bf16[112,768]{1,0:T(8,128)(2,1)S(1)}, u32[]{:S(2)}, u32[]{:S(2)}) %collective-permute-start.1) | collective-permute-done | bytes 172064 | tf_op jit(solution)/shard_map/ppermute | solution.py:107
  46.9 1.6 collective-permute-start.6
  48.5 1.5 collective-permute-start.4
  50.0 20.0 %collective-permute-done.6.rest_4_.rest_14_ = bf16[4,96,768]{2,1,0:T(8,128)(2,1)} collective-permute-done((bf16[4,96,768]{2,1,0:T(8,128)(2,1)S(1)}, bf16[4,96,768]{2,1,0:T(8,128)(2,1)}, u32[]{:S(2)}, u32[]{:S(2)}) %collective-permute-start.6) | collective-permute-done | bytes 589856 | tf_op jit(solution)/shard_map/ppermute | solution.py:24
  72.6 1.6 collective-permute-start.8
  74.9 3.3 %all-to-all-start.1 = ((bf16[4,8,96]{2,0,1:T(4,128)(2,1)}), bf16[4,8,96]{2,0,1:T(4,128)(2,1)S(1)}, u32[]{:S(2)}, u32[]{:S(2)}) async-start(bf16[4,8,96]{2,0,1:T(4,128)(2,1)} %copy.110), calls=%async_computation.1 | async-start | bytes 16384 | tf_op jit(solution)/shard_map/all_to_all | solution.py:578
  80.0 2.8 all-to-all-done.1
  83.8 15.5 %all-to-all-start.2 = ((f32[32,1,1152]{2,1,0:T(1,128)}), f32[32,1,1152]{2,1,0:T(1,128)S(1)}, u32[]{:S(2)}, u32[]{:S(2)}) async-start(f32[32,1,1152]{2,1,0:T(1,128)} %copy.111), calls=%async_computation.2 | async-start | bytes 294912 | tf_op jit(solution)/shard_map/all_to_all | solution.py:583
  99.4 2.0 slice.185
  101.4 2.0 slice.186
  103.3 4.7 %all-to-all-done.2 = f32[32,1,1152]{2,1,0:T(1,128)S(1)} async-done(((f32[32,1,1152]{2,1,0:T(1,128)}), f32[32,1,1152]{2,1,0:T(1,128)S(1)}, u32[]{:S(2)}, u32[]{:S(2)}) %all-to-all-start.2) | async-done | bytes 147488 | tf_op jit(solution)/shard_map/all_to_all | solution.py:583
  108.0 3.5 %all-to-all-start = ((bf16[4,64,768]{2,1,0:T(8,128)(2,1)}), bf16[4,64,768]{2,1,0:T(8,128)(2,1)S(1)}, u32[]{:S(2)}, u32[]{:S(2)}) async-start(bf16[4,64,768]{2,1,0:T(8,128)(2,1)} %bitcast.87), calls=%async_computation | async-start | bytes 786432 | tf_op jit(solution)/shard_map/all_to_all | solution.py:566
  114.2 8.5 %all-to-all-done = bf16[4,64,768]{2,1,0:T(8,128)(2,1)S(1)} async-done(((bf16[4,64,768]{2,1,0:T(8,128)(2,1)}), bf16[4,64,768]{2,1,0:T(8,128)(2,1)S(1)}, u32[]{:S(2)}, u32[]{:S(2)}) %all-to-all-start) | async-done | bytes 393248 | tf_op jit(solution)/shard_map/all_to_all | solution.py:566
  122.6 3.5 %all-to-all-start.3 = ((bf16[4,64,768]{2,1,0:T(8,128)(2,1)}), bf16[4,64,768]{2,1,0:T(8,128)(2,1)S(1)}, u32[]{:S(2)}, u32[]{:S(2)}) async-start(bf16[4,64,768]{2,1,0:T(8,128)(2,1)} %bitcast.88), calls=%async_computation.3 | async-start | bytes 786432 | tf_op jit(solution)/shard_map/all_to_all | solution.py:566
  127.5 1.7 collective-permute-done.22.rest_8_
  129.7 7.8 %attention.1 = (bf16[256,768]{1,0:T(8,128)(2,1)S(1)}, bf16[3,256,768]{2,1,0:T(8,128)(2,1)}, bf16[256,768]{1,0:T(8,128)(2,1)S(1)}, f32[256,768]{1,0:T(8,128)}, f32[256,768]{1,0:T(8,128)}) custom-call(s32[1]{0:T(128)} %bitcast.me_ref, bf16[256,768]{1,0:T(8,128)(2,1)} %bitcast.75, f32[1,4608]{1,0:T(1,128)S(1)} %bitcast.77, ...), custom_call_target="tpu_custom_call" | custom-call | tf_op jit(solution)/shard_map/attention/pallas_call | solution.py:481
  138.4 17.0 %mlp.1 = (bf16[4,8,96,768]{3,2,1,0:T(8,128)(2,1)}, bf16[4,8,96,768]{3,2,1,0:T(8,128)(2,1)}, bf16[256,768]{1,0:T(8,128)(2,1)S(1)}, bf16[4,256,768]{2,1,0:T(8,128)...) custom-call(s32[1]{0:T(128)} %bitcast.me_ref, f32[256,768]{1,0:T(8,128)} %get-tuple-element.54.middle_ref, ...), custom_call_target="tpu_custom_call" | custom-call | tf_op jit(solution)/shard_map/mlp/pallas_call | solution.py:481
  155.9 19.4 %attention_back.1 = (bf16[4,4,96,768]{3,2,1,0:T(8,128)(2,1)}, bf16[4,4,96,768]{3,2,1,0:T(8,128)(2,1)}, f32[256,768]{1,0:T(8,128)}, bf16[3,256,768]{2,1,0:T(8,128...) custom-call(s32[1]{0:T(128)} %bitcast.me_ref, f32[256,768]{1,0:T(8,128)} %get-tuple-element.54.middle_ref, ...), custom_call_target="tpu_custom_call" | custom-call | tf_op jit(solution)/shard_map/attention_back/pallas_call | solution.py:481
  175.5 4.6 %input_back.1 = (bf16[256,768]{1,0:T(8,128)(2,1)S(1)}, f32[1,1536]{1,0:T(1,128)S(1)}) custom-call(s32[1]{0:T(128)} %bitcast.me_ref, bf16[256,768]{1,0:T(8,128)(2,1)S(1)} %bitcast.76, f32[1,4608]{1,0:T(1,128)S(1)} %bitcast.80, f32[256,768]{1,0:T(8,128)} %get-tuple-element.63.dmiddle_ref, bf16[3,256,768]{2,1,0:T(8,128)(2,1)} %get-tuple-element.64.dqkv_ref, ...), custom_call_target="tpu_custom_call" | custom-call | tf_op jit(solution)/shard_map/input_back/pallas_call | solution.py:481
  181.5 1.7 reduce.13
  184.0 5.1 %all-to-all-start.5 = ((bf16[32,2,1344]{2,1,0:T(2,128)(2,1)}), bf16[32,2,1344]{2,1,0:T(2,128)(2,1)S(1)}, u32[]{:S(2)}, u32[]{:S(2)}) async-start(bf16[32,2,1344]{2,1,0:T(2,128)(2,1)} %reshape.220), calls=%async_computation.5 | async-start | bytes 360448 | tf_op jit(solution)/shard_map/all_to_all | solution.py:679
  190.1 8.1 %all-to-all-done.5 = bf16[32,2,1344]{2,1,0:T(2,128)(2,1)S(1)} async-done(((bf16[32,2,1344]{2,1,0:T(2,128)(2,1)}), bf16[32,2,1344]{2,1,0:T(2,128)(2,1)S(1)}, u32[]{:S(2)}, u32[]{:S(2)}) %all-to-all-start.5) | async-done | bytes 172064 | tf_op jit(solution)/shard_map/all_to_all | solution.py:679
  198.5 4.1 %fusion.5 = (bf16[4,96,768]{2,1,0:T(8,128)(2,1)}, bf16[4,96,768]{2,1,0:T(8,128)(2,1)}, bf16[4,96,768]{2,1,0:T(8,128)(2,1)S(1)}, bf16[4,96,768]{2,1,0:T(8,128)(2,1)}) fusion(bf16[4,8,96,768]{3,2,1,0:T(8,128)(2,1)} %collective-permute-done.32.refs_1_, bf16[4,8,96,768]{3,2,1,0:T(8,128)(2,1)} %get-tuple-element.80.refs_0_), kind=kLoop, calls=%fused_computation.15 | loop fusion | flops 4718592 | bytes 7077888 | tf_op jit(solution)/shard_map/add | solution.py:95
  204.8 3.3 %all-to-all-start.6 = ((f32[32,4,96]{2,1,0:T(4,128)}), f32[32,4,96]{2,1,0:T(4,128)S(1)}, u32[]{:S(2)}, u32[]{:S(2)}) async-start(f32[32,4,96]{2,1,0:T(4,128)} %bitcast.19), calls=%async_computation.6 | async-start | bytes 131072 | tf_op jit(solution)/shard_map/all_to_all | solution.py:689
  208.1 2.5 fusion.12
  210.6 1.8 collective-permute-start.25
  212.3 1.5 collective-permute-start.27
  213.8 5.9 %collective-permute-done.33 = bf16[4,96,768]{2,1,0:T(8,128)(2,1)} collective-permute-done((bf16[4,96,768]{2,1,0:T(8,128)(2,1)}, bf16[4,96,768]{2,1,0:T(8,128)(2,1)}, u32[]{:S(2)}, u32[]{:S(2)}) %collective-permute-start.33) | collective-permute-done | bytes 589856 | tf_op jit(solution)/shard_map/ppermute | solution.py:24
  220.5 2.4 fusion.1
  227.2 4.2 %all-to-all-start.4 = ((bf16[4,2,64,768]{3,2,1,0:T(8,128)(2,1)}), bf16[4,2,64,768]{3,2,1,0:T(8,128)(2,1)}, u32[]{:S(2)}, u32[]{:S(2)}) async-start(bf16[4,2,64,768]{3,2,1,0:T(8,128)(2,1)} %pad_maximum_fusion.2), calls=%async_computation.4 | async-start | bytes 1572864 | tf_op jit(solution)/shard_map/all_to_all | solution.py:570
  231.4 1.5 fusion.7
  238.3 24.1 %collective-permute-done.28.refs_3_ = bf16[4,96,768]{2,1,0:T(8,128)(2,1)S(1)} collective-permute-done((bf16[4,96,768]{2,1,0:T(8,128)(2,1)S(1)}, bf16[4,96,768]{2,1,0:T(8,128)(2,1)S(1)}, u32[]{:S(2)}, u32[]{:S(2)}) %collective-permute-start.28) | collective-permute-done | bytes 589856 | tf_op jit(solution)/shard_map/ppermute | solution.py:24
  263.6 3.5 %collect1.1 = (bf16[96,768]{1,0:T(8,128)(2,1)S(1)}, bf16[96,768]{1,0:T(8,128)(2,1)S(1)}, bf16[96,768]{1,0:T(8,128)(2,1)S(1)}, bf16[96,768]{1,0:T(8,128)(2,1)S(1)}) custom-call(s32[1]{0:T(128)} %bitcast.7.me_ref, bf16[4,4,96,768]{3,2,1,0:T(8,128)(2,1)} %get-tuple-element.72.refs_0_, bf16[4,4,96,768]{3,2,1,0:T(8,128)(2,1)} %collective-permute-done.24.refs_1_, ...), custom_call_target="tpu_custom_call" | custom-call | tf_op jit(solution)/shard_map/collect1/pallas_call | solution.py:481
  267.1 2.0 collective-permute-start.29
  269.2 5.4 %collect2.1 = (bf16[2,96,768]{2,1,0:T(8,128)(2,1)S(1)}, bf16[2,96,768]{2,1,0:T(8,128)(2,1)S(1)}, bf16[2,96,768]{2,1,0:T(8,128)(2,1)S(1)}, bf16[2,96,768]{2,1,0:T(8,128)(2,1)S(1)}) custom-call(s32[1]{0:T(128)} %bitcast.7.me_ref, bf16[4,8,96,768]{3,2,1,0:T(8,128)(2,1)} %get-tuple-element.80.refs_0_, bf16[4,8,96,768]{3,2,1,0:T(8,128)(2,1)} %collective-permute-done.32.refs_1_, ...), custom_call_target="tpu_custom_call" | custom-call | tf_op jit(solution)/shard_map/collect2/pallas_call | solution.py:481
  274.7 1.5 collective-permute-start.38
  276.2 2.9 collective-permute-start.39
  279.7 1.5 collective-permute-start.31
  281.2 2.0 fusion.21
  283.3 29.4 %collective-permute-done.30.refs_2_ = bf16[96,768]{1,0:T(8,128)(2,1)S(1)} collective-permute-done((bf16[96,768]{1,0:T(8,128)(2,1)S(1)}, bf16[96,768]{1,0:T(8,128)(2,1)S(1)}, u32[]{:S(2)}, u32[]{:S(2)}) %collective-permute-start.30) | collective-permute-done | bytes 147488 | tf_op jit(solution)/shard_map/ppermute | solution.py:107
  (166 shorter events, 37.4 us)
Async XLA Ops:
  0.6 82.2 %copy-start = (bf16[96,1152]{1,0:T(8,128)(2,1)S(1)}, bf16[96,1152]{1,0:T(8,128)(2,1)}, u32[]{:S(2)}) copy-start(bf16[96,1152]{1,0:T(8,128)(2,1)} %param.16) | copy-start | bytes 663556
  2.6 16.5 %collective-permute-start.12 = (bf16[2,96,768]{2,1,0:T(8,128)(2,1)S(1)}, bf16[2,96,768]{2,1,0:T(8,128)(2,1)S(1)}, u32[]{:S(2)}, u32[]{:S(2)}) collective-permute-start(bf16[2,96,768]{2,1,0:T(8,128)(2,1)S(1)} %pad_maximum_fusion.5.refs_0_), channel_id=1, source_target_pairs={{0,1},{1,0},{2,3},{3,2},{4,5},{5,4},{6,7},{7,6},{8,9},{9,8},{10,11... | collective-permute-start | bytes 884744 | tf_op jit(solution)/shard_map/ppermute | solution.py:107
  5.6 23.5 %collective-permute-start.13 = (bf16[2,96,768]{2,1,0:T(8,128)(2,1)S(1)}, bf16[2,96,768]{2,1,0:T(8,128)(2,1)S(1)}, u32[]{:S(2)}, u32[]{:S(2)}) collective-permute-start(bf16[2,96,768]{2,1,0:T(8,128)(2,1)S(1)} %pad_maximum_fusion.5.refs_0_), channel_id=1, source_target_pairs={{0,2},{1,3},{2,0},{3,1},{4,6},{5,7},{6,4},{7,5},{8,10},{9,11},{10,... | collective-permute-start | bytes 884744 | tf_op jit(solution)/shard_map/ppermute | solution.py:107
  8.2 20.9 %collective-permute-start.14 = (bf16[2,96,768]{2,1,0:T(8,128)(2,1)S(1)}, bf16[2,96,768]{2,1,0:T(8,128)(2,1)S(1)}, u32[]{:S(2)}, u32[]{:S(2)}) collective-permute-start(bf16[2,96,768]{2,1,0:T(8,128)(2,1)S(1)} %pad_maximum_fusion.5.refs_0_), channel_id=1, source_target_pairs={{0,3},{1,2},{2,1},{3,0},{4,7},{5,6},{6,5},{7,4},{8,11},{9,10},{10,... | collective-permute-start | bytes 884744 | tf_op jit(solution)/shard_map/ppermute | solution.py:107
  8.5 25.1 %collective-permute-start = (bf16[112,768]{1,0:T(8,128)(2,1)S(1)}, bf16[112,768]{1,0:T(8,128)(2,1)S(1)}, u32[]{:S(2)}, u32[]{:S(2)}) collective-permute-start(bf16[112,768]{1,0:T(8,128)(2,1)S(1)} %fusion.14.refs_0_), channel_id=1, source_target_pairs={{0,1},{1,0},{2,3},{3,2},{4,5},{5,4},{6,7},{7,6},{8,9},{9,8},{10,11... | collective-permute-start | bytes 516104 | tf_op jit(solution)/shard_map/ppermute | solution.py:107
  9.4 37.1 %collective-permute-start.1 = (bf16[112,768]{1,0:T(8,128)(2,1)S(1)}, bf16[112,768]{1,0:T(8,128)(2,1)S(1)}, u32[]{:S(2)}, u32[]{:S(2)}) collective-permute-start(bf16[112,768]{1,0:T(8,128)(2,1)S(1)} %fusion.14.refs_0_), channel_id=1, source_target_pairs={{0,2},{1,3},{2,0},{3,1},{4,6},{5,7},{6,4},{7,5},{8,10},{9,11},{10,... | collective-permute-start | bytes 516104 | tf_op jit(solution)/shard_map/ppermute | solution.py:107
  19.0 27.5 %collective-permute-start.2 = (bf16[112,768]{1,0:T(8,128)(2,1)S(1)}, bf16[112,768]{1,0:T(8,128)(2,1)S(1)}, u32[]{:S(2)}, u32[]{:S(2)}) collective-permute-start(bf16[112,768]{1,0:T(8,128)(2,1)S(1)} %fusion.14.refs_0_), channel_id=1, source_target_pairs={{0,3},{1,2},{2,1},{3,0},{4,7},{5,6},{6,5},{7,4},{8,11},{9,10},{10,... | collective-permute-start | bytes 516104 | tf_op jit(solution)/shard_map/ppermute | solution.py:107
  30.6 48.8 %collective-permute-start.16 = (bf16[8,96,768]{2,1,0:T(8,128)(2,1)}, bf16[8,96,768]{2,1,0:T(8,128)(2,1)}, u32[]{:S(2)}, u32[]{:S(2)}) collective-permute-start(bf16[8,96,768]{2,1,0:T(8,128)(2,1)} %spread2.1.rest_0_), channel_id=1, source_target_pairs={{0,8},{4,12},{8,0},{12,4},{16,24},{20,28},{24,16},{28,20},{1,9},{5... | collective-permute-start | bytes 3538952 | tf_op jit(solution)/shard_map/ppermute | solution.py:24
  32.1 47.9 %collective-permute-start.18 = (bf16[8,96,768]{2,1,0:T(8,128)(2,1)}, bf16[8,96,768]{2,1,0:T(8,128)(2,1)}, u32[]{:S(2)}, u32[]{:S(2)}) collective-permute-start(bf16[8,96,768]{2,1,0:T(8,128)(2,1)} %spread2.1.rest_0_), channel_id=1, source_target_pairs={{0,16},{4,20},{8,24},{12,28},{16,0},{20,4},{24,8},{28,12},{1,17},{... | collective-permute-start | bytes 3538952 | tf_op jit(solution)/shard_map/ppermute | solution.py:24
  46.9 23.1 %collective-permute-start.6 = (bf16[4,96,768]{2,1,0:T(8,128)(2,1)S(1)}, bf16[4,96,768]{2,1,0:T(8,128)(2,1)}, u32[]{:S(2)}, u32[]{:S(2)}) collective-permute-start(bf16[4,96,768]{2,1,0:T(8,128)(2,1)S(1)} %get-tuple-element.53.rest_0_.rest_10_), channel_id=1, source_target_pairs={{0,16},{4,20},{8,24},{12,28},{16,0},{20,4},{24,8},{28,12},{1,17},{... | collective-permute-start | bytes 1769480 | tf_op jit(solution)/shard_map/ppermute | solution.py:24
  48.5 23.1 %collective-permute-start.4 = (bf16[4,96,768]{2,1,0:T(8,128)(2,1)S(1)}, bf16[4,96,768]{2,1,0:T(8,128)(2,1)}, u32[]{:S(2)}, u32[]{:S(2)}) collective-permute-start(bf16[4,96,768]{2,1,0:T(8,128)(2,1)S(1)} %get-tuple-element.53.rest_0_.rest_10_), channel_id=1, source_target_pairs={{0,8},{4,12},{8,0},{12,4},{16,24},{20,28},{24,16},{28,20},{1,9},{5... | collective-permute-start | bytes 1769480 | tf_op jit(solution)/shard_map/ppermute | solution.py:24
  71.0 7.6 %collective-permute-start.10 = (bf16[2,96,768]{2,1,0:T(8,128)(2,1)S(1)}, bf16[2,96,768]{2,1,0:T(8,128)(2,1)S(1)}, u32[]{:S(2)}, u32[]{:S(2)}) collective-permute-start(bf16[2,96,768]{2,1,0:T(8,128)(2,1)S(1)} %slice.184), channel_id=1, source_target_pairs={{0,8},{4,12},{8,0},{12,4},{16,24},{20,28},{24,16},{28,20},{1,9},{5... | collective-permute-start | bytes 884744 | tf_op jit(solution)/shard_map/ppermute | solution.py:24
  72.6 6.8 %collective-permute-start.8 = (bf16[2,96,768]{2,1,0:T(8,128)(2,1)S(1)}, bf16[2,96,768]{2,1,0:T(8,128)(2,1)S(1)}, u32[]{:S(2)}, u32[]{:S(2)}) collective-permute-start(bf16[2,96,768]{2,1,0:T(8,128)(2,1)S(1)} %slice.183), channel_id=1, source_target_pairs={{0,16},{4,20},{8,24},{12,28},{16,0},{20,4},{24,8},{28,12},{1,17},{... | collective-permute-start | bytes 884744 | tf_op jit(solution)/shard_map/ppermute | solution.py:24
  74.9 8.0 %all-to-all-start.1 = ((bf16[4,8,96]{2,0,1:T(4,128)(2,1)}), bf16[4,8,96]{2,0,1:T(4,128)(2,1)S(1)}, u32[]{:S(2)}, u32[]{:S(2)}) async-start(bf16[4,8,96]{2,0,1:T(4,128)(2,1)} %copy.110), calls=%async_computation.1 | async-start | bytes 16384 | tf_op jit(solution)/shard_map/all_to_all | solution.py:578
  78.2 33.3 %collective-permute-start.3 = (bf16[4,96,768]{2,1,0:T(8,128)(2,1)S(1)}, bf16[4,96,768]{2,1,0:T(8,128)(2,1)S(1)}, u32[]{:S(2)}, u32[]{:S(2)}) collective-permute-start(bf16[4,96,768]{2,1,0:T(8,128)(2,1)S(1)} %get-tuple-element.53.rest_0_.rest_10_), channel_id=1, source_target_pairs={{0,4},{4,0},{8,12},{12,8},{16,20},{20,16},{24,28},{28,24},{1,5},{5... | collective-permute-start | bytes 1769480 | tf_op jit(solution)/shard_map/ppermute | solution.py:24
  78.6 34.5 %collective-permute-start.5 = (bf16[4,96,768]{2,1,0:T(8,128)(2,1)}, bf16[4,96,768]{2,1,0:T(8,128)(2,1)}, u32[]{:S(2)}, u32[]{:S(2)}) collective-permute-start(bf16[4,96,768]{2,1,0:T(8,128)(2,1)} %collective-permute-done.4.rest_2_.rest_12_), channel_id=1, source_target_pairs={{0,4},{4,0},{8,12},{12,8},{16,20},{20,16},{24,28},{28,24},{1,5},{5... | collective-permute-start | bytes 1769480 | tf_op jit(solution)/shard_map/ppermute | solution.py:24
  79.4 34.3 %collective-permute-start.7 = (bf16[4,96,768]{2,1,0:T(8,128)(2,1)}, bf16[4,96,768]{2,1,0:T(8,128)(2,1)}, u32[]{:S(2)}, u32[]{:S(2)}) collective-permute-start(bf16[4,96,768]{2,1,0:T(8,128)(2,1)} %collective-permute-done.6.rest_4_.rest_14_), channel_id=1, source_target_pairs={{0,4},{4,0},{8,12},{12,8},{16,20},{20,16},{24,28},{28,24},{1,5},{5... | collective-permute-start | bytes 1769480 | tf_op jit(solution)/shard_map/ppermute | solution.py:24
  79.4 32.9 %collective-permute-start.11 = (bf16[2,96,768]{2,1,0:T(8,128)(2,1)S(1)}, bf16[2,96,768]{2,1,0:T(8,128)(2,1)S(1)}, u32[]{:S(2)}, u32[]{:S(2)}) collective-permute-start(bf16[2,96,768]{2,1,0:T(8,128)(2,1)S(1)} %collective-permute-done.10.rest_8_.rest_18_), channel_id=1, source_target_pairs={{0,4},{4,0},{8,12},{12,8},{16,20},{20,16},{24,28},{28,24},{1,5},{5... | collective-permute-start | bytes 884744 | tf_op jit(solution)/shard_map/ppermute | solution.py:24
  80.0 33.2 %collective-permute-start.9 = (bf16[2,96,768]{2,1,0:T(8,128)(2,1)S(1)}, bf16[2,96,768]{2,1,0:T(8,128)(2,1)S(1)}, u32[]{:S(2)}, u32[]{:S(2)}) collective-permute-start(bf16[2,96,768]{2,1,0:T(8,128)(2,1)S(1)} %collective-permute-done.8.rest_6_.rest_16_), channel_id=1, source_target_pairs={{0,4},{4,0},{8,12},{12,8},{16,20},{20,16},{24,28},{28,24},{1,5},{5... | collective-permute-start | bytes 884744 | tf_op jit(solution)/shard_map/ppermute | solution.py:24
  83.8 24.2 %all-to-all-start.2 = ((f32[32,1,1152]{2,1,0:T(1,128)}), f32[32,1,1152]{2,1,0:T(1,128)S(1)}, u32[]{:S(2)}, u32[]{:S(2)}) async-start(f32[32,1,1152]{2,1,0:T(1,128)} %copy.111), calls=%async_computation.2 | async-start | bytes 294912 | tf_op jit(solution)/shard_map/all_to_all | solution.py:583
  108.0 14.6 %all-to-all-start = ((bf16[4,64,768]{2,1,0:T(8,128)(2,1)}), bf16[4,64,768]{2,1,0:T(8,128)(2,1)S(1)}, u32[]{:S(2)}, u32[]{:S(2)}) async-start(bf16[4,64,768]{2,1,0:T(8,128)(2,1)} %bitcast.87), calls=%async_computation | async-start | bytes 786432 | tf_op jit(solution)/shard_map/all_to_all | solution.py:566
  111.5 26.9 %collective-permute-start.15 = (bf16[8,96,768]{2,1,0:T(8,128)(2,1)}, bf16[8,96,768]{2,1,0:T(8,128)(2,1)}, u32[]{:S(2)}, u32[]{:S(2)}) collective-permute-start(bf16[8,96,768]{2,1,0:T(8,128)(2,1)} %spread2.1.rest_0_), channel_id=1, source_target_pairs={{0,4},{4,0},{8,12},{12,8},{16,20},{20,16},{24,28},{28,24},{1,5},{5... | collective-permute-start | bytes 3538952 | tf_op jit(solution)/shard_map/ppermute | solution.py:24
  112.3 15.2 %collective-permute-start.20 = (bf16[4,96,768]{2,1,0:T(8,128)(2,1)}, bf16[4,96,768]{2,1,0:T(8,128)(2,1)S(1)}, u32[]{:S(2)}, u32[]{:S(2)}) collective-permute-start(bf16[4,96,768]{2,1,0:T(8,128)(2,1)} %slice.185), channel_id=1, source_target_pairs={{0,16},{4,20},{8,24},{12,28},{16,0},{20,4},{24,8},{28,12},{1,17},{... | collective-permute-start | bytes 1769480 | tf_op jit(solution)/shard_map/ppermute | solution.py:24
  113.1 25.2 %collective-permute-start.17 = (bf16[8,96,768]{2,1,0:T(8,128)(2,1)}, bf16[8,96,768]{2,1,0:T(8,128)(2,1)}, u32[]{:S(2)}, u32[]{:S(2)}) collective-permute-start(bf16[8,96,768]{2,1,0:T(8,128)(2,1)} %collective-permute-done.16.rest_2_), channel_id=1, source_target_pairs={{0,4},{4,0},{8,12},{12,8},{16,20},{20,16},{24,28},{28,24},{1,5},{5... | collective-permute-start | bytes 3538952 | tf_op jit(solution)/shard_map/ppermute | solution.py:24
  113.1 25.2 %collective-permute-start.19 = (bf16[8,96,768]{2,1,0:T(8,128)(2,1)}, bf16[8,96,768]{2,1,0:T(8,128)(2,1)}, u32[]{:S(2)}, u32[]{:S(2)}) collective-permute-start(bf16[8,96,768]{2,1,0:T(8,128)(2,1)} %collective-permute-done.18.rest_4_), channel_id=1, source_target_pairs={{0,4},{4,0},{8,12},{12,8},{16,20},{20,16},{24,28},{28,24},{1,5},{5... | collective-permute-start | bytes 3538952 | tf_op jit(solution)/shard_map/ppermute | solution.py:24
  113.6 15.6 %collective-permute-start.22 = (bf16[4,96,768]{2,1,0:T(8,128)(2,1)}, bf16[4,96,768]{2,1,0:T(8,128)(2,1)}, u32[]{:S(2)}, u32[]{:S(2)}) collective-permute-start(bf16[4,96,768]{2,1,0:T(8,128)(2,1)} %slice.186), channel_id=1, source_target_pairs={{0,8},{4,12},{8,0},{12,4},{16,24},{20,28},{24,16},{28,20},{1,9},{5... | collective-permute-start | bytes 1769480 | tf_op jit(solution)/shard_map/ppermute | solution.py:24
  122.6 15.7 %all-to-all-start.3 = ((bf16[4,64,768]{2,1,0:T(8,128)(2,1)}), bf16[4,64,768]{2,1,0:T(8,128)(2,1)S(1)}, u32[]{:S(2)}, u32[]{:S(2)}) async-start(bf16[4,64,768]{2,1,0:T(8,128)(2,1)} %bitcast.88), calls=%async_computation.3 | async-start | bytes 786432 | tf_op jit(solution)/shard_map/all_to_all | solution.py:566
  127.5 10.8 %collective-permute-start.21 = (bf16[4,96,768]{2,1,0:T(8,128)(2,1)S(1)}, bf16[4,96,768]{2,1,0:T(8,128)(2,1)}, u32[]{:S(2)}, u32[]{:S(2)}) collective-permute-start(bf16[4,96,768]{2,1,0:T(8,128)(2,1)S(1)} %collective-permute-done.20.rest_6_), channel_id=1, source_target_pairs={{0,4},{4,0},{8,12},{12,8},{16,20},{20,16},{24,28},{28,24},{1,5},{5... | collective-permute-start | bytes 1769480 | tf_op jit(solution)/shard_map/ppermute | solution.py:24
  129.3 9.1 %collective-permute-start.23 = (bf16[4,96,768]{2,1,0:T(8,128)(2,1)}, bf16[4,96,768]{2,1,0:T(8,128)(2,1)}, u32[]{:S(2)}, u32[]{:S(2)}) collective-permute-start(bf16[4,96,768]{2,1,0:T(8,128)(2,1)} %collective-permute-done.22.rest_8_), channel_id=1, source_target_pairs={{0,4},{4,0},{8,12},{12,8},{16,20},{20,16},{24,28},{28,24},{1,5},{5... | collective-permute-start | bytes 1769480 | tf_op jit(solution)/shard_map/ppermute | solution.py:24
  155.4 43.1 %collective-permute-start.32 = (bf16[4,8,96,768]{3,2,1,0:T(8,128)(2,1)}, bf16[4,8,96,768]{3,2,1,0:T(8,128)(2,1)}, u32[]{:S(2)}, u32[]{:S(2)}) collective-permute-start(bf16[4,8,96,768]{3,2,1,0:T(8,128)(2,1)} %get-tuple-element.81), channel_id=1, source_target_pairs={{0,4},{4,0},{8,12},{12,8},{16,20},{20,16},{24,28},{28,24},{1,5},{5... | collective-permute-start | bytes 14155784 | tf_op jit(solution)/shard_map/ppermute | solution.py:24
  175.3 32.8 %collective-permute-start.24 = (bf16[4,4,96,768]{3,2,1,0:T(8,128)(2,1)}, bf16[4,4,96,768]{3,2,1,0:T(8,128)(2,1)}, u32[]{:S(2)}, u32[]{:S(2)}) collective-permute-start(bf16[4,4,96,768]{3,2,1,0:T(8,128)(2,1)} %get-tuple-element.73), channel_id=1, source_target_pairs={{0,4},{4,0},{8,12},{12,8},{16,20},{20,16},{24,28},{28,24},{1,5},{5... | collective-permute-start | bytes 7077896 | tf_op jit(solution)/shard_map/ppermute | solution.py:24
  184.0 14.2 %all-to-all-start.5 = ((bf16[32,2,1344]{2,1,0:T(2,128)(2,1)}), bf16[32,2,1344]{2,1,0:T(2,128)(2,1)S(1)}, u32[]{:S(2)}, u32[]{:S(2)}) async-start(bf16[32,2,1344]{2,1,0:T(2,128)(2,1)} %reshape.220), calls=%async_computation.5 | async-start | bytes 360448 | tf_op jit(solution)/shard_map/all_to_all | solution.py:679
  202.6 17.2 %collective-permute-start.33 = (bf16[4,96,768]{2,1,0:T(8,128)(2,1)}, bf16[4,96,768]{2,1,0:T(8,128)(2,1)}, u32[]{:S(2)}, u32[]{:S(2)}) collective-permute-start(bf16[4,96,768]{2,1,0:T(8,128)(2,1)} %get-tuple-element.220), channel_id=1, source_target_pairs={{0,16},{4,20},{8,24},{12,28},{16,0},{20,4},{24,8},{28,12},{1,17},{... | collective-permute-start | bytes 1769480 | tf_op jit(solution)/shard_map/ppermute | solution.py:24
  203.4 17.1 %collective-permute-start.35 = (bf16[4,96,768]{2,1,0:T(8,128)(2,1)}, bf16[4,96,768]{2,1,0:T(8,128)(2,1)}, u32[]{:S(2)}, u32[]{:S(2)}) collective-permute-start(bf16[4,96,768]{2,1,0:T(8,128)(2,1)} %get-tuple-element.218), channel_id=1, source_target_pairs={{0,8},{4,12},{8,0},{12,4},{16,24},{20,28},{24,16},{28,20},{1,9},{5... | collective-permute-start | bytes 1769480 | tf_op jit(solution)/shard_map/ppermute | solution.py:24
  204.8 22.4 %all-to-all-start.6 = ((f32[32,4,96]{2,1,0:T(4,128)}), f32[32,4,96]{2,1,0:T(4,128)S(1)}, u32[]{:S(2)}, u32[]{:S(2)}) async-start(f32[32,4,96]{2,1,0:T(4,128)} %bitcast.19), calls=%async_computation.6 | async-start | bytes 131072 | tf_op jit(solution)/shard_map/all_to_all | solution.py:689
  210.6 20.8 %collective-permute-start.25 = (bf16[2,96,768]{2,1,0:T(8,128)(2,1)}, bf16[2,96,768]{2,1,0:T(8,128)(2,1)}, u32[]{:S(2)}, u32[]{:S(2)}) collective-permute-start(bf16[2,96,768]{2,1,0:T(8,128)(2,1)} %get-tuple-element.226), channel_id=1, source_target_pairs={{0,16},{4,20},{8,24},{12,28},{16,0},{20,4},{24,8},{28,12},{1,17},{... | collective-permute-start | bytes 884744 | tf_op jit(solution)/shard_map/ppermute | solution.py:24
  212.3 19.1 %collective-permute-start.27 = (bf16[2,96,768]{2,1,0:T(8,128)(2,1)}, bf16[2,96,768]{2,1,0:T(8,128)(2,1)}, u32[]{:S(2)}, u32[]{:S(2)}) collective-permute-start(bf16[2,96,768]{2,1,0:T(8,128)(2,1)} %get-tuple-element.224), channel_id=1, source_target_pairs={{0,8},{4,12},{8,0},{12,4},{16,24},{20,28},{24,16},{28,20},{1,9},{5... | collective-permute-start | bytes 884744 | tf_op jit(solution)/shard_map/ppermute | solution.py:24
  224.0 45.1 %collective-permute-start.36 = (bf16[8,96,768]{2,1,0:T(8,128)(2,1)}, bf16[8,96,768]{2,1,0:T(8,128)(2,1)}, u32[]{:S(2)}, u32[]{:S(2)}) collective-permute-start(bf16[8,96,768]{2,1,0:T(8,128)(2,1)} %pad_maximum_fusion.1), channel_id=1, source_target_pairs={{0,16},{4,20},{8,24},{12,28},{16,0},{20,4},{24,8},{28,12},{1,17},{... | collective-permute-start | bytes 3538952 | tf_op jit(solution)/shard_map/ppermute | solution.py:24
  226.4 42.8 %collective-permute-start.34 = (bf16[8,96,768]{2,1,0:T(8,128)(2,1)}, bf16[8,96,768]{2,1,0:T(8,128)(2,1)}, u32[]{:S(2)}, u32[]{:S(2)}) collective-permute-start(bf16[8,96,768]{2,1,0:T(8,128)(2,1)} %pad_maximum_fusion), channel_id=1, source_target_pairs={{0,8},{4,12},{8,0},{12,4},{16,24},{20,28},{24,16},{28,20},{1,9},{5... | collective-permute-start | bytes 3538952 | tf_op jit(solution)/shard_map/ppermute | solution.py:24
  227.2 54.0 %all-to-all-start.4 = ((bf16[4,2,64,768]{3,2,1,0:T(8,128)(2,1)}), bf16[4,2,64,768]{3,2,1,0:T(8,128)(2,1)}, u32[]{:S(2)}, u32[]{:S(2)}) async-start(bf16[4,2,64,768]{3,2,1,0:T(8,128)(2,1)} %pad_maximum_fusion.2), calls=%async_computation.4 | async-start | bytes 1572864 | tf_op jit(solution)/shard_map/all_to_all | solution.py:570
  233.0 29.4 %collective-permute-start.28 = (bf16[4,96,768]{2,1,0:T(8,128)(2,1)S(1)}, bf16[4,96,768]{2,1,0:T(8,128)(2,1)S(1)}, u32[]{:S(2)}, u32[]{:S(2)}) collective-permute-start(bf16[4,96,768]{2,1,0:T(8,128)(2,1)S(1)} %pad_maximum_fusion.4), channel_id=1, source_target_pairs={{0,16},{4,20},{8,24},{12,28},{16,0},{20,4},{24,8},{28,12},{1,17},{... | collective-permute-start | bytes 1769480 | tf_op jit(solution)/shard_map/ppermute | solution.py:24
  233.9 29.6 %collective-permute-start.26 = (bf16[4,96,768]{2,1,0:T(8,128)(2,1)S(1)}, bf16[4,96,768]{2,1,0:T(8,128)(2,1)S(1)}, u32[]{:S(2)}, u32[]{:S(2)}) collective-permute-start(bf16[4,96,768]{2,1,0:T(8,128)(2,1)S(1)} %pad_maximum_fusion.3), channel_id=1, source_target_pairs={{0,8},{4,12},{8,0},{12,4},{16,24},{20,28},{24,16},{28,20},{1,9},{5... | collective-permute-start | bytes 1769480 | tf_op jit(solution)/shard_map/ppermute | solution.py:24
  267.1 12.6 %collective-permute-start.29 = (bf16[96,768]{1,0:T(8,128)(2,1)S(1)}, bf16[96,768]{1,0:T(8,128)(2,1)S(1)}, u32[]{:S(2)}, u32[]{:S(2)}) collective-permute-start(bf16[96,768]{1,0:T(8,128)(2,1)S(1)} %get-tuple-element.75), channel_id=1, source_target_pairs={{0,1},{1,0},{2,3},{3,2},{4,5},{5,4},{6,7},{7,6},{8,9},{9,8},{10,11... | collective-permute-start | bytes 442376 | tf_op jit(solution)/shard_map/ppermute | solution.py:107
  274.6 38.9 %collective-permute-start.37 = (bf16[2,96,768]{2,1,0:T(8,128)(2,1)S(1)}, bf16[2,96,768]{2,1,0:T(8,128)(2,1)S(1)}, u32[]{:S(2)}, u32[]{:S(2)}) collective-permute-start(bf16[2,96,768]{2,1,0:T(8,128)(2,1)S(1)} %get-tuple-element.83), channel_id=1, source_target_pairs={{0,1},{1,0},{2,3},{3,2},{4,5},{5,4},{6,7},{7,6},{8,9},{9,8},{10,11... | collective-permute-start | bytes 884744 | tf_op jit(solution)/shard_map/ppermute | solution.py:107
  274.7 38.8 %collective-permute-start.38 = (bf16[2,96,768]{2,1,0:T(8,128)(2,1)S(1)}, bf16[2,96,768]{2,1,0:T(8,128)(2,1)S(1)}, u32[]{:S(2)}, u32[]{:S(2)}) collective-permute-start(bf16[2,96,768]{2,1,0:T(8,128)(2,1)S(1)} %get-tuple-element.84), channel_id=1, source_target_pairs={{0,2},{1,3},{2,0},{3,1},{4,6},{5,7},{6,4},{7,5},{8,10},{9,11},{10,... | collective-permute-start | bytes 884744 | tf_op jit(solution)/shard_map/ppermute | solution.py:107
  276.2 37.3 %collective-permute-start.39 = (bf16[2,96,768]{2,1,0:T(8,128)(2,1)S(1)}, bf16[2,96,768]{2,1,0:T(8,128)(2,1)S(1)}, u32[]{:S(2)}, u32[]{:S(2)}) collective-permute-start(bf16[2,96,768]{2,1,0:T(8,128)(2,1)S(1)} %get-tuple-element.85), channel_id=1, source_target_pairs={{0,3},{1,2},{2,1},{3,0},{4,7},{5,6},{6,5},{7,4},{8,11},{9,10},{10,... | collective-permute-start | bytes 884744 | tf_op jit(solution)/shard_map/ppermute | solution.py:107
  279.7 33.0 %collective-permute-start.30 = (bf16[96,768]{1,0:T(8,128)(2,1)S(1)}, bf16[96,768]{1,0:T(8,128)(2,1)S(1)}, u32[]{:S(2)}, u32[]{:S(2)}) collective-permute-start(bf16[96,768]{1,0:T(8,128)(2,1)S(1)} %get-tuple-element.76), channel_id=1, source_target_pairs={{0,2},{1,3},{2,0},{3,1},{4,6},{5,7},{6,4},{7,5},{8,10},{9,11},{10,... | collective-permute-start | bytes 442376 | tf_op jit(solution)/shard_map/ppermute | solution.py:107
  279.7 33.0 %collective-permute-start.31 = (bf16[96,768]{1,0:T(8,128)(2,1)S(1)}, bf16[96,768]{1,0:T(8,128)(2,1)S(1)}, u32[]{:S(2)}, u32[]{:S(2)}) collective-permute-start(bf16[96,768]{1,0:T(8,128)(2,1)S(1)} %get-tuple-element.77), channel_id=1, source_target_pairs={{0,3},{1,2},{2,1},{3,0},{4,7},{5,6},{6,5},{7,4},{8,11},{9,10},{10,... | collective-permute-start | bytes 442376 | tf_op jit(solution)/shard_map/ppermute | solution.py:107
  (20 other events, 263.6 us)
where the time goes:
time: 316 us; the launch traced here: 315 us
  waiting for transfers between devices  134 us (42%)
  starting transfers between devices  81.6 us (26%)
  Pallas kernels  61.2 us (19%)
  local copies, waits for them, and re-layouts  18.4 us (6%)
  other arithmetic  17.5 us (6%)
    pallas_call x10, Pallas kernels, call(): pl.pallas_call(functools.partial(body, spec), out_shape=far_outs + outs,...  61.2 us
    ppermute x28, waiting for transfers between devices, swap(): return lax.ppermute(values, axis, [(i, i ^ 1 << bit) for i in range(count)])  55.8 us
    ppermute x12, waiting for transfers between devices, swap_seq(): lax.ppermute(values[mask - 1] if isinstance(values, list) else values, 's...  54 us
    ppermute x12, starting transfers between devices, swap_seq(): lax.ppermute(values[mask - 1] if isinstance(values, list) else values, 's...  22.7 us
    ppermute x28, starting transfers between devices, swap(): return lax.ppermute(values, axis, [(i, i ^ 1 << bit) for i in range(count)])  20.6 us
    all_to_all x1, starting transfers between devices, local(): part = lax.all_to_all(part, ('dp', 'seq'), 0, 0, tiled=True)  15.5 us
    all_to_all x2, waiting for transfers between devices, to_latents(): lax.all_to_all(values, 'seq', 0, 0, tiled=True).reshape(length, width)  8.49 us
    all_to_all x1, waiting for transfers between devices, local(): small = lax.all_to_all(small, ('dp', 'seq'), 0, 0, tiled=True)  8.11 us
  transfers between devices with their start and end apart: 47, of which 16 were waited for; matrix products, arithmetic and copies ran while one was open for 10% of the time, Pallas kernels for 14%

commit v1 on v0

--- a/solution.py
+++ b/solution.py
@@ -26,6 +26,19 @@
 
 def own_bit(axis, bit):
     return (lax.axis_index(axis) >> bit) & 1
+
+
+def after(values, first):
+    far = pl.BlockSpec(memory_space=pl.ANY)
+    return pl.pallas_call(
+        lambda *refs: None,
+        out_shape=[jax.ShapeDtypeStruct(v.shape, v.dtype) for v in values],
+        in_specs=[far] * (len(values) + len(first)),
+        out_specs=[far] * len(values),
+        input_output_aliases={i: i for i in range(len(values))},
+        cost_estimate=pl.CostEstimate(flops=0, bytes_accessed=0, transcendentals=0),
+        name="after",
+    )(*values, *first)
 
 
 def halve(values, axis, bit):
@@ -47,8 +60,8 @@
 
 
 class Layout:
-    def __init__(self, n_dp, rows, width):
-        self.direct = rows % 16 == 0 and n_dp == 8
+    def __init__(self, n_dp, n_seq, rows, width):
+        self.direct = rows % 16 == 0 and n_dp == 8 and n_seq == 4
         self.blocks = n_dp if self.direct else 1
         self.rows = rows if self.direct else width
 
@@ -79,34 +92,64 @@
     return values
 
 
-def gather_square(units):
+def gather_square(units, first=()):
     middle = units.shape[0] // 2
     over_x, over_y = swap(units, "dp", 1), swap(units, "dp", 2)
-    low = swap(over_x[:middle], "dp", 2)
-    high = swap(over_y[middle:], "dp", 1)
+    low, high = cut(over_x, over_y, first)
+    low, high = swap(low, "dp", 2), swap(high, "dp", 1)
     near = [(units, 0, 0), (over_x, 2, 0), (over_y, 4, 0), (low, 6, 0), (high, 6, middle)]
     far = [(swap(part, "dp", 0), mask | 1, first) for part, mask, first in near]
     return [entry for pair in zip(near, far) for entry in pair]
 
 
-def scatter_square(kept, sent):
-    other = swap(sent, "dp", 0)
-    middle = kept.shape[1] // 2
-    both = lambda place, units: kept[place, units].astype(F32) + other[place, units].astype(F32)
-    low, high, every = slice(0, middle), slice(middle, None), slice(0, None)
-    low_in = swap(both(3, low).astype(BF), "dp", 2)
-    high_in = swap(both(3, high).astype(BF), "dp", 1)
-    to_x = jnp.concatenate([both(1, low) + low_in.astype(F32), both(1, high)]).astype(BF)
-    to_y = jnp.concatenate([both(2, low), both(2, high) + high_in.astype(F32)]).astype(BF)
-    return (kept, other, swap(to_x, "dp", 1), swap(to_y, "dp", 2))
+def scatter_first(kept, others, first=()):
+    _, units, rows, columns = kept.shape
+    middle = units // 2
+    half = jax.ShapeDtypeStruct((middle, rows, columns), BF)
+    part = lambda place, high: (kept, (place, high), (1, middle))
+    low_in, high_in, over_x, over_y = others[3], others[4], others[1], others[2]
+    return call(
+        add_kernel, 2, jnp.zeros((1,), jnp.int32),
+        [part(3, 0), low_in, part(3, 1), high_in]
+        + [part(1, 1), (over_x, (1,), (middle,)), part(2, 0), (over_y, (0,), (middle,))],
+        [], [half] * 4, [], [], "first_sums", first,
+    )
+
+
+def scatter_last(kept, others, low_in, high_in, first=()):
+    _, units, rows, columns = kept.shape
+    middle = units // 2
+    half = jax.ShapeDtypeStruct((middle, rows, columns), BF)
+    part = lambda place, high: (kept, (place, high), (1, middle))
+    return call(
+        add_kernel, 3, jnp.zeros((1,), jnp.int32),
+        [part(1, 0), (others[1], (0,), (middle,)), low_in]
+        + [part(2, 1), (others[2], (1,), (middle,)), high_in],
+        [], [half] * 2, [], [], "last_sums", first,
+    )
+
+
+def cut(over_x, over_y, first=()):
+    half = jax.ShapeDtypeStruct((over_x.shape[0] // 2,) + over_x.shape[1:], BF)
+    return call(
+        cut_kernel, None, jnp.zeros((1,), jnp.int32),
+        [(over_x, (0,), half.shape[:1]), (over_y, (1,), half.shape[:1])], [],
+        [half, half], [], [], "cut", first,
+    )
+
+
+def gather_seq(values):
+    found = {0: values}
+    for bit in range(bits_of(lax.axis_size("seq")) - 1, -1, -1):
+        found.update({mask | 1 << bit: swap(v, "seq", bit) for mask, v in list(found.items())})
+    return [found[mask] for mask in range(len(found))]
 
 
 def swap_seq(values):
     count = lax.axis_size("seq")
     return [
-        lax.ppermute(values[mask - 1] if isinstance(values, list) else values, "seq",
-                     [(i, i ^ mask) for i in range(count)])
-        for mask in range(1, count)
+        lax.ppermute(value, "seq", [(i, i ^ (mask + 1)) for i in range(count)])
+        for mask, value in enumerate(values)
     ]
 
 
@@ -177,13 +220,28 @@
     copies = []
     blocks = scratch.shape[0]
     for mask in range(blocks):
-        out = outs[mask & 1] if blocks > 1 else outs[0]
         place = mask >> 1
-        copies.append(
-            pltpu.make_async_copy(
-                scratch.at[me ^ mask], out.at[place, units[0] : units[1]], sems.at[base + len(copies)]
-            )
-        )
+        out = outs[0].at[place]
+        if mask & 1:
+            out = outs[1 + place] if place < 3 else None
+        count = units[1] - units[0]
+        spans = [(out, 0, units[0], count)]
+        if out is None:
+            middle = outs[4].shape[0]
+            spans = [
+                (outs[4 + half], max(half * middle - units[0], 0), max(units[0] - half * middle, 0),
+                 min(units[1], (half + 1) * middle) - max(units[0], half * middle))
+                for half in range(2)
+            ]
+        for target, source, first, number in spans:
+            if number > 0:
+                copies.append(
+                    pltpu.make_async_copy(
+                        scratch.at[me ^ mask, source : source + number],
+                        target.at[first : first + number],
+                        sems.at[base + len(copies)],
+                    )
+                )
     return copies
 
 
@@ -191,11 +249,42 @@
     return lax.broadcasted_iota(jnp.int32, shape, 1)
 
 
-def attend_kernel(spec, me_ref, tokens_ref, mod_ref, qkv_off_ref, proj_off_ref, *rest):
+def copy_kernel(spec, me_ref, source, target):
+    target[...] = source[...]
+
+
+def pack_kernel(spec, me_ref, tokens_ref, part_ref, out_ref, rows):
+    held, tok, width = tokens_ref.shape
+    half = width // 2
+    mod = part_ref[0]
+    for index in range(1, part_ref.shape[0]):
+        mod = mod + part_ref[index]
+    high = mod.astype(BF).astype(F32)
+    low = mod - high
+    rows[...] = jnp.zeros_like(rows)
+    for index in range(held):
+        out_ref[index, :tok] = tokens_ref[index]
+        own = slice(index, index + 1)
+        rows[0:1] = high[own, :width]
+        rows[1:2] = low[own, :width]
+        rows[2:3, :half] = high[own, width:]
+        rows[2:3, half:] = low[own, width:]
+        out_ref[index, tok:] = rows[...].astype(BF)
+
+
+def attend_kernel(spec, me_ref, packed_ref, qkv_off_ref, proj_off_ref, *rest):
     width, pieces, factor, pairs = spec
     refs, rest = rest[: len(pieces)], rest[len(pieces) :]
-    hidden_ref, qkv_ref, att_ref, branch_ref, middle_ref, weights, sems = rest
+    hidden_ref, qkv_ref, att_ref, branch_ref, middle_ref, mod_ref, tokens_ref, weights, sems = rest
     me = me_ref[0]
+    count, tok = packed_ref.shape[0], packed_ref.shape[1] - 16
+    half = width // 2
+    for seq in range(count):
+        tokens_ref[seq * tok : (seq + 1) * tok] = packed_ref[seq, :tok]
+        row = packed_ref[seq, tok:].astype(F32)
+        at = seq * (width + half)
+        mod_ref[:, at : at + width] = row[0:1] + row[1:2]
+        mod_ref[:, at + width : at + width + half] = row[2:3, :half] + row[2:3, half:]
     copies = loads(pieces, refs, me, by_unit(weights), (0, 4), sems)
     start(copies)
     tokens = tokens_ref[...].astype(F32)
@@ -281,19 +370,17 @@
         up_bias_ref[:, unit * width : (unit + 1) * width] = total(dbefore)
         grad = dot_outer(hidden, dbefore).astype(BF)
         up_grad[:, unit] = grad.reshape(up_grad.shape[0], up_grad.shape[2], width)
-    up_stores = stores(up_grad, outs, me, (0, wide), out_sems, up_grad.shape[0])
+    up_stores = stores(up_grad, outs, me, (0, wide), out_sems, len(down_stores))
     start(up_stores)
     finish(down_stores)
     finish(up_stores)
 
 
-def attend_back_kernel(spec, me_ref, middle_ref, mod_ref, cot_ref, dbefore_ref, branch_ref, att_ref,
-                       hidden_ref, qkv_ref, *rest):
-    width, wide, up_pieces, pieces, factor, pairs = spec
+def middle_back_kernel(spec, me_ref, middle_ref, mod_ref, cot_ref, dbefore_ref, branch_ref, *rest):
+    width, wide, up_pieces, pieces = spec
     up_refs, rest = rest[: len(up_pieces)], rest[len(up_pieces) :]
     refs, rest = rest[: len(pieces)], rest[len(pieces) :]
-    outs, rest = rest[: len(rest) - 10], rest[len(rest) - 10 :]
-    dmiddle_ref, dqkv_ref, sums_ref, bias_ref, up, proj, grads, up_sems, proj_sems, out_sems = rest
+    dmiddle_ref, dbranch_ref, datt_ref, sums_ref, bias_ref, up, proj, up_sems, proj_sems = rest
     me = me_ref[0]
     up_copies = loads(up_pieces, up_refs, me, by_unit(up), (0, wide), up_sems)
     proj_copies = loads(pieces, refs, me, by_unit(proj), (3, 4), proj_sems)
@@ -308,16 +395,24 @@
     dmiddle = cot_ref[...].astype(F32) + norm_back(dhidden * (1.0 + part(4)), normed, inverse)
     dmiddle_ref[...] = dmiddle
     dbranch = (part(2) * dmiddle).astype(BF)
+    dbranch_ref[...] = dbranch
     sums_ref[:, :width] = total(dmiddle * branch_ref[...])
     sums_ref[:, width : 2 * width] = total(dhidden)
     sums_ref[:, 2 * width : 3 * width] = total(dhidden * normed)
-    bias_ref[:, 2 * width : 3 * width] = total(dbranch)
+    bias_ref[...] = total(dbranch)
     finish(proj_copies)
-    datt = dot_back(dbranch, matrix_of(proj, 0)).astype(BF)
+    datt_ref[...] = dot_back(dbranch, matrix_of(proj, 0)).astype(BF)
+
+
+def attend_back_kernel(spec, me_ref, dbranch_ref, datt_ref, att_ref, hidden_ref, qkv_ref, *rest):
+    width, factor, pairs = spec
+    outs, rest = rest[: len(rest) - 4], rest[len(rest) - 4 :]
+    dqkv_ref, bias_ref, grads, out_sems = rest
+    me = me_ref[0]
     for pair in range(pairs):
         cols = slice(pair * 128, (pair + 1) * 128)
         q, k, v = qkv_ref[0, :, cols], qkv_ref[1, :, cols], qkv_ref[2, :, cols]
-        da = datt[:, cols]
+        da = datt_ref[:, cols]
         first = lanes(k.shape) < 64
         zero = jnp.zeros_like(k)
         grad_q, grad_k, grad_v = [], [], []
@@ -340,16 +435,17 @@
     shape = (grads.shape[0], grads.shape[2], width)
     for unit in range(3):
         grads[:, unit] = dot_outer(hidden_ref[...], dqkv_ref[unit]).astype(BF).reshape(shape)
-    grads[:, 3] = dot_outer(att_ref[...], dbranch).astype(BF).reshape(shape)
+    grads[:, 3] = dot_outer(att_ref[...], dbranch_ref[...]).astype(BF).reshape(shape)
     out_copies = stores(grads, outs, me, (0, 4), out_sems, 0)
     start(out_copies)
     finish(out_copies)
 
 
-def input_back_kernel(spec, me_ref, tokens_ref, mod_ref, dmiddle_ref, dqkv_ref, *rest):
-    width, pieces = spec
+def input_back_kernel(spec, me_ref, tokens_ref, mod_ref, dmiddle_ref, dqkv_ref, sums_ref, gate_ref,
+                      qv_ref, proj_off_ref, up_off_ref, down_off_ref, *rest):
+    width, tok, chunk, pieces = spec
     refs, rest = rest[: len(pieces)], rest[len(pieces) :]
-    dtokens_ref, sums_ref, weights, sems = rest
+    packed_ref, weights, dmod, rows, sems = rest
     copies = loads(pieces, refs, me_ref[0], by_unit(weights), (0, 3), sems)
     start(copies)
     normed, inverse = normalize(tokens_ref[...].astype(F32))
@@ -357,13 +453,41 @@
     dhidden = dot_back(dqkv_ref[0], matrix_of(weights, 0))
     for unit in range(1, 3):
         dhidden = dhidden + dot_back(dqkv_ref[unit], matrix_of(weights, unit))
-    sums_ref[:, :width] = total(dhidden)
-    sums_ref[:, width : 2 * width] = total(dhidden * normed)
+    dmod[:, :width] = total(dhidden)
+    dmod[:, width : 2 * width] = total(dhidden * normed)
+    dmod[:, 2 * width : 5 * width] = sums_ref[...]
+    dmod[:, 5 * width :] = gate_ref[...]
     scale = 1.0 + mod_ref[:, width : 2 * width]
-    dtokens_ref[...] = (dmiddle_ref[...] + norm_back(dhidden * scale, normed, inverse)).astype(BF)
-
-
-def chunks(width, chunk, wide):
+    dtokens = (dmiddle_ref[...] + norm_back(dhidden * scale, normed, inverse)).astype(BF)
+    rows[...] = jnp.zeros_like(rows)
+    half = width // 2
+    for seq in range(packed_ref.shape[0]):
+        packed_ref[seq, :tok] = dtokens[seq * tok : (seq + 1) * tok]
+        at, own = seq * (width + half), slice(seq * chunk, (seq + 1) * chunk)
+        rows[0:1, :] = dmod[:, at : at + width]
+        rows[1:2, :half] = dmod[:, at + width : at + width + half]
+        rows[1:2, half : half + chunk] = qv_ref[:, own]
+        rows[1:2, half + chunk :] = qv_ref[:, width + seq * chunk : width + (seq + 1) * chunk]
+        rows[2:3, :] = up_off_ref[:, seq * width : (seq + 1) * width]
+        rows[3:4, :chunk] = proj_off_ref[:, own]
+        rows[3:4, chunk : 2 * chunk] = down_off_ref[:, own]
+        packed_ref[seq, tok:] = rows[...].astype(BF)
+
+
+def mod_grad_kernel(spec, me_ref, small_ref, cond_ref, matrix_ref, grad_ref, sums_ref, dcond_ref):
+    n_seq = spec
+    columns = matrix_ref.shape[1]
+    dmod = small_ref[:, :columns]
+    grad_ref[...] = dot_outer(cond_ref[...], dmod)
+    sums_ref[...] = total(small_ref[...])
+    dcond = dot_back(dmod, matrix_ref[...])
+    held = dcond_ref.shape[1]
+    for index in range(dcond_ref.shape[0]):
+        first = index // n_seq * held
+        dcond_ref[index] = dcond[first : first + held]
+
+
+def chunks(width, chunk):
     table = []
     for seq in range(width // chunk):
         entry = []
@@ -376,10 +500,10 @@
     return table
 
 
-def pick(refs, me, seq):
-    value = refs[0][...]
-    for mask in range(1, len(refs)):
-        value = jnp.where((me ^ seq) == mask, refs[mask][...], value)
+def pick(values, me, seq):
+    value = values[0]
+    for mask in range(1, len(values)):
+        value = jnp.where((me ^ seq) == mask, values[mask], value)
     return value
 
 
@@ -388,8 +512,8 @@
     blocks, (units_ref, qkv_off_ref, proj_off_ref, up_off_ref, down_off_ref) = refs[:n_seq], refs[n_seq:]
     me = me_ref[0]
     qkv_off_ref[...] = jnp.zeros_like(qkv_off_ref)
-    for seq, entry in enumerate(chunks(width, chunk, 0)):
-        value = pick(blocks, me, seq)
+    for seq, entry in enumerate(chunks(width, chunk)):
+        value = pick([ref[...] for ref in blocks], me, seq)
         for unit, there, here, columns in entry:
             units_ref[unit, :, there : there + columns] = value[:rows, here : here + columns]
         tail = value[rows:].astype(F32)
@@ -399,12 +523,11 @@
         up_off_ref[:, seq * width : (seq + 1) * width] = tail[1:2]
 
 
-def spread2_kernel(spec, me_ref, *refs):
+def spread2_kernel(spec, me_ref, own_ref, far_ref, near_ref, units_ref):
     width, chunk, wide, n_seq = spec
-    blocks, units_ref = refs[:n_seq], refs[n_seq]
     me = me_ref[0]
     for seq in range(n_seq):
-        value = pick(blocks, me, seq)
+        value = pick([own_ref[...], near_ref[0], far_ref[...], near_ref[1]], me, seq)
         units_ref[seq] = value[0]
         for unit in range(wide):
             units_ref[wide + unit, :, seq * chunk : (seq + 1) * chunk] = value[
@@ -412,10 +535,28 @@
             ]
 
 
+def add_kernel(spec, me_ref, *refs):
+    outs = refs[len(refs) * spec // (spec + 1) :]
+    for index, out in enumerate(outs):
+        terms = refs[index * spec : (index + 1) * spec]
+        for unit in range(out.shape[0]):
+            value = terms[0][0, unit].astype(F32)
+            for term in terms[1:]:
+                value = value + term[unit].astype(F32)
+            out[unit] = value.astype(BF)
+
+
+def cut_kernel(spec, me_ref, over_x, over_y, low, high):
+    low[...] = over_x[...]
+    high[...] = over_y[...]
+
+
 def summed(refs, unit):
-    kept, other, over_x, over_y = refs
-    value = kept[0, unit].astype(F32) + other[0, unit].astype(F32)
-    return value + (over_x[unit].astype(F32) + over_y[unit].astype(F32))
+    kept, other, x_low, x_high, y_low, y_high = refs
+    middle = x_low.shape[0]
+    over_x, over_y = (x_low, y_low) if unit < middle else (x_high, y_high)
+    value = kept[0, unit].astype(F32) + other[unit].astype(F32)
+    return value + (over_x[unit % middle].astype(F32) + over_y[unit % middle].astype(F32))
 
 
 def send_blocks(scratch, outs, me, sems):
@@ -428,8 +569,8 @@
 
 def collect1_kernel(spec, me_ref, *refs):
     width, chunk, wide, n_seq = spec
-    ins, outs, (scratch, sems) = refs[:4], refs[4 : 4 + n_seq], refs[4 + n_seq :]
-    table = chunks(width, chunk, wide)
+    ins, outs, (scratch, sems) = refs[:6], refs[6 : 6 + n_seq], refs[6 + n_seq :]
+    table = chunks(width, chunk)
     for unit in range(4):
         value = summed(ins, unit).astype(BF)
         for seq, entry in enumerate(table):
@@ -441,7 +582,7 @@
 
 def collect2_kernel(spec, me_ref, *refs):
     width, chunk, wide, n_seq = spec
-    ins, outs, (scratch, sems) = refs[:4], refs[4 : 4 + n_seq], refs[4 + n_seq :]
+    ins, outs, (scratch, sems) = refs[:6], refs[6 : 6 + n_seq], refs[6 + n_seq :]
     for unit in range(wide):
         scratch[unit, 0] = summed(ins, unit).astype(BF)
         value = summed(ins, wide + unit).astype(BF)
@@ -475,19 +616,37 @@
                 down_ref[unit * rows : (unit + 1) * rows] = value[:, unit * chunk : (unit + 1) * chunk]
 
 
-def call(body, spec, me, inputs, pieces, outs, far_outs, scratch, name):
+def call(body, spec, me, inputs, pieces, outs, far_outs, scratch, name, first=(), flops=0):
     vmem = pl.BlockSpec(memory_space=pltpu.VMEM)
     far = pl.BlockSpec(memory_space=pl.ANY)
+    specs, arrays = [], []
+    for value in inputs:
+        if isinstance(value, tuple):
+            value, index, shape = value
+            index = index + (0,) * (value.ndim - len(index))
+            shape = shape + value.shape[len(shape) :]
+            specs.append(pl.BlockSpec(shape, lambda step, index=index: index))
+        else:
+            specs.append(vmem)
+        arrays.append(value)
+    used = 1 + len(inputs) + len(pieces)
+
+    def run(*refs):
+        body(spec, *refs[:used], *refs[used + len(first) :])
+
     return pl.pallas_call(
-        functools.partial(body, spec),
+        run,
+        grid=(1,),
         out_shape=far_outs + outs,
-        in_specs=[pl.BlockSpec(memory_space=pltpu.SMEM)] + [vmem] * len(inputs) + [far] * len(pieces),
+        in_specs=[pl.BlockSpec(memory_space=pltpu.SMEM)]
+        + specs
+        + [far] * (len(pieces) + len(first)),
         out_specs=[far] * len(far_outs) + [vmem] * len(outs),
         scratch_shapes=scratch,
         compiler_params=pltpu.CompilerParams(vmem_limit_bytes=52 * 1024 * 1024),
-        cost_estimate=pl.CostEstimate(flops=0, bytes_accessed=0, transcendentals=0),
+        cost_estimate=pl.CostEstimate(flops=flops, bytes_accessed=0, transcendentals=0),
         name=name,
-    )(me, *inputs, *pieces)
+    )(me, *arrays, *pieces, *first)
 
 
 def local(
@@ -517,7 +676,15 @@
     head = width // H
     assert 2 * head == 128
     factor = head ** (-0.5)
-    layout = Layout(n_dp, rows, width)
+    layout = Layout(n_dp, n_seq, rows, width)
+
+    def to_latents(values):
+        return lax.all_to_all(values, "seq", 0, 0, tiled=True)
+
+    def to_tokens(values):
+        values = values.reshape(n_seq, tok, width)
+        values = lax.all_to_all(values, "seq", 0, 0, tiled=True)
+        return values.reshape(micro, lats, tok, width)
 
     shaped = jax.ShapeDtypeStruct
     dma = pltpu.SemaphoreType.DMA
@@ -525,75 +692,91 @@
     spec_seq = (width, chunk, wide, n_seq)
     offsets_low = jnp.concatenate([querybias, valuebias, projbias, contractbias, expandbias])
     tail = jnp.pad(offsets_low.reshape(-1, width), ((0, 14), (0, 0)))
+    down_shard = contract.reshape(wide, rows, chunk)
     shards1 = jnp.concatenate([jnp.concatenate([qkvweight, projection], axis=1), tail])
-    down_shard = contract.reshape(wide, rows, chunk)
     shards2 = jnp.stack([expand, jnp.concatenate([down_shard[i] for i in range(wide)], axis=1)])
-    blocks1 = [shards1] + swap_seq(shards1)
-    blocks2 = [shards2] + swap_seq(shards2)
-    offset_shapes = [shaped((1, n), F32) for n in (3 * width, width, wide * width, width)]
+    if layout.direct:
+        blocks1 = [shards1] + swap_seq([shards1] * (n_seq - 1))
+    else:
+        blocks1, blocks2 = gather_seq(shards1), gather_seq(shards2)
+
+    cond_float = conditions.reshape(held, width).astype(F32)
+    cond_act = jax.nn.silu(cond_float).astype(BF)
+    cond_parts = cond_act.reshape(held, n_dp, rows)
+    if layout.direct:
+        (cond_parts,) = after([cond_parts], [swap(modbias, "dp", 0)])
+    cond_rows = lax.all_to_all(cond_parts, "dp", 1, 0, tiled=True).reshape(n_dp * held, rows)
+    part = jnp.dot(cond_rows, modulator, preferred_element_type=F32)
+    part = part + jnp.where(lax.axis_index("dp") == 0, modbias.astype(F32), 0.0)
+    part = lax.all_to_all(part.reshape(n_dp, held, -1), "dp", 0, 0, tiled=True)
+
+    def pack(*first):
+        return call(
+            pack_kernel, None, here, [latents.reshape(held, tok, width), part], [],
+            [shaped((held, tok + 16, width), BF)], [], [pltpu.VMEM((16, width), F32)], "pack", first,
+        )[0]
+
+    offset_shapes = [shaped((1, n), F32) for n in ( 3 * width, width, wide * width, width)]
     if layout.direct:
         me = lax.axis_index("dp").reshape(1).astype(jnp.int32)
         u1, offsets, proj_offset, up_offset, down_offset = call(
             spread1_kernel, (width, chunk, rows, n_seq), here, blocks1, [],
-            [shaped((4, rows, width), BF)] + offset_shapes, [], [], "spread1",
+            [shaped((4, rows, width), BF)] + offset_shapes, [], [], "spread1", [part],
         )
+        (shards2,) = after([shards2], blocks1[1:])
+        far2 = swap(shards2, "seq", 1)
+        near2 = swap(jnp.stack([shards2, far2]), "seq", 0)
+        w1 = gather_square(u1, [near2])
         (u2,) = call(
-            spread2_kernel, spec_seq, here, blocks2, [],
-            [shaped((2 * wide, rows, width), BF)], [], [], "spread2",
+            spread2_kernel, spec_seq, here, [shards2, far2, near2], [],
+            [shaped((2 * wide, rows, width), BF)], [], [], "spread2", [w1[6][0], w1[8][0]],
         )
-        w1, w2 = gather_square(u1), gather_square(u2)
+        packed = to_latents(pack(near2))
+        (cotangent,) = call(
+            copy_kernel, None, here, [cotangent], [],
+            [shaped(cotangent.shape, BF)], [], [], "cotangent", [packed],
+        )
+        cot = to_latents(cotangent.reshape(held, tok, width)).reshape(length, width)
     else:
+        packed = to_latents(pack())
+        cot = to_latents(cotangent.reshape(held, tok, width)).reshape(length, width)
         me = jnp.zeros((1,), jnp.int32)
         order = jnp.arange(n_seq) ^ lax.axis_index("seq")
-        b1 = jnp.take(jnp.stack(blocks1), order, axis=0)
-        b2 = jnp.take(jnp.stack(blocks2), order, axis=0)
-        u_qkv = b1[:, :rows, : 3 * chunk].transpose(1, 0, 2).reshape(rows, 3, width).transpose(1, 0, 2)
-        u_proj = b1[:, :rows, 3 * chunk :].transpose(1, 0, 2).reshape(1, rows, width)
-        u_up = b2[:, 0].transpose(1, 0, 2).reshape(rows, wide, width).transpose(1, 0, 2)
-        u_down = b2[:, 1].reshape(n_seq, rows, wide, chunk).transpose(2, 1, 0, 3).reshape(wide, rows, width)
+        b1, b2 = (jnp.take(jnp.stack(b), order, axis=0) for b in (blocks1, blocks2))
+        b1, b_off = b1[:, :rows], b1[:, rows:]
+        b_up, b_down = b2[:, 0], b2[:, 1]
+        u_qkv = b1[:, :, : 3 * chunk].transpose(1, 0, 2).reshape(rows, 3, width).transpose(1, 0, 2)
+        u_proj = b1[:, :, 3 * chunk :].transpose(1, 0, 2).reshape(1, rows, width)
+        u_up = b_up.transpose(1, 0, 2).reshape(rows, wide, width).transpose(1, 0, 2)
+        u_down = b_down.reshape(n_seq, rows, wide, chunk).transpose(2, 1, 0, 3).reshape(wide, rows, width)
         natural = lambda v: gather_dp(v).transpose(1, 0, 2, 3).reshape(v.shape[0], width, width)
         w1 = [(natural(jnp.concatenate([u_qkv, u_proj])), 0, 0)]
         w2 = [(natural(u_up), 0, 0), (gather_dp(u_down).reshape(wide, width, width), 0, wide)]
-        four = b1[:, rows].reshape(n_seq, 4, chunk).transpose(1, 0, 2).reshape(4, 1, width).astype(F32)
+        four = b_off[:, 0].reshape(n_seq, 4, chunk).transpose(1, 0, 2).reshape(4, 1, width).astype(F32)
         offsets = jnp.concatenate([four[0], jnp.zeros_like(four[0]), four[1]], axis=1)
         proj_offset, down_offset = four[2], four[3]
-        up_offset = b1[:, rows + 1].reshape(1, -1).astype(F32)
+        up_offset = b_off[:, 1].reshape(1, -1).astype(F32)
     arrays1, spec1 = [w[0] for w in w1], tuple(w[1:] for w in w1)
-    arrays2, spec2 = [w[0] for w in w2], tuple(w[1:] for w in w2)
-
-    def to_latents(values):
-        values = values.reshape(held, tok, width)
-        return lax.all_to_all(values, "seq", 0, 0, tiled=True).reshape(length, width)
-
-    def to_tokens(*values):
-        values = jnp.stack([v.reshape(n_seq, tok, width) for v in values], axis=1)
-        values = lax.all_to_all(values, "seq", 0, 0, tiled=True)
-        return [values[:, i].reshape(micro, lats, tok, width) for i in range(values.shape[1])]
-
-    tokens = to_latents(latents)
-    cot = to_latents(cotangent)
-
-    cond_float = conditions.reshape(held, width).astype(F32)
-    cond_act = jax.nn.silu(cond_float).astype(BF)
-    cond_rows = lax.all_to_all(
-        cond_act.reshape(held, n_dp, rows), "dp", 1, 0, tiled=True
-    ).reshape(n_dp * held, rows)
-    part = jnp.dot(cond_rows, modulator, preferred_element_type=F32)
-    part = part + jnp.where(lax.axis_index("dp") == 0, modbias.astype(F32), 0.0)
-    part = lax.all_to_all(part, ("dp", "seq"), 0, 0, tiled=True)
-    mod = jnp.sum(part.reshape(n_dp, n_seq, -1), axis=0)
-    mod = mod.reshape(1, -1)
 
     pairs = H // 2
     blocks, block_rows = layout.blocks, layout.rows
-    places = max(blocks // 2, 1)
-    n_far = min(blocks, 2)
-    n1, n2 = len(w1), len(w2)
-    hidden1, qkv, attended, branch1, middle = call(
+
+    def far_shapes(units):
+        if not layout.direct:
+            return [shaped((1, units, block_rows, width), BF)]
+        block = (block_rows, width)
+        return (
+            [shaped((4, units) + block, BF)]
+            + [shaped((units,) + block, BF)] * 3
+            + [shaped((units // 2,) + block, BF)] * 2
+        )
+
+    n1, n2 = len(w1), 10 if layout.direct else len(w2)
+    hidden1, qkv, attended, branch1, middle, mod, tokens = call(
         attend_kernel,
         (width, spec1, factor, pairs),
         me,
-        [tokens, mod, offsets, proj_offset],
+        [packed, offsets, proj_offset],
         arrays1,
         [
             shaped((length, width), BF),
@@ -601,11 +784,16 @@
             shaped((length, width), BF),
             shaped((length, width), F32),
             shaped((length, width), F32),
+            shaped((1, 6 * width), F32),
+            shaped((length, width), BF),
         ],
         [],
         [pltpu.VMEM((4, blocks, block_rows, width), BF), dma((n1,))],
         "attention",
     )
+    if layout.direct:
+        w2 = gather_square(u2, [middle, cot])
+    arrays2, spec2 = [w[0] for w in w2], tuple(w[1:] for w in w2)
     *grads2, result, dbefore, dgate2, up_bias, down_bias = call(
         mlp_kernel,
         (width, wide, spec2),
@@ -619,7 +807,7 @@
             shaped((1, wide * width), F32),
             shaped((1, width), F32),
         ],
-        [shaped((places, 2 * wide, block_rows, width), BF)] * n_far,
+        far_shapes(2 * wide),
         [
             pltpu.VMEM((wide, blocks, block_rows, width), BF),
             pltpu.VMEM((blocks, wide, block_rows, width), BF),
@@ -629,86 +817,123 @@
             pltpu.VMEM((wide, length, width), F32),
             dma((n2,)),
             dma((n2,)),
-            dma((2 * blocks,)),
+            dma((2 * blocks + 2,)),
         ],
         "mlp",
     )
-    *grads1, dmiddle, dqkv, sums1, bias1 = call(
-        attend_back_kernel,
-        (width, wide, spec2, spec1, factor, pairs),
+    dmiddle, dbranch1, datt, sums1, proj_bias = call(
+        middle_back_kernel,
+        (width, wide, spec2, spec1),
         me,
-        [middle, mod, cot, dbefore, branch1, attended, hidden1, qkv],
+        [middle, mod, cot, dbefore, branch1],
         arrays2 + arrays1,
         [
             shaped((length, width), F32),
-            shaped((3, length, width), BF),
+            shaped((length, width), BF),
+            shaped((length, width), BF),
             shaped((1, 3 * width), F32),
-            shaped((1, 3 * width), F32),
+            shaped((1, width), F32),
         ],
-        [shaped((places, 4, block_rows, width), BF)] * n_far,
+        [],
         [
             pltpu.VMEM((wide, blocks, block_rows, width), BF),
             pltpu.VMEM((1, blocks, block_rows, width), BF),
-            pltpu.VMEM((blocks, 4, block_rows, width), BF),
             dma((n2,)),
             dma((n1,)),
-            dma((blocks,)),
         ],
+        "middle_back",
+    )
+    if layout.direct:
+        kept2, others2 = grads2[0], [swap(g, "dp", 0) for g in grads2[1:]]
+        first2 = scatter_first(kept2, others2, [datt])
+        low2, high2 = swap(first2[0], "dp", 2), swap(first2[1], "dp", 1)
+        x_high2, y_low2 = swap(first2[2], "dp", 1), swap(first2[3], "dp", 2)
+        result = to_tokens(result)
+    *grads1, dqkv, qv_bias = call(
+        attend_back_kernel,
+        (width, factor, pairs),
+        me,
+        [dbranch1, datt, attended, hidden1, qkv],
+        [],
+        [shaped((3, length, width), BF), shaped((1, 2 * width), F32)],
+        far_shapes(4),
+        [pltpu.VMEM((blocks, 4, block_rows, width), BF), dma((blocks + 1,))],
         "attention_back",
-    )
-    dtokens, sums0 = call(
+        first2 if layout.direct else (),
+    )
+    if layout.direct:
+        kept1, others1 = grads1[0], [swap(g, "dp", 0) for g in grads1[1:]]
+        last2 = scatter_last(kept2, others2, low2, high2, [dqkv, x_high2, y_low2])
+        x_low2, y_high2 = swap(last2[0], "dp", 1), swap(last2[1], "dp", 2)
+    assert n_seq == 4 and wide == 4
+    (packed,) = call(
         input_back_kernel,
-        (width, spec1),
+        (width, tok, chunk, spec1),
         me,
-        [tokens, mod, dmiddle, dqkv],
+        [tokens, mod, dmiddle, dqkv, sums1, dgate2, qv_bias, proj_bias, up_bias, down_bias],
         arrays1,
-        [shaped((length, width), BF), shaped((1, 2 * width), F32)],
+        [shaped((n_seq, tok + 16, width), BF)],
         [],
-        [pltpu.VMEM((3, blocks, block_rows, width), BF), dma((n1,))],
+        [
+            pltpu.VMEM((3, blocks, block_rows, width), BF),
+            pltpu.VMEM((1, 6 * width), F32),
+            pltpu.VMEM((16, width), F32),
+            dma((n1,)),
+        ],
         "input_back",
-    )
-    result, token_grad = to_tokens(result, dtokens)
-
-    dmod = jnp.concatenate([sums0, sums1, dgate2], axis=1)
-    offset_grads = (
-        bias1[:, :width], bias1[:, width : 2 * width], bias1[:, 2 * width :], up_bias, down_bias
-    )
-    offset_grads = jnp.concatenate([g.reshape(n_seq, -1) for g in offset_grads], axis=1)
-    small = jnp.concatenate([dmod.reshape(n_seq, -1), offset_grads], axis=1).astype(BF)
-    small = jnp.broadcast_to(small[None], (n_dp,) + small.shape).reshape(n_dp * n_seq, -1)
-    small = lax.all_to_all(small, ("dp", "seq"), 0, 0, tiled=True)
-    cols = modulator.shape[1]
-    dmod_all = small[:, :cols]
-    offset_sums = jnp.sum(small[:, cols:].astype(F32), axis=0)
-    grad_mod = jnp.einsum("ld,ln->dn", cond_rows, dmod_all, preferred_element_type=F32)
-    grad_mod_offset = jnp.sum(dmod_all.astype(F32), axis=0)
-    dcond_rows = jnp.einsum("ln,dn->ld", dmod_all, modulator, preferred_element_type=F32)
-    dcond = jnp.broadcast_to(
-        dcond_rows.reshape(n_dp, 1, held, rows), (n_dp, n_seq, held, rows)
-    ).reshape(n_dp * n_seq, held, rows)
+        [result] + list(last2) if layout.direct else (),
+        4 * 10**9,
+    )
+
+    if layout.direct:
+        first1 = scatter_first(kept1, others1, [x_low2, y_high2])
+        low1, high1 = swap(first1[0], "dp", 2), swap(first1[1], "dp", 1)
+        x_high1, y_low1 = swap(first1[2], "dp", 1), swap(first1[3], "dp", 2)
+        (packed,) = after([packed], [x_low2, y_high2])
+    packed = lax.all_to_all(packed, "seq", 0, 0, tiled=True)
+    token_grad = packed[:, :tok].reshape(micro, lats, tok, width)
+    small = packed[:, tok : tok + 4].reshape(n_seq, 4 * width)
+    small = jnp.broadcast_to(small[None], (n_dp,) + small.shape)
+    small = lax.all_to_all(small, "dp", 0, 0, tiled=True).reshape(n_dp * held, 4 * width)
+    grad_mod, row_sums, dcond = call(
+        mod_grad_kernel, n_seq, here, [small, cond_rows, modulator], [],
+        [
+            shaped(modulator.shape, F32),
+            shaped((1, 4 * width), F32),
+            shaped((n_dp * n_seq, held, rows), F32),
+        ],
+        [], [], "mod_grad",
+    )
+    row_sums = row_sums.reshape(4 * width)
+    grad_mod_offset = row_sums[: modulator.shape[1]]
     dcond = lax.all_to_all(dcond, ("dp", "seq"), 0, 0, tiled=True)
-    dcond = jnp.sum(dcond.reshape(n_dp, n_seq, held, rows), axis=1)
-    dcond = dcond.transpose(1, 0, 2).reshape(held, width)
-    dconds = jax.vjp(jax.nn.silu, cond_float)[1](dcond)[0].reshape(micro, lats, width)
-
     if layout.direct:
         blocks2 = call(
-            collect2_kernel, spec_seq, here, list(scatter_square(*grads2)), [], [],
+            collect2_kernel, spec_seq, here,
+            [(kept2, (0,), (1,)), others2[0], x_low2, x_high2, y_low2, y_high2], [], [],
             [shaped((2, rows, width), BF)] * n_seq,
             [pltpu.VMEM((n_seq, 2, rows, width), BF), dma((n_seq,))], "collect2",
         )
+        over_z2 = swap_seq(blocks2[1:])
+        last1 = scatter_last(kept1, others1, low1, high1, [blocks2[0], x_high1, y_low1])
+        x_low1, y_high1 = swap(last1[0], "dp", 1), swap(last1[1], "dp", 2)
+    if layout.direct:
         blocks1 = call(
-            collect1_kernel, spec_seq, here, list(scatter_square(*grads1)), [], [],
+            collect1_kernel, spec_seq, here,
+            [(kept1, (0,), (1,)), others1[0], x_low1, x_high1, y_low1, y_high1], [], [],
             [shaped((rows, width), BF)] * n_seq,
-            [pltpu.VMEM((n_seq, rows, width), BF), dma((n_seq,))], "collect1",
+            [pltpu.VMEM((n_seq, rows, width), BF), dma((n_seq,))], "collect1", over_z2,
         )
+        over_z1 = swap_seq(blocks1[1:])
+
+    if layout.direct:
         up_out, down_out = call(
-            final2_kernel, spec_seq, here, [blocks2[0]] + swap_seq(list(blocks2[1:])), [],
+            final2_kernel, spec_seq, here, [blocks2[0]] + over_z2, [],
             [shaped((rows, width), F32), shaped((wide * rows, chunk), F32)], [], [], "final2",
         )
         qkv_out, proj_out = call(
-            final1_kernel, spec_seq, here, [blocks1[0]] + swap_seq(list(blocks1[1:])), [],
-            [shaped((rows, 3 * chunk), F32), shaped((rows, chunk), F32)], [], [], "final1",
+            final1_kernel, spec_seq, here, [blocks1[0]] + over_z1, [],
+            [shaped((rows, 3 * chunk), F32), shaped((rows, chunk), F32)], [], [], "final1", [dcond],
         )
     else:
         unit_rows = lambda v: v.reshape(-1, n_dp, rows, width).transpose(1, 0, 2, 3)
@@ -721,9 +946,15 @@
         t3 = s_down.reshape(wide * rows, n_seq, chunk).transpose(1, 0, 2)
         r1, up_out, down_out = scatter_seq(t1), scatter_seq(t2), scatter_seq(t3)
         qkv_out, proj_out = r1[:, : 3 * chunk], r1[:, 3 * chunk :]
-    sizes = [b.shape[0] for b in (querybias, valuebias, projbias, expandbias, contractbias)]
-    starts = [sum(sizes[:i]) for i in range(len(sizes))]
-    sums = [offset_sums[a : a + n] for a, n in zip(starts, sizes)]
+        result = to_tokens(result)
+    dcond = jnp.sum(dcond.reshape(n_dp, n_seq, held, rows), axis=1)
+    dcond = dcond.transpose(1, 0, 2).reshape(held, width)
+    dconds = jax.vjp(jax.nn.silu, cond_float)[1](dcond)[0].reshape(micro, lats, width)
+
+    at_q = 3 * width // 2
+    at = [at_q, at_q + chunk, 3 * width, 2 * width, 3 * width + chunk]
+    bias_grads = (querybias, valuebias, projbias, expandbias, contractbias)
+    sums = [row_sums[first : first + b.shape[0]] for first, b in zip(at, bias_grads)]
     return (
         result,
         token_grad,

time: 316 us -> 280 us (0.89)
  waiting for transfers between devices: 134 us -> 85.8 us
  Pallas kernels: 61.2 us -> 75.2 us
  other arithmetic: 17.5 us -> 3.88 us
  local copies, waits for them, and re-layouts: 18.4 us -> 30.8 us
    ppermute x12 -> x9, waiting for transfers between devices: 54 us -> 9.24 us  [swap_seq(): lax.ppermute(value, 'seq', [(i, i ^ mask + 1) for i in range(count)])]
    unnamed x52 -> x120, local copies, waits for them, and re-layouts: 4.28 us -> 19 us
    pallas_call x10 -> x23, Pallas kernels: 61.2 us -> 75.2 us  [the longest x20 75.2 us: call(): pl.pallas_call(run, grid=(1,), out_shape=far_outs + outs, in_specs=[pl.Bl...]
    all_to_all x5 -> x6, waiting for transfers between devices: 24.1 us -> 13.5 us  [the longest x2 7.78 us: to_latents(): return lax.all_to_all(values, 'seq', 0, 0, tiled=True)]
    all_to_all x5 -> x6, starting transfers between devices: 30.9 us -> 22.6 us  [the longest x2 7.24 us: to_latents(): return lax.all_to_all(values, 'seq', 0, 0, tiled=True)]
    all_to_all x1, waiting for transfers between devices: 0.01 us -> 6.89 us  [local(): dcond = lax.all_to_all(dcond, ('dp', 'seq'), 0, 0, tiled=True)]
    add x2 -> x0, other arithmetic: 6.5 us -> none  [scatter_square(): kept[place, units].astype(F32) + other[place, units].astype(F32)]
    slice x8 -> x4, local copies, waits for them, and re-layouts: 9.3 us -> 3.63 us  [the longest x1 1.77 us: local(): token_grad = packed[:, :tok].reshape(micro, lats, tok, width)]
  transfers between devices with their start and end apart: 47 -> 60, of which waited for: 16 -> 23; matrix products, arithmetic and copies ran while one was open for 10% -> 5% of each run, Pallas kernels for 14% -> 18%
where the time goes in v1:
time: 280 us; the launch traced here: 278 us
  waiting for transfers between devices  85.8 us (31%)
  starting transfers between devices  80.8 us (29%)
  Pallas kernels  75.2 us (27%)
  local copies, waits for them, and re-layouts  30.8 us (11%)
  other arithmetic  3.88 us (1%)
    pallas_call x20, Pallas kernels, call(): pl.pallas_call(run, grid=(1,), out_shape=far_outs + outs, in_specs=[pl.Bl...  75.2 us
    ppermute x43, waiting for transfers between devices, swap(): return lax.ppermute(values, axis, [(i, i ^ 1 << bit) for i in range(count)])  54.6 us
    ppermute x43, starting transfers between devices, swap(): return lax.ppermute(values, axis, [(i, i ^ 1 << bit) for i in range(count)])  25.9 us
    ppermute x9, starting transfers between devices, swap_seq(): lax.ppermute(value, 'seq', [(i, i ^ mask + 1) for i in range(count)])  23.1 us
    unnamed x120, local copies, waits for them, and re-layouts  19 us
    ppermute x9, waiting for transfers between devices, swap_seq(): lax.ppermute(value, 'seq', [(i, i ^ mask + 1) for i in range(count)])  9.24 us
    all_to_all x2, waiting for transfers between devices, to_latents(): return lax.all_to_all(values, 'seq', 0, 0, tiled=True)  7.78 us
    all_to_all x2, starting transfers between devices, to_latents(): return lax.all_to_all(values, 'seq', 0, 0, tiled=True)  7.24 us
  transfers between devices with their start and end apart: 60, of which 23 were waited for; matrix products, arithmetic and copies ran while one was open for 5% of the time, Pallas kernels for 18%

profile of v1, /device:TPU:0, one launch (start us, length us, event | category | flops | bytes accessed | tf_op | source)
XLA Modules:
  0.0 277.9 jit_solution(13204253751087882099)
XLA Ops:
  0.7 3.5 %concatenate.14 = bf16[1536]{0:T(1024)(128)(2,1)S(1)} concatenate(bf16[192]{0:T(256)(128)(2,1)} %param.19, bf16[192]{0:T(256)(128)(2,1)} %param.20, bf16[192]{0:T(256)(128)(2,1)} %param.22, bf16[192]{0:T(256)(128)(2,1)} %param.26, bf16[768]{0:T(1024)(128)(2,1)} %param.24), dimensions={0} | concatenate | bytes 6144 | tf_op jit(solution)/shard_map/concatenate | solution.py:693
  5.2 5.1 %collective-permute-start.3 = (bf16[112,768]{1,0:T(8,128)(2,1)S(1)}, bf16[112,768]{1,0:T(8,128)(2,1)S(1)}, u32[]{:S(2)}, u32[]{:S(2)}) collective-permute-start(bf16[112,768]{1,0:T(8,128)(2,1)S(1)} %fusion.1.refs_1_), channel_id=1, source_target_pairs={{0,3},{1,2},{2,1},{3,0},{4,7},{5,6},{6,5},{7,4},{8,11},{9,10},{10,... | collective-permute-start | bytes 516104 | tf_op jit(solution)/shard_map/ppermute | solution.py:151
  16.5 4.0 %all-to-all-start = ((bf16[4,8,96]{2,0,1:T(4,128)(2,1)}), bf16[4,8,96]{2,0,1:T(4,128)(2,1)S(1)}, u32[]{:S(2)}, u32[]{:S(2)}) async-start(bf16[4,8,96]{2,0,1:T(4,128)(2,1)} %copy.43), calls=%async_computation | async-start | bytes 16384 | tf_op jit(solution)/shard_map/all_to_all | solution.py:708
  21.3 3.6 %collective-permute-done.2.refs_2_.refs_3_ = bf16[112,768]{1,0:T(8,128)(2,1)S(1)} collective-permute-done((bf16[112,768]{1,0:T(8,128)(2,1)S(1)}, bf16[112,768]{1,0:T(8,128)(2,1)S(1)}, u32[]{:S(2)}, u32[]{:S(2)}) %collective-permute-start.2) | collective-permute-done | bytes 172064 | tf_op jit(solution)/shard_map/ppermute | solution.py:151
  27.1 3.7 %all-to-all-start.1 = ((f32[8,4,1152]{2,1,0:T(4,128)}), f32[8,4,1152]{2,1,0:T(4,128)S(1)}, u32[]{:S(2)}, u32[]{:S(2)}) async-start(f32[8,4,1152]{2,1,0:T(4,128)} %reshape.100), calls=%async_computation.1 | async-start | bytes 294912 | tf_op jit(solution)/shard_map/all_to_all | solution.py:711
  30.8 5.7 %all-to-all-done.1.refs_2_.refs_5_ = f32[8,4,1152]{2,1,0:T(4,128)S(1)} async-done(((f32[8,4,1152]{2,1,0:T(4,128)}), f32[8,4,1152]{2,1,0:T(4,128)S(1)}, u32[]{:S(2)}, u32[]{:S(2)}) %all-to-all-start.1) | async-done | bytes 147488 | tf_op jit(solution)/shard_map/all_to_all | solution.py:711
  41.7 3.1 %collective-permute-start.5 = (bf16[2,2,96,768]{3,2,1,0:T(8,128)(2,1)S(1)}, bf16[2,2,96,768]{3,2,1,0:T(8,128)(2,1)S(1)}, u32[]{:S(2)}, u32[]{:S(2)}) collective-permute-start(bf16[2,2,96,768]{3,2,1,0:T(8,128)(2,1)S(1)} %pad_maximum_fusion), channel_id=1, source_target_pairs={{0,1},{1,0},{2,3},{3,2},{4,5},{5,4},{6,7},{7,6},{8,9},{9,8},{10,11... | collective-permute-start | bytes 1769480 | tf_op jit(solution)/shard_map/ppermute | solution.py:24
  44.8 10.9 %collective-permute-done.9.refs_2_.refs_8_.refs_20_.refs_15_ = bf16[4,96,768]{2,1,0:T(8,128)(2,1)S(1)} collective-permute-done((bf16[4,96,768]{2,1,0:T(8,128)(2,1)}, bf16[4,96,768]{2,1,0:T(8,128)(2,1)S(1)}, u32[]{:S(2)}, u32[]{:S(2)}) %collective-permute-start.9) | collective-permute-done | bytes 589856 | tf_op jit(solution)/shard_map/ppermute | solution.py:24
  55.8 1.6 collective-permute-done.5.refs_3_
  59.1 1.5 collective-permute-start.11
  63.9 3.6 %all-to-all-start.2 = ((bf16[4,80,768]{2,1,0:T(8,128)(2,1)}), bf16[4,80,768]{2,1,0:T(8,128)(2,1)S(1)}, u32[]{:S(2)}, u32[]{:S(2)}) async-start(bf16[4,80,768]{2,1,0:T(8,128)(2,1)} %copy-done.10), calls=%async_computation.2 | async-start | bytes 983040 | tf_op jit(solution)/shard_map/all_to_all | solution.py:682
  68.0 1.4 spread2.1.refs_6_
  71.8 7.8 %all-to-all-done.2.refs_1_.refs_2_ = bf16[4,80,768]{2,1,0:T(8,128)(2,1)S(1)} async-done(((bf16[4,80,768]{2,1,0:T(8,128)(2,1)}), bf16[4,80,768]{2,1,0:T(8,128)(2,1)S(1)}, u32[]{:S(2)}, u32[]{:S(2)}) %all-to-all-start.2) | async-done | bytes 491552 | tf_op jit(solution)/shard_map/all_to_all | solution.py:682
  81.4 3.6 %all-to-all-start.3 = ((bf16[4,64,768]{2,1,0:T(8,128)(2,1)}), bf16[4,64,768]{2,1,0:T(8,128)(2,1)S(1)}, u32[]{:S(2)}, u32[]{:S(2)}) async-start(bf16[4,64,768]{2,1,0:T(8,128)(2,1)} %bitcast.10), calls=%async_computation.3 | async-start | bytes 786432 | tf_op jit(solution)/shard_map/all_to_all | solution.py:682
  87.9 7.9 %attention.1 = (bf16[256,768]{1,0:T(8,128)(2,1)S(1)}, bf16[3,256,768]{2,1,0:T(8,128)(2,1)}, bf16[256,768]{1,0:T(8,128)(2,1)S(1)}, f32[256,768]{1,0:T(8,128)}, f3...) custom-call(s32[1]{0:T(128)} %bitcast.refs_0_, bf16[4,80,768]{2,1,0:T(8,128)(2,1)} %copy-done.9, ...), custom_call_target="tpu_custom_call" | custom-call | tf_op jit(solution)/shard_map/attention/pallas_call | solution.py:637
  96.5 1.6 cut.3
  100.0 13.6 %collective-permute-done.20.refs_12_ = bf16[4,96,768]{2,1,0:T(8,128)(2,1)S(1)} collective-permute-done((bf16[4,96,768]{2,1,0:T(8,128)(2,1)S(1)}, bf16[4,96,768]{2,1,0:T(8,128)(2,1)S(1)}, u32[]{:S(2)}, u32[]{:S(2)}) %collective-permute-start.20) | collective-permute-done | bytes 589856 | tf_op jit(solution)/shard_map/ppermute | solution.py:24
  117.4 17.2 %mlp.1 = (bf16[4,8,96,768]{3,2,1,0:T(8,128)(2,1)}, bf16[8,96,768]{2,1,0:T(8,128)(2,1)}, bf16[8,96,768]{2,1,0:T(8,128)(2,1)}, bf16[8,96,768]{2,1,0:T(8,128)(2,1)}...) custom-call(s32[1]{0:T(128)} %bitcast.refs_0_, ...), custom_call_target="tpu_custom_call" | custom-call | tf_op jit(solution)/shard_map/mlp/pallas_call | solution.py:637
  135.6 7.7 %middle_back.1 = (f32[256,768]{1,0:T(8,128)}, bf16[256,768]{1,0:T(8,128)(2,1)S(1)}, bf16[256,768]{1,0:T(8,128)(2,1)S(1)}, f32[1,2304]{1,0:T(1,128)S(1)}, f32[1,768]{1,0:T(1,128)S(1)}) custom-call(s32[1]{0:T(128)} %bitcast.refs_0_, f32[256,768]{1,0:T(8,128)} %get-tuple-element.86.refs_3_.refs_1_, f32[1,4608]{1,0:T(1,128)S(1)} %get-tuple-element.87.refs_2_, ...), custom_call_target="tpu_custom_call" | custom-call | tf_op jit(solution)/shard_map/middle_back/pallas_call | solution.py:637
  145.1 3.5 %first_sums.2 = (bf16[4,96,768]{2,1,0:T(8,128)(2,1)S(1)}, bf16[4,96,768]{2,1,0:T(8,128)(2,1)S(1)}, bf16[4,96,768]{2,1,0:T(8,128)(2,1)}, bf16[4,96,768]{2,1,0:T(8,128)(2,1)}) custom-call(s32[1]{0:T(128)} %constant.21.clone.1.refs_0_, bf16[4,8,96,768]{3,2,1,0:T(8,128)(2,1)} %get-tuple-element.102.refs_1_.refs_3_.refs_5_.refs_7_.refs_4_, ...), custom_call_target="tpu_custom_call" | custom-call | tf_op jit(solution)/shard_map/first_sums/pallas_call | solution.py:637
  148.7 1.5 collective-permute-start.28
  152.7 12.6 %attention_back.1 = (bf16[4,4,96,768]{3,2,1,0:T(8,128)(2,1)}, bf16[4,96,768]{2,1,0:T(8,128)(2,1)}, bf16[4,96,768]{2,1,0:T(8,128)(2,1)}, bf16[4,96,768]{2,1,0:T(8...) custom-call(s32[1]{0:T(128)} %bitcast.refs_0_, ...), custom_call_target="tpu_custom_call" | custom-call | tf_op jit(solution)/shard_map/attention_back/pallas_call | solution.py:637
  166.4 11.5 %collective-permute-done.30.refs_8_.refs_4_ = bf16[4,96,768]{2,1,0:T(8,128)(2,1)S(1)} collective-permute-done((bf16[4,96,768]{2,1,0:T(8,128)(2,1)}, bf16[4,96,768]{2,1,0:T(8,128)(2,1)S(1)}, u32[]{:S(2)}, u32[]{:S(2)}) %collective-permute-start.30) | collective-permute-done | bytes 589856 | tf_op jit(solution)/shard_map/ppermute | solution.py:24
  178.9 2.8 %last_sums.2 = (bf16[4,96,768]{2,1,0:T(8,128)(2,1)S(1)}, bf16[4,96,768]{2,1,0:T(8,128)(2,1)}) custom-call(s32[1]{0:T(128)} %constant.21.clone.1.refs_0_, bf16[4,8,96,768]{3,2,1,0:T(8,128)(2,1)} %get-tuple-element.102.refs_1_.refs_3_.refs_5_.refs_7_.refs_4_, bf16[8,96,768]{2,1,0:T(8,128)(2,1)} %copy-done.40, ...), custom_call_target="tpu_custom_call" | custom-call | tf_op jit(solution)/shard_map/last_sums/pallas_call | solution.py:637
  183.0 4.8 %all-to-all-start.4 = ((bf16[4,64,768]{2,1,0:T(8,128)(2,1)}), bf16[4,64,768]{2,1,0:T(8,128)(2,1)}, u32[]{:S(2)}, u32[]{:S(2)}) async-start(bf16[4,64,768]{2,1,0:T(8,128)(2,1)} %bitcast.12), calls=%async_computation.4 | async-start | bytes 786432 | tf_op jit(solution)/shard_map/all_to_all | solution.py:686
  188.3 7.6 %collective-permute-done.32.refs_1_.refs_9_.refs_3_ = bf16[4,96,768]{2,1,0:T(8,128)(2,1)S(1)} collective-permute-done((bf16[4,96,768]{2,1,0:T(8,128)(2,1)S(1)}, bf16[4,96,768]{2,1,0:T(8,128)(2,1)S(1)}, u32[]{:S(2)}, u32[]{:S(2)}) %collective-permute-start.32) | collective-permute-done | bytes 589856 | tf_op jit(solution)/shard_map/ppermute | solution.py:24
  196.7 1.6 all-to-all-done.4
  199.2 5.4 %input_back.1.refs_0_ = bf16[4,80,768]{2,1,0:T(8,128)(2,1)} custom-call(s32[1]{0:T(128)} %bitcast.refs_0_, bf16[256,768]{1,0:T(8,128)(2,1)S(1)} %copy-done.38, f32[1,4608]{1,0:T(1,128)S(1)} %get-tuple-element.87.refs_2_, f32[256,768]{1,0:T(8,128)} %get-tuple-element.96.refs_3_, bf16[3,256,768]{2,1,0:T(8,128)(2,1)} %get-tuple-element.111.refs_7_.refs_4_, ...), custom_call_target="tpu_custom_call" | custom-call | flops 4000000000 | tf_op jit(solution)/shard_map/input_back/pallas_call | solution.py:637
  204.7 4.1 %all-to-all-start.5 = ((bf16[4,80,768]{2,1,0:T(8,128)(2,1)}), bf16[4,80,768]{2,1,0:T(8,128)(2,1)}, u32[]{:S(2)}, u32[]{:S(2)}) async-start(bf16[4,80,768]{2,1,0:T(8,128)(2,1)} %after.5), calls=%async_computation.5 | async-start | bytes 983040 | tf_op jit(solution)/shard_map/all_to_all | solution.py:893
  208.9 1.7 first_sums.3
  210.6 1.5 collective-permute-start.39
  214.7 3.2 %collect2.1 = (bf16[2,96,768]{2,1,0:T(8,128)(2,1)S(1)}, bf16[2,96,768]{2,1,0:T(8,128)(2,1)S(1)}, bf16[2,96,768]{2,1,0:T(8,128)(2,1)S(1)}, bf16[2,96,768]{2,1,0:T(8,128)(2,1)S(1)}) custom-call(s32[1]{0:T(128)} %bitcast.1.refs_0_, bf16[4,8,96,768]{3,2,1,0:T(8,128)(2,1)} %get-tuple-element.102.refs_1_.refs_3_.refs_5_.refs_7_.refs_4_, ...), custom_call_target="tpu_custom_call" | custom-call | tf_op jit(solution)/shard_map/collect2/pallas_call | solution.py:637
  217.9 2.0 collective-permute-start.46
  220.6 1.4 collective-permute-done.40.refs_6_
  222.1 2.9 %collective-permute-start.47 = (bf16[2,96,768]{2,1,0:T(8,128)(2,1)S(1)}, bf16[2,96,768]{2,1,0:T(8,128)(2,1)S(1)}, u32[]{:S(2)}, u32[]{:S(2)}) collective-permute-start(bf16[2,96,768]{2,1,0:T(8,128)(2,1)S(1)} %get-tuple-element.138), channel_id=1, source_target_pairs={{0,2},{1,3},{2,0},{3,1},{4,6},{5,7},{6,4},{7,5},{8,10},{9,11},{10,... | collective-permute-start | bytes 884744 | tf_op jit(solution)/shard_map/ppermute | solution.py:151
  225.6 3.5 %collective-permute-start.48 = (bf16[2,96,768]{2,1,0:T(8,128)(2,1)S(1)}, bf16[2,96,768]{2,1,0:T(8,128)(2,1)S(1)}, u32[]{:S(2)}, u32[]{:S(2)}) collective-permute-start(bf16[2,96,768]{2,1,0:T(8,128)(2,1)S(1)} %get-tuple-element.139), channel_id=1, source_target_pairs={{0,3},{1,2},{2,1},{3,0},{4,7},{5,6},{6,5},{7,4},{8,11},{9,10},{10,... | collective-permute-start | bytes 884744 | tf_op jit(solution)/shard_map/ppermute | solution.py:151
  229.9 2.1 last_sums.3
  233.2 1.4 collective-permute-start.45
  236.2 3.5 %all-to-all-start.6 = ((bf16[8,4,3072]{2,1,0:T(4,128)(2,1)}), bf16[8,4,3072]{2,1,0:T(4,128)(2,1)S(1)}, u32[]{:S(2)}, u32[]{:S(2)}) async-start(bf16[8,4,3072]{2,1,0:T(4,128)(2,1)} %broadcast_in_dim.14), calls=%async_computation.6 | async-start | bytes 393216 | tf_op jit(solution)/shard_map/all_to_all | solution.py:897
  239.7 5.6 %collective-permute-done.47.refs_8_.refs_3_ = bf16[2,96,768]{2,1,0:T(8,128)(2,1)S(1)} collective-permute-done((bf16[2,96,768]{2,1,0:T(8,128)(2,1)S(1)}, bf16[2,96,768]{2,1,0:T(8,128)(2,1)S(1)}, u32[]{:S(2)}, u32[]{:S(2)}) %collective-permute-start.47) | collective-permute-done | bytes 294944 | tf_op jit(solution)/shard_map/ppermute | solution.py:151
  247.2 2.4 collect1.1
  249.6 5.6 %collective-permute-start.49 = (bf16[96,768]{1,0:T(8,128)(2,1)S(1)}, bf16[96,768]{1,0:T(8,128)(2,1)S(1)}, u32[]{:S(2)}, u32[]{:S(2)}) collective-permute-start(bf16[96,768]{1,0:T(8,128)(2,1)S(1)} %get-tuple-element.141), channel_id=1, source_target_pairs={{0,1},{1,0},{2,3},{3,2},{4,5},{5,4},{6,7},{7,6},{8,9},{9,8},{10,11... | collective-permute-start | bytes 442376 | tf_op jit(solution)/shard_map/ppermute | solution.py:151
  255.2 2.0 collective-permute-start.50
  257.2 1.4 collective-permute-start.51
  258.6 1.8 slice.76
  262.7 4.4 %all-to-all-start.7 = ((f32[32,4,96]{2,1,0:T(4,128)}), f32[32,4,96]{2,1,0:T(4,128)S(1)}, u32[]{:S(2)}, u32[]{:S(2)}) async-start(f32[32,4,96]{2,1,0:T(4,128)} %get-tuple-element.120), calls=%async_computation.7 | async-start | bytes 131072 | tf_op jit(solution)/shard_map/all_to_all | solution.py:909
  267.7 6.9 %all-to-all-done.7.refs_5_ = f32[32,4,96]{2,1,0:T(4,128)S(1)} async-done(((f32[32,4,96]{2,1,0:T(4,128)}), f32[32,4,96]{2,1,0:T(4,128)S(1)}, u32[]{:S(2)}, u32[]{:S(2)}) %all-to-all-start.7) | async-done | bytes 49184 | tf_op jit(solution)/shard_map/all_to_all | solution.py:909
  276.1 1.8 copy.59
  (238 shorter events, 59.1 us)
Async XLA Ops:
  5.2 16.1 %collective-permute-start.3 = (bf16[112,768]{1,0:T(8,128)(2,1)S(1)}, bf16[112,768]{1,0:T(8,128)(2,1)S(1)}, u32[]{:S(2)}, u32[]{:S(2)}) collective-permute-start(bf16[112,768]{1,0:T(8,128)(2,1)S(1)} %fusion.1.refs_1_), channel_id=1, source_target_pairs={{0,3},{1,2},{2,1},{3,0},{4,7},{5,6},{6,5},{7,4},{8,11},{9,10},{10,... | collective-permute-start | bytes 516104 | tf_op jit(solution)/shard_map/ppermute | solution.py:151
  10.3 14.6 %collective-permute-start.2 = (bf16[112,768]{1,0:T(8,128)(2,1)S(1)}, bf16[112,768]{1,0:T(8,128)(2,1)S(1)}, u32[]{:S(2)}, u32[]{:S(2)}) collective-permute-start(bf16[112,768]{1,0:T(8,128)(2,1)S(1)} %fusion.1.refs_1_), channel_id=1, source_target_pairs={{0,2},{1,3},{2,0},{3,1},{4,6},{5,7},{6,4},{7,5},{8,10},{9,11},{10,... | collective-permute-start | bytes 516104 | tf_op jit(solution)/shard_map/ppermute | solution.py:151
  10.3 14.6 %collective-permute-start.1 = (bf16[112,768]{1,0:T(8,128)(2,1)S(1)}, bf16[112,768]{1,0:T(8,128)(2,1)S(1)}, u32[]{:S(2)}, u32[]{:S(2)}) collective-permute-start(bf16[112,768]{1,0:T(8,128)(2,1)S(1)} %fusion.1.refs_1_), channel_id=1, source_target_pairs={{0,1},{1,0},{2,3},{3,2},{4,5},{5,4},{6,7},{7,6},{8,9},{9,8},{10,11... | collective-permute-start | bytes 516104 | tf_op jit(solution)/shard_map/ppermute | solution.py:151
  16.5 9.7 %all-to-all-start = ((bf16[4,8,96]{2,0,1:T(4,128)(2,1)}), bf16[4,8,96]{2,0,1:T(4,128)(2,1)S(1)}, u32[]{:S(2)}, u32[]{:S(2)}) async-start(bf16[4,8,96]{2,0,1:T(4,128)(2,1)} %copy.43), calls=%async_computation | async-start | bytes 16384 | tf_op jit(solution)/shard_map/all_to_all | solution.py:708
  26.2 15.4 %collective-permute-start.4 = (bf16[2,96,768]{2,1,0:T(8,128)(2,1)}, bf16[2,96,768]{2,1,0:T(8,128)(2,1)S(1)}, u32[]{:S(2)}, u32[]{:S(2)}) collective-permute-start(bf16[2,96,768]{2,1,0:T(8,128)(2,1)} %after.4.refs_1_), channel_id=1, source_target_pairs={{0,2},{1,3},{2,0},{3,1},{4,6},{5,7},{6,4},{7,5},{8,10},{9,11},{10,... | collective-permute-start | bytes 884744 | tf_op jit(solution)/shard_map/ppermute | solution.py:24
  40.5 15.2 %collective-permute-start.9 = (bf16[4,96,768]{2,1,0:T(8,128)(2,1)}, bf16[4,96,768]{2,1,0:T(8,128)(2,1)S(1)}, u32[]{:S(2)}, u32[]{:S(2)}) collective-permute-start(bf16[4,96,768]{2,1,0:T(8,128)(2,1)} %get-tuple-element.83.refs_4_.refs_16_.refs_11_), channel_id=1, source_target_pairs={{0,16},{4,20},{8,24},{12,28},{16,0},{20,4},{24,8},{28,12},{1,17},{... | collective-permute-start | bytes 1769480 | tf_op jit(solution)/shard_map/ppermute | solution.py:24
  41.0 14.8 %collective-permute-start.7 = (bf16[4,96,768]{2,1,0:T(8,128)(2,1)}, bf16[4,96,768]{2,1,0:T(8,128)(2,1)S(1)}, u32[]{:S(2)}, u32[]{:S(2)}) collective-permute-start(bf16[4,96,768]{2,1,0:T(8,128)(2,1)} %get-tuple-element.83.refs_4_.refs_16_.refs_11_), channel_id=1, source_target_pairs={{0,8},{4,12},{8,0},{12,4},{16,24},{20,28},{24,16},{28,20},{1,9},{5... | collective-permute-start | bytes 1769480 | tf_op jit(solution)/shard_map/ppermute | solution.py:24
  41.7 15.7 %collective-permute-start.5 = (bf16[2,2,96,768]{3,2,1,0:T(8,128)(2,1)S(1)}, bf16[2,2,96,768]{3,2,1,0:T(8,128)(2,1)S(1)}, u32[]{:S(2)}, u32[]{:S(2)}) collective-permute-start(bf16[2,2,96,768]{3,2,1,0:T(8,128)(2,1)S(1)} %pad_maximum_fusion), channel_id=1, source_target_pairs={{0,1},{1,0},{2,3},{3,2},{4,5},{5,4},{6,7},{7,6},{8,9},{9,8},{10,11... | collective-permute-start | bytes 1769480 | tf_op jit(solution)/shard_map/ppermute | solution.py:24
  63.9 15.7 %all-to-all-start.2 = ((bf16[4,80,768]{2,1,0:T(8,128)(2,1)}), bf16[4,80,768]{2,1,0:T(8,128)(2,1)S(1)}, u32[]{:S(2)}, u32[]{:S(2)}) async-start(bf16[4,80,768]{2,1,0:T(8,128)(2,1)} %copy-done.10), calls=%async_computation.2 | async-start | bytes 983040 | tf_op jit(solution)/shard_map/all_to_all | solution.py:682
  69.4 27.1 %collective-permute-start.18 = (bf16[8,96,768]{2,1,0:T(8,128)(2,1)}, bf16[8,96,768]{2,1,0:T(8,128)(2,1)}, u32[]{:S(2)}, u32[]{:S(2)}) collective-permute-start(bf16[8,96,768]{2,1,0:T(8,128)(2,1)} %spread2.1.refs_6_), channel_id=1, source_target_pairs={{0,16},{4,20},{8,24},{12,28},{16,0},{20,4},{24,8},{28,12},{1,17},{... | collective-permute-start | bytes 3538952 | tf_op jit(solution)/shard_map/ppermute | solution.py:24
  70.0 26.6 %collective-permute-start.16 = (bf16[8,96,768]{2,1,0:T(8,128)(2,1)}, bf16[8,96,768]{2,1,0:T(8,128)(2,1)}, u32[]{:S(2)}, u32[]{:S(2)}) collective-permute-start(bf16[8,96,768]{2,1,0:T(8,128)(2,1)} %spread2.1.refs_6_), channel_id=1, source_target_pairs={{0,8},{4,12},{8,0},{12,4},{16,24},{20,28},{24,16},{28,20},{1,9},{5... | collective-permute-start | bytes 3538952 | tf_op jit(solution)/shard_map/ppermute | solution.py:24
  71.2 13.8 %collective-permute-start.6 = (bf16[4,96,768]{2,1,0:T(8,128)(2,1)}, bf16[4,96,768]{2,1,0:T(8,128)(2,1)}, u32[]{:S(2)}, u32[]{:S(2)}) collective-permute-start(bf16[4,96,768]{2,1,0:T(8,128)(2,1)} %get-tuple-element.83.refs_4_.refs_16_.refs_11_), channel_id=1, source_target_pairs={{0,4},{4,0},{8,12},{12,8},{16,20},{20,16},{24,28},{28,24},{1,5},{5... | collective-permute-start | bytes 1769480 | tf_op jit(solution)/shard_map/ppermute | solution.py:24
  71.3 13.9 %collective-permute-start.10 = (bf16[4,96,768]{2,1,0:T(8,128)(2,1)S(1)}, bf16[4,96,768]{2,1,0:T(8,128)(2,1)}, u32[]{:S(2)}, u32[]{:S(2)}) collective-permute-start(bf16[4,96,768]{2,1,0:T(8,128)(2,1)S(1)} %collective-permute-done.9.refs_2_.refs_8_.refs_20_.refs_15_), channel_id=1, source_target_pairs={{0,4},{4,0},{8,12},{12,8},{16,20},{20,16},{24,28},{28,24},{1,5},{5... | collective-permute-start | bytes 1769480 | tf_op jit(solution)/shard_map/ppermute | solution.py:24
  71.8 13.9 %collective-permute-start.8 = (bf16[4,96,768]{2,1,0:T(8,128)(2,1)S(1)}, bf16[4,96,768]{2,1,0:T(8,128)(2,1)}, u32[]{:S(2)}, u32[]{:S(2)}) collective-permute-start(bf16[4,96,768]{2,1,0:T(8,128)(2,1)S(1)} %collective-permute-done.7.refs_1_.refs_6_.refs_18_.refs_13_), channel_id=1, source_target_pairs={{0,4},{4,0},{8,12},{12,8},{16,20},{20,16},{24,28},{28,24},{1,5},{5... | collective-permute-start | bytes 1769480 | tf_op jit(solution)/shard_map/ppermute | solution.py:24
  81.4 15.1 %all-to-all-start.3 = ((bf16[4,64,768]{2,1,0:T(8,128)(2,1)}), bf16[4,64,768]{2,1,0:T(8,128)(2,1)S(1)}, u32[]{:S(2)}, u32[]{:S(2)}) async-start(bf16[4,64,768]{2,1,0:T(8,128)(2,1)} %bitcast.10), calls=%async_computation.3 | async-start | bytes 786432 | tf_op jit(solution)/shard_map/all_to_all | solution.py:682
  85.7 28.9 %collective-permute-start.15 = (bf16[8,96,768]{2,1,0:T(8,128)(2,1)}, bf16[8,96,768]{2,1,0:T(8,128)(2,1)}, u32[]{:S(2)}, u32[]{:S(2)}) collective-permute-start(bf16[8,96,768]{2,1,0:T(8,128)(2,1)} %spread2.1.refs_6_), channel_id=1, source_target_pairs={{0,4},{4,0},{8,12},{12,8},{16,20},{20,16},{24,28},{28,24},{1,5},{5... | collective-permute-start | bytes 3538952 | tf_op jit(solution)/shard_map/ppermute | solution.py:24
  98.2 15.4 %collective-permute-start.20 = (bf16[4,96,768]{2,1,0:T(8,128)(2,1)S(1)}, bf16[4,96,768]{2,1,0:T(8,128)(2,1)S(1)}, u32[]{:S(2)}, u32[]{:S(2)}) collective-permute-start(bf16[4,96,768]{2,1,0:T(8,128)(2,1)S(1)} %get-tuple-element.90), channel_id=1, source_target_pairs={{0,16},{4,20},{8,24},{12,28},{16,0},{20,4},{24,8},{28,12},{1,17},{... | collective-permute-start | bytes 1769480 | tf_op jit(solution)/shard_map/ppermute | solution.py:24
  98.8 15.8 %collective-permute-start.19 = (bf16[8,96,768]{2,1,0:T(8,128)(2,1)}, bf16[8,96,768]{2,1,0:T(8,128)(2,1)S(1)}, u32[]{:S(2)}, u32[]{:S(2)}) collective-permute-start(bf16[8,96,768]{2,1,0:T(8,128)(2,1)} %collective-permute-done.18.refs_2_.refs_10_), channel_id=1, source_target_pairs={{0,4},{4,0},{8,12},{12,8},{16,20},{20,16},{24,28},{28,24},{1,5},{5... | collective-permute-start | bytes 3538952 | tf_op jit(solution)/shard_map/ppermute | solution.py:24
  98.8 15.8 %collective-permute-start.17 = (bf16[8,96,768]{2,1,0:T(8,128)(2,1)}, bf16[8,96,768]{2,1,0:T(8,128)(2,1)S(1)}, u32[]{:S(2)}, u32[]{:S(2)}) collective-permute-start(bf16[8,96,768]{2,1,0:T(8,128)(2,1)} %collective-permute-done.16.refs_1_.refs_8_), channel_id=1, source_target_pairs={{0,4},{4,0},{8,12},{12,8},{16,20},{20,16},{24,28},{28,24},{1,5},{5... | collective-permute-start | bytes 3538952 | tf_op jit(solution)/shard_map/ppermute | solution.py:24
  99.3 15.2 %collective-permute-start.22 = (bf16[4,96,768]{2,1,0:T(8,128)(2,1)S(1)}, bf16[4,96,768]{2,1,0:T(8,128)(2,1)S(1)}, u32[]{:S(2)}, u32[]{:S(2)}) collective-permute-start(bf16[4,96,768]{2,1,0:T(8,128)(2,1)S(1)} %get-tuple-element.91), channel_id=1, source_target_pairs={{0,8},{4,12},{8,0},{12,4},{16,24},{20,28},{24,16},{28,20},{1,9},{5... | collective-permute-start | bytes 1769480 | tf_op jit(solution)/shard_map/ppermute | solution.py:24
  148.7 16.7 %collective-permute-start.28 = (bf16[4,96,768]{2,1,0:T(8,128)(2,1)S(1)}, bf16[4,96,768]{2,1,0:T(8,128)(2,1)S(1)}, u32[]{:S(2)}, u32[]{:S(2)}) collective-permute-start(bf16[4,96,768]{2,1,0:T(8,128)(2,1)S(1)} %get-tuple-element.107.refs_6_), channel_id=1, source_target_pairs={{0,16},{4,20},{8,24},{12,28},{16,0},{20,4},{24,8},{28,12},{1,17},{... | collective-permute-start | bytes 1769480 | tf_op jit(solution)/shard_map/ppermute | solution.py:24
  150.1 16.2 %collective-permute-start.29 = (bf16[4,96,768]{2,1,0:T(8,128)(2,1)S(1)}, bf16[4,96,768]{2,1,0:T(8,128)(2,1)S(1)}, u32[]{:S(2)}, u32[]{:S(2)}) collective-permute-start(bf16[4,96,768]{2,1,0:T(8,128)(2,1)S(1)} %get-tuple-element.108.refs_7_), channel_id=1, source_target_pairs={{0,8},{4,12},{8,0},{12,4},{16,24},{20,28},{24,16},{28,20},{1,9},{5... | collective-permute-start | bytes 1769480 | tf_op jit(solution)/shard_map/ppermute | solution.py:24
  150.9 27.0 %collective-permute-start.30 = (bf16[4,96,768]{2,1,0:T(8,128)(2,1)}, bf16[4,96,768]{2,1,0:T(8,128)(2,1)S(1)}, u32[]{:S(2)}, u32[]{:S(2)}) collective-permute-start(bf16[4,96,768]{2,1,0:T(8,128)(2,1)} %get-tuple-element.109.refs_8_), channel_id=1, source_target_pairs={{0,8},{4,12},{8,0},{12,4},{16,24},{20,28},{24,16},{28,20},{1,9},{5... | collective-permute-start | bytes 1769480 | tf_op jit(solution)/shard_map/ppermute | solution.py:24
  152.2 25.7 %collective-permute-start.31 = (bf16[4,96,768]{2,1,0:T(8,128)(2,1)}, bf16[4,96,768]{2,1,0:T(8,128)(2,1)S(1)}, u32[]{:S(2)}, u32[]{:S(2)}) collective-permute-start(bf16[4,96,768]{2,1,0:T(8,128)(2,1)} %get-tuple-element.110.refs_9_), channel_id=1, source_target_pairs={{0,16},{4,20},{8,24},{12,28},{16,0},{20,4},{24,8},{28,12},{1,17},{... | collective-permute-start | bytes 1769480 | tf_op jit(solution)/shard_map/ppermute | solution.py:24
  181.7 14.2 %collective-permute-start.32 = (bf16[4,96,768]{2,1,0:T(8,128)(2,1)S(1)}, bf16[4,96,768]{2,1,0:T(8,128)(2,1)S(1)}, u32[]{:S(2)}, u32[]{:S(2)}) collective-permute-start(bf16[4,96,768]{2,1,0:T(8,128)(2,1)S(1)} %get-tuple-element.118.refs_22_), channel_id=1, source_target_pairs={{0,8},{4,12},{8,0},{12,4},{16,24},{20,28},{24,16},{28,20},{1,9},{5... | collective-permute-start | bytes 1769480 | tf_op jit(solution)/shard_map/ppermute | solution.py:24
  182.4 14.2 %collective-permute-start.33 = (bf16[4,96,768]{2,1,0:T(8,128)(2,1)}, bf16[4,96,768]{2,1,0:T(8,128)(2,1)}, u32[]{:S(2)}, u32[]{:S(2)}) collective-permute-start(bf16[4,96,768]{2,1,0:T(8,128)(2,1)} %get-tuple-element.119.refs_23_), channel_id=1, source_target_pairs={{0,16},{4,20},{8,24},{12,28},{16,0},{20,4},{24,8},{28,12},{1,17},{... | collective-permute-start | bytes 1769480 | tf_op jit(solution)/shard_map/ppermute | solution.py:24
  183.0 15.2 %all-to-all-start.4 = ((bf16[4,64,768]{2,1,0:T(8,128)(2,1)}), bf16[4,64,768]{2,1,0:T(8,128)(2,1)}, u32[]{:S(2)}, u32[]{:S(2)}) async-start(bf16[4,64,768]{2,1,0:T(8,128)(2,1)} %bitcast.12), calls=%async_computation.4 | async-start | bytes 786432 | tf_op jit(solution)/shard_map/all_to_all | solution.py:686
  187.8 26.9 %collective-permute-start.41 = (bf16[8,96,768]{2,1,0:T(8,128)(2,1)}, bf16[8,96,768]{2,1,0:T(8,128)(2,1)}, u32[]{:S(2)}, u32[]{:S(2)}) collective-permute-start(bf16[8,96,768]{2,1,0:T(8,128)(2,1)} %get-tuple-element.131), channel_id=1, source_target_pairs={{0,4},{4,0},{8,12},{12,8},{16,20},{20,16},{24,28},{28,24},{1,5},{5... | collective-permute-start | bytes 3538952 | tf_op jit(solution)/shard_map/ppermute | solution.py:24
  187.8 21.0 %collective-permute-start.36 = (bf16[2,96,768]{2,1,0:T(8,128)(2,1)}, bf16[2,96,768]{2,1,0:T(8,128)(2,1)S(1)}, u32[]{:S(2)}, u32[]{:S(2)}) collective-permute-start(bf16[2,96,768]{2,1,0:T(8,128)(2,1)} %copy-done.39), channel_id=1, source_target_pairs={{0,4},{4,0},{8,12},{12,8},{16,20},{20,16},{24,28},{28,24},{1,5},{5... | collective-permute-start | bytes 884744 | tf_op jit(solution)/shard_map/ppermute | solution.py:24
  188.3 20.5 %collective-permute-start.37 = (bf16[2,96,768]{2,1,0:T(8,128)(2,1)S(1)}, bf16[2,96,768]{2,1,0:T(8,128)(2,1)S(1)}, u32[]{:S(2)}, u32[]{:S(2)}) collective-permute-start(bf16[2,96,768]{2,1,0:T(8,128)(2,1)S(1)} %get-tuple-element.127), channel_id=1, source_target_pairs={{0,4},{4,0},{8,12},{12,8},{16,20},{20,16},{24,28},{28,24},{1,5},{5... | collective-permute-start | bytes 884744 | tf_op jit(solution)/shard_map/ppermute | solution.py:24
  195.9 12.9 %collective-permute-start.35 = (bf16[4,96,768]{2,1,0:T(8,128)(2,1)}, bf16[4,96,768]{2,1,0:T(8,128)(2,1)}, u32[]{:S(2)}, u32[]{:S(2)}) collective-permute-start(bf16[4,96,768]{2,1,0:T(8,128)(2,1)} %get-tuple-element.125), channel_id=1, source_target_pairs={{0,4},{4,0},{8,12},{12,8},{16,20},{20,16},{24,28},{28,24},{1,5},{5... | collective-permute-start | bytes 1769480 | tf_op jit(solution)/shard_map/ppermute | solution.py:24
  196.6 12.2 %collective-permute-start.38 = (bf16[4,96,768]{2,1,0:T(8,128)(2,1)}, bf16[4,96,768]{2,1,0:T(8,128)(2,1)}, u32[]{:S(2)}, u32[]{:S(2)}) collective-permute-start(bf16[4,96,768]{2,1,0:T(8,128)(2,1)} %get-tuple-element.128), channel_id=1, source_target_pairs={{0,4},{4,0},{8,12},{12,8},{16,20},{20,16},{24,28},{28,24},{1,5},{5... | collective-permute-start | bytes 1769480 | tf_op jit(solution)/shard_map/ppermute | solution.py:24
  204.7 29.9 %all-to-all-start.5 = ((bf16[4,80,768]{2,1,0:T(8,128)(2,1)}), bf16[4,80,768]{2,1,0:T(8,128)(2,1)}, u32[]{:S(2)}, u32[]{:S(2)}) async-start(bf16[4,80,768]{2,1,0:T(8,128)(2,1)} %after.5), calls=%async_computation.5 | async-start | bytes 983040 | tf_op jit(solution)/shard_map/all_to_all | solution.py:893
  210.6 10.0 %collective-permute-start.39 = (bf16[2,96,768]{2,1,0:T(8,128)(2,1)S(1)}, bf16[2,96,768]{2,1,0:T(8,128)(2,1)S(1)}, u32[]{:S(2)}, u32[]{:S(2)}) collective-permute-start(bf16[2,96,768]{2,1,0:T(8,128)(2,1)S(1)} %get-tuple-element.129), channel_id=1, source_target_pairs={{0,16},{4,20},{8,24},{12,28},{16,0},{20,4},{24,8},{28,12},{1,17},{... | collective-permute-start | bytes 884744 | tf_op jit(solution)/shard_map/ppermute | solution.py:24
  212.1 9.9 %collective-permute-start.40 = (bf16[2,96,768]{2,1,0:T(8,128)(2,1)S(1)}, bf16[2,96,768]{2,1,0:T(8,128)(2,1)S(1)}, u32[]{:S(2)}, u32[]{:S(2)}) collective-permute-start(bf16[2,96,768]{2,1,0:T(8,128)(2,1)S(1)} %get-tuple-element.130), channel_id=1, source_target_pairs={{0,8},{4,12},{8,0},{12,4},{16,24},{20,28},{24,16},{28,20},{1,9},{5... | collective-permute-start | bytes 884744 | tf_op jit(solution)/shard_map/ppermute | solution.py:24
  213.4 12.2 %collective-permute-start.42 = (bf16[2,96,768]{2,1,0:T(8,128)(2,1)S(1)}, bf16[2,96,768]{2,1,0:T(8,128)(2,1)S(1)}, u32[]{:S(2)}, u32[]{:S(2)}) collective-permute-start(bf16[2,96,768]{2,1,0:T(8,128)(2,1)S(1)} %get-tuple-element.133), channel_id=1, source_target_pairs={{0,8},{4,12},{8,0},{12,4},{16,24},{20,28},{24,16},{28,20},{1,9},{5... | collective-permute-start | bytes 884744 | tf_op jit(solution)/shard_map/ppermute | solution.py:24
  214.2 15.0 %collective-permute-start.43 = (bf16[2,96,768]{2,1,0:T(8,128)(2,1)S(1)}, bf16[2,96,768]{2,1,0:T(8,128)(2,1)S(1)}, u32[]{:S(2)}, u32[]{:S(2)}) collective-permute-start(bf16[2,96,768]{2,1,0:T(8,128)(2,1)S(1)} %get-tuple-element.134), channel_id=1, source_target_pairs={{0,16},{4,20},{8,24},{12,28},{16,0},{20,4},{24,8},{28,12},{1,17},{... | collective-permute-start | bytes 884744 | tf_op jit(solution)/shard_map/ppermute | solution.py:24
  217.9 15.3 %collective-permute-start.46 = (bf16[2,96,768]{2,1,0:T(8,128)(2,1)S(1)}, bf16[2,96,768]{2,1,0:T(8,128)(2,1)S(1)}, u32[]{:S(2)}, u32[]{:S(2)}) collective-permute-start(bf16[2,96,768]{2,1,0:T(8,128)(2,1)S(1)} %get-tuple-element.137), channel_id=1, source_target_pairs={{0,1},{1,0},{2,3},{3,2},{4,5},{5,4},{6,7},{7,6},{8,9},{9,8},{10,11... | collective-permute-start | bytes 884744 | tf_op jit(solution)/shard_map/ppermute | solution.py:151
  220.6 26.5 %collective-permute-start.34 = (bf16[4,96,768]{2,1,0:T(8,128)(2,1)}, bf16[4,96,768]{2,1,0:T(8,128)(2,1)}, u32[]{:S(2)}, u32[]{:S(2)}) collective-permute-start(bf16[4,96,768]{2,1,0:T(8,128)(2,1)} %get-tuple-element.124), channel_id=1, source_target_pairs={{0,4},{4,0},{8,12},{12,8},{16,20},{20,16},{24,28},{28,24},{1,5},{5... | collective-permute-start | bytes 1769480 | tf_op jit(solution)/shard_map/ppermute | solution.py:24
  222.1 23.3 %collective-permute-start.47 = (bf16[2,96,768]{2,1,0:T(8,128)(2,1)S(1)}, bf16[2,96,768]{2,1,0:T(8,128)(2,1)S(1)}, u32[]{:S(2)}, u32[]{:S(2)}) collective-permute-start(bf16[2,96,768]{2,1,0:T(8,128)(2,1)S(1)} %get-tuple-element.138), channel_id=1, source_target_pairs={{0,2},{1,3},{2,0},{3,1},{4,6},{5,7},{6,4},{7,5},{8,10},{9,11},{10,... | collective-permute-start | bytes 884744 | tf_op jit(solution)/shard_map/ppermute | solution.py:151
  225.6 19.7 %collective-permute-start.48 = (bf16[2,96,768]{2,1,0:T(8,128)(2,1)S(1)}, bf16[2,96,768]{2,1,0:T(8,128)(2,1)S(1)}, u32[]{:S(2)}, u32[]{:S(2)}) collective-permute-start(bf16[2,96,768]{2,1,0:T(8,128)(2,1)S(1)} %get-tuple-element.139), channel_id=1, source_target_pairs={{0,3},{1,2},{2,1},{3,0},{4,7},{5,6},{6,5},{7,4},{8,11},{9,10},{10,... | collective-permute-start | bytes 884744 | tf_op jit(solution)/shard_map/ppermute | solution.py:151
  231.9 15.2 %collective-permute-start.44 = (bf16[2,96,768]{2,1,0:T(8,128)(2,1)}, bf16[2,96,768]{2,1,0:T(8,128)(2,1)S(1)}, u32[]{:S(2)}, u32[]{:S(2)}) collective-permute-start(bf16[2,96,768]{2,1,0:T(8,128)(2,1)} %get-tuple-element.135), channel_id=1, source_target_pairs={{0,8},{4,12},{8,0},{12,4},{16,24},{20,28},{24,16},{28,20},{1,9},{5... | collective-permute-start | bytes 884744 | tf_op jit(solution)/shard_map/ppermute | solution.py:24
  233.2 13.9 %collective-permute-start.45 = (bf16[2,96,768]{2,1,0:T(8,128)(2,1)S(1)}, bf16[2,96,768]{2,1,0:T(8,128)(2,1)S(1)}, u32[]{:S(2)}, u32[]{:S(2)}) collective-permute-start(bf16[2,96,768]{2,1,0:T(8,128)(2,1)S(1)} %get-tuple-element.136), channel_id=1, source_target_pairs={{0,16},{4,20},{8,24},{12,28},{16,0},{20,4},{24,8},{28,12},{1,17},{... | collective-permute-start | bytes 884744 | tf_op jit(solution)/shard_map/ppermute | solution.py:24
  236.2 24.1 %all-to-all-start.6 = ((bf16[8,4,3072]{2,1,0:T(4,128)(2,1)}), bf16[8,4,3072]{2,1,0:T(4,128)(2,1)S(1)}, u32[]{:S(2)}, u32[]{:S(2)}) async-start(bf16[8,4,3072]{2,1,0:T(4,128)(2,1)} %broadcast_in_dim.14), calls=%async_computation.6 | async-start | bytes 393216 | tf_op jit(solution)/shard_map/all_to_all | solution.py:897
  249.6 25.7 %collective-permute-start.49 = (bf16[96,768]{1,0:T(8,128)(2,1)S(1)}, bf16[96,768]{1,0:T(8,128)(2,1)S(1)}, u32[]{:S(2)}, u32[]{:S(2)}) collective-permute-start(bf16[96,768]{1,0:T(8,128)(2,1)S(1)} %get-tuple-element.141), channel_id=1, source_target_pairs={{0,1},{1,0},{2,3},{3,2},{4,5},{5,4},{6,7},{7,6},{8,9},{9,8},{10,11... | collective-permute-start | bytes 442376 | tf_op jit(solution)/shard_map/ppermute | solution.py:151
  255.2 20.2 %collective-permute-start.50 = (bf16[96,768]{1,0:T(8,128)(2,1)S(1)}, bf16[96,768]{1,0:T(8,128)(2,1)S(1)}, u32[]{:S(2)}, u32[]{:S(2)}) collective-permute-start(bf16[96,768]{1,0:T(8,128)(2,1)S(1)} %get-tuple-element.142), channel_id=1, source_target_pairs={{0,2},{1,3},{2,0},{3,1},{4,6},{5,7},{6,4},{7,5},{8,10},{9,11},{10,... | collective-permute-start | bytes 442376 | tf_op jit(solution)/shard_map/ppermute | solution.py:151
  257.2 18.2 %collective-permute-start.51 = (bf16[96,768]{1,0:T(8,128)(2,1)S(1)}, bf16[96,768]{1,0:T(8,128)(2,1)S(1)}, u32[]{:S(2)}, u32[]{:S(2)}) collective-permute-start(bf16[96,768]{1,0:T(8,128)(2,1)S(1)} %get-tuple-element.143), channel_id=1, source_target_pairs={{0,3},{1,2},{2,1},{3,0},{4,7},{5,6},{6,5},{7,4},{8,11},{9,10},{10,... | collective-permute-start | bytes 442376 | tf_op jit(solution)/shard_map/ppermute | solution.py:151
  262.7 11.9 %all-to-all-start.7 = ((f32[32,4,96]{2,1,0:T(4,128)}), f32[32,4,96]{2,1,0:T(4,128)S(1)}, u32[]{:S(2)}, u32[]{:S(2)}) async-start(f32[32,4,96]{2,1,0:T(4,128)} %get-tuple-element.120), calls=%async_computation.7 | async-start | bytes 131072 | tf_op jit(solution)/shard_map/all_to_all | solution.py:909
  (68 other events, 454.3 us)

commit v2 on v1

--- a/solution.py
+++ b/solution.py
@@ -603,7 +603,9 @@
 
 def final2_kernel(spec, me_ref, *refs):
     width, chunk, wide, n_seq = spec
-    up_ref, down_ref = refs[n_seq:]
+    result_in, packed_ref, up_ref, down_ref, result_ref, tokens_ref = refs[n_seq:]
+    result_ref[...] = result_in[...]
+    tokens_ref[...] = packed_ref[:, : tokens_ref.shape[1]]
     rows = up_ref.shape[0]
     for index in range(2):
         value = refs[0][index].astype(F32)
@@ -682,9 +684,7 @@
         return lax.all_to_all(values, "seq", 0, 0, tiled=True)
 
     def to_tokens(values):
-        values = values.reshape(n_seq, tok, width)
-        values = lax.all_to_all(values, "seq", 0, 0, tiled=True)
-        return values.reshape(micro, lats, tok, width)
+        return lax.all_to_all(values.reshape(n_seq, tok, width), "seq", 0, 0, tiled=True)
 
     shaped = jax.ShapeDtypeStruct
     dma = pltpu.SemaphoreType.DMA
@@ -881,7 +881,7 @@
             dma((n1,)),
         ],
         "input_back",
-        [result] + list(last2) if layout.direct else (),
+        list(last2) if layout.direct else (),
         4 * 10**9,
     )
 
@@ -889,13 +889,13 @@
         first1 = scatter_first(kept1, others1, [x_low2, y_high2])
         low1, high1 = swap(first1[0], "dp", 2), swap(first1[1], "dp", 1)
         x_high1, y_low1 = swap(first1[2], "dp", 1), swap(first1[3], "dp", 2)
-        (packed,) = after([packed], [x_low2, y_high2])
+        (packed,) = after([packed], list(first1) + [result])
     packed = lax.all_to_all(packed, "seq", 0, 0, tiled=True)
-    token_grad = packed[:, :tok].reshape(micro, lats, tok, width)
+    token_grad = packed[:, :tok]
     small = packed[:, tok : tok + 4].reshape(n_seq, 4 * width)
     small = jnp.broadcast_to(small[None], (n_dp,) + small.shape)
     small = lax.all_to_all(small, "dp", 0, 0, tiled=True).reshape(n_dp * held, 4 * width)
-    grad_mod, row_sums, dcond = call(
+    grad_mod, row_sums, dcond_part = call(
         mod_grad_kernel, n_seq, here, [small, cond_rows, modulator], [],
         [
             shaped(modulator.shape, F32),
@@ -906,7 +906,7 @@
     )
     row_sums = row_sums.reshape(4 * width)
     grad_mod_offset = row_sums[: modulator.shape[1]]
-    dcond = lax.all_to_all(dcond, ("dp", "seq"), 0, 0, tiled=True)
+    dcond = lax.all_to_all(dcond_part, ("dp", "seq"), 0, 0, tiled=True)
     if layout.direct:
         blocks2 = call(
             collect2_kernel, spec_seq, here,
@@ -927,9 +927,10 @@
         over_z1 = swap_seq(blocks1[1:])
 
     if layout.direct:
-        up_out, down_out = call(
-            final2_kernel, spec_seq, here, [blocks2[0]] + over_z2, [],
-            [shaped((rows, width), F32), shaped((wide * rows, chunk), F32)], [], [], "final2",
+        up_out, down_out, result, token_grad = call(
+            final2_kernel, spec_seq, here, [blocks2[0]] + over_z2 + [result, packed], [],
+            [shaped((rows, width), F32), shaped((wide * rows, chunk), F32)]
+            + [shaped((held, tok, width), BF)] * 2, [], [], "final2", [dcond_part],
         )
         qkv_out, proj_out = call(
             final1_kernel, spec_seq, here, [blocks1[0]] + over_z1, [],
@@ -956,8 +957,8 @@
     bias_grads = (querybias, valuebias, projbias, expandbias, contractbias)
     sums = [row_sums[first : first + b.shape[0]] for first, b in zip(at, bias_grads)]
     return (
-        result,
-        token_grad,
+        result.reshape(micro, lats, tok, width),
+        token_grad.reshape(micro, lats, tok, width),
         dconds,
         grad_mod,
         grad_mod_offset,

time: 280 us -> 273 us (0.975)
  waiting for transfers between devices: 85.8 us -> 75.4 us
  local copies, waits for them, and re-layouts: 30.8 us -> 33.6 us
    all_to_all x2, waiting for transfers between devices: 8.44 us -> 3.77 us  [the longest x1 3.76 us: local(): dcond = lax.all_to_all(dcond_part, ('dp', 'seq'), 0, 0, tiled=True)]
    ppermute x43, waiting for transfers between devices: 54.6 us -> 50.9 us  [swap(): return lax.ppermute(values, axis, [(i, i ^ 1 << bit) for i in range(count)])]
    unnamed x120 -> x141, local copies, waits for them, and re-layouts: 19 us -> 22.6 us
  transfers between devices with their start and end apart: 60 -> 60, of which waited for: 23 -> 21; matrix products, arithmetic and copies ran while one was open for 5% -> 5% of each run, Pallas kernels for 18% -> 20%
where the time goes in v2:
time: 273 us; the launch traced here: 271 us
  starting transfers between devices  80.1 us (29%)
  Pallas kernels  76.4 us (28%)
  waiting for transfers between devices  75.4 us (28%)
  local copies, waits for them, and re-layouts  33.6 us (12%)
  other arithmetic  3.88 us (1%)
    pallas_call x20, Pallas kernels, call(): pl.pallas_call(run, grid=(1,), out_shape=far_outs + outs, in_specs=[pl.Bl...  76.4 us
    ppermute x43, waiting for transfers between devices, swap(): return lax.ppermute(values, axis, [(i, i ^ 1 << bit) for i in range(count)])  50.9 us
    ppermute x43, starting transfers between devices, swap(): return lax.ppermute(values, axis, [(i, i ^ 1 << bit) for i in range(count)])  26 us
    unnamed x141, local copies, waits for them, and re-layouts  22.6 us
    ppermute x9, starting transfers between devices, swap_seq(): lax.ppermute(value, 'seq', [(i, i ^ mask + 1) for i in range(count)])  21.6 us
    all_to_all x2, waiting for transfers between devices, to_latents(): return lax.all_to_all(values, 'seq', 0, 0, tiled=True)  7.78 us
    all_to_all x2, starting transfers between devices, to_latents(): return lax.all_to_all(values, 'seq', 0, 0, tiled=True)  7.24 us
    ppermute x9, waiting for transfers between devices, swap_seq(): lax.ppermute(value, 'seq', [(i, i ^ mask + 1) for i in range(count)])  7.21 us
  transfers between devices with their start and end apart: 60, of which 21 were waited for; matrix products, arithmetic and copies ran while one was open for 5% of the time, Pallas kernels for 20%

profile of v2, /device:TPU:0, one launch (start us, length us, event | category | flops | bytes accessed | tf_op | source)
XLA Modules:
  0.0 270.9 jit_solution(16158828465982965135)
XLA Ops:
  0.7 3.5 %concatenate.14 = bf16[1536]{0:T(1024)(128)(2,1)S(1)} concatenate(bf16[192]{0:T(256)(128)(2,1)} %param.19, bf16[192]{0:T(256)(128)(2,1)} %param.20, bf16[192]{0:T(256)(128)(2,1)} %param.22, bf16[192]{0:T(256)(128)(2,1)} %param.26, bf16[768]{0:T(1024)(128)(2,1)} %param.24), dimensions={0} | concatenate | bytes 6144 | tf_op jit(solution)/shard_map/concatenate | solution.py:693
  5.2 5.1 %collective-permute-start.3 = (bf16[112,768]{1,0:T(8,128)(2,1)S(1)}, bf16[112,768]{1,0:T(8,128)(2,1)S(1)}, u32[]{:S(2)}, u32[]{:S(2)}) collective-permute-start(bf16[112,768]{1,0:T(8,128)(2,1)S(1)} %fusion.1.refs_1_), channel_id=1, source_target_pairs={{0,3},{1,2},{2,1},{3,0},{4,7},{5,6},{6,5},{7,4},{8,11},{9,10},{10,... | collective-permute-start | bytes 516104 | tf_op jit(solution)/shard_map/ppermute | solution.py:151
  15.2 1.3 copy.43
  16.5 4.0 %all-to-all-start = ((bf16[4,8,96]{2,0,1:T(4,128)(2,1)}), bf16[4,8,96]{2,0,1:T(4,128)(2,1)S(1)}, u32[]{:S(2)}, u32[]{:S(2)}) async-start(bf16[4,8,96]{2,0,1:T(4,128)(2,1)} %copy.43), calls=%async_computation | async-start | bytes 16384 | tf_op jit(solution)/shard_map/all_to_all | solution.py:708
  21.3 3.6 %collective-permute-done.2.refs_2_.refs_3_ = bf16[112,768]{1,0:T(8,128)(2,1)S(1)} collective-permute-done((bf16[112,768]{1,0:T(8,128)(2,1)S(1)}, bf16[112,768]{1,0:T(8,128)(2,1)S(1)}, u32[]{:S(2)}, u32[]{:S(2)}) %collective-permute-start.2) | collective-permute-done | bytes 172064 | tf_op jit(solution)/shard_map/ppermute | solution.py:151
  27.1 3.7 %all-to-all-start.1 = ((f32[8,4,1152]{2,1,0:T(4,128)}), f32[8,4,1152]{2,1,0:T(4,128)S(1)}, u32[]{:S(2)}, u32[]{:S(2)}) async-start(f32[8,4,1152]{2,1,0:T(4,128)} %reshape.100), calls=%async_computation.1 | async-start | bytes 294912 | tf_op jit(solution)/shard_map/all_to_all | solution.py:711
  30.8 5.7 %all-to-all-done.1.refs_2_.refs_5_ = f32[8,4,1152]{2,1,0:T(4,128)S(1)} async-done(((f32[8,4,1152]{2,1,0:T(4,128)}), f32[8,4,1152]{2,1,0:T(4,128)S(1)}, u32[]{:S(2)}, u32[]{:S(2)}) %all-to-all-start.1) | async-done | bytes 147488 | tf_op jit(solution)/shard_map/all_to_all | solution.py:711
  41.7 3.1 %collective-permute-start.5 = (bf16[2,2,96,768]{3,2,1,0:T(8,128)(2,1)S(1)}, bf16[2,2,96,768]{3,2,1,0:T(8,128)(2,1)S(1)}, u32[]{:S(2)}, u32[]{:S(2)}) collective-permute-start(bf16[2,2,96,768]{3,2,1,0:T(8,128)(2,1)S(1)} %pad_maximum_fusion), channel_id=1, source_target_pairs={{0,1},{1,0},{2,3},{3,2},{4,5},{5,4},{6,7},{7,6},{8,9},{9,8},{10,11... | collective-permute-start | bytes 1769480 | tf_op jit(solution)/shard_map/ppermute | solution.py:24
  44.8 10.9 %collective-permute-done.9.refs_2_.refs_8_.refs_20_.refs_15_ = bf16[4,96,768]{2,1,0:T(8,128)(2,1)S(1)} collective-permute-done((bf16[4,96,768]{2,1,0:T(8,128)(2,1)}, bf16[4,96,768]{2,1,0:T(8,128)(2,1)S(1)}, u32[]{:S(2)}, u32[]{:S(2)}) %collective-permute-start.9) | collective-permute-done | bytes 589856 | tf_op jit(solution)/shard_map/ppermute | solution.py:24
  55.8 1.6 collective-permute-done.5.refs_3_
  59.1 1.5 collective-permute-start.11
  60.6 1.4 collective-permute-start.13
  63.9 3.6 %all-to-all-start.2 = ((bf16[4,80,768]{2,1,0:T(8,128)(2,1)}), bf16[4,80,768]{2,1,0:T(8,128)(2,1)S(1)}, u32[]{:S(2)}, u32[]{:S(2)}) async-start(bf16[4,80,768]{2,1,0:T(8,128)(2,1)} %copy-done.10), calls=%async_computation.2 | async-start | bytes 983040 | tf_op jit(solution)/shard_map/all_to_all | solution.py:684
  68.0 1.4 spread2.1.refs_6_
  71.8 7.8 %all-to-all-done.2.refs_1_.refs_2_ = bf16[4,80,768]{2,1,0:T(8,128)(2,1)S(1)} async-done(((bf16[4,80,768]{2,1,0:T(8,128)(2,1)}), bf16[4,80,768]{2,1,0:T(8,128)(2,1)S(1)}, u32[]{:S(2)}, u32[]{:S(2)}) %all-to-all-start.2) | async-done | bytes 491552 | tf_op jit(solution)/shard_map/all_to_all | solution.py:684
  81.4 3.6 %all-to-all-start.3 = ((bf16[4,64,768]{2,1,0:T(8,128)(2,1)}), bf16[4,64,768]{2,1,0:T(8,128)(2,1)S(1)}, u32[]{:S(2)}, u32[]{:S(2)}) async-start(bf16[4,64,768]{2,1,0:T(8,128)(2,1)} %bitcast.10), calls=%async_computation.3 | async-start | bytes 786432 | tf_op jit(solution)/shard_map/all_to_all | solution.py:684
  87.9 7.9 %attention.1 = (bf16[256,768]{1,0:T(8,128)(2,1)S(1)}, bf16[3,256,768]{2,1,0:T(8,128)(2,1)}, bf16[256,768]{1,0:T(8,128)(2,1)S(1)}, f32[256,768]{1,0:T(8,128)}, f3...) custom-call(s32[1]{0:T(128)} %bitcast.1.refs_0_, bf16[4,80,768]{2,1,0:T(8,128)(2,1)} %copy-done.7, ...), custom_call_target="tpu_custom_call" | custom-call | tf_op jit(solution)/shard_map/attention/pallas_call | solution.py:639
  96.6 1.6 cut.3
  100.1 13.6 %collective-permute-done.20.refs_12_ = bf16[4,96,768]{2,1,0:T(8,128)(2,1)S(1)} collective-permute-done((bf16[4,96,768]{2,1,0:T(8,128)(2,1)S(1)}, bf16[4,96,768]{2,1,0:T(8,128)(2,1)S(1)}, u32[]{:S(2)}, u32[]{:S(2)}) %collective-permute-start.20) | collective-permute-done | bytes 589856 | tf_op jit(solution)/shard_map/ppermute | solution.py:24
  117.4 17.2 %mlp.1 = (bf16[4,8,96,768]{3,2,1,0:T(8,128)(2,1)}, bf16[8,96,768]{2,1,0:T(8,128)(2,1)}, bf16[8,96,768]{2,1,0:T(8,128)(2,1)}, bf16[8,96,768]{2,1,0:T(8,128)(2,1)}...) custom-call(s32[1]{0:T(128)} %bitcast.1.refs_0_, ...), custom_call_target="tpu_custom_call" | custom-call | tf_op jit(solution)/shard_map/mlp/pallas_call | solution.py:639
  135.7 7.7 %middle_back.1 = (f32[256,768]{1,0:T(8,128)}, bf16[256,768]{1,0:T(8,128)(2,1)S(1)}, bf16[256,768]{1,0:T(8,128)(2,1)S(1)}, f32[1,2304]{1,0:T(1,128)S(1)}, f32[1,768]{1,0:T(1,128)S(1)}) custom-call(s32[1]{0:T(128)} %bitcast.1.refs_0_, f32[256,768]{1,0:T(8,128)} %get-tuple-element.88.refs_3_.refs_1_, f32[1,4608]{1,0:T(1,128)S(1)} %get-tuple-element.89.refs_2_, ...), custom_call_target="tpu_custom_call" | custom-call | tf_op jit(solution)/shard_map/middle_back/pallas_call | solution.py:639
  145.2 3.5 %first_sums.2 = (bf16[4,96,768]{2,1,0:T(8,128)(2,1)S(1)}, bf16[4,96,768]{2,1,0:T(8,128)(2,1)S(1)}, bf16[4,96,768]{2,1,0:T(8,128)(2,1)}, bf16[4,96,768]{2,1,0:T(8,128)(2,1)}) custom-call(s32[1]{0:T(128)} %constant.21.clone.1.refs_0_, bf16[4,8,96,768]{3,2,1,0:T(8,128)(2,1)} %get-tuple-element.94.refs_1_.refs_3_.refs_5_.refs_7_.refs_4_, ...), custom_call_target="tpu_custom_call" | custom-call | tf_op jit(solution)/shard_map/first_sums/pallas_call | solution.py:639
  148.8 1.5 collective-permute-start.29
  152.8 12.6 %attention_back.1 = (bf16[4,4,96,768]{3,2,1,0:T(8,128)(2,1)}, bf16[4,96,768]{2,1,0:T(8,128)(2,1)}, bf16[4,96,768]{2,1,0:T(8,128)(2,1)}, bf16[4,96,768]{2,1,0:T(8...) custom-call(s32[1]{0:T(128)} %bitcast.1.refs_0_, ...), custom_call_target="tpu_custom_call" | custom-call | tf_op jit(solution)/shard_map/attention_back/pallas_call | solution.py:639
  166.5 11.5 %collective-permute-done.31.refs_8_.refs_4_ = bf16[4,96,768]{2,1,0:T(8,128)(2,1)S(1)} collective-permute-done((bf16[4,96,768]{2,1,0:T(8,128)(2,1)}, bf16[4,96,768]{2,1,0:T(8,128)(2,1)S(1)}, u32[]{:S(2)}, u32[]{:S(2)}) %collective-permute-start.31) | collective-permute-done | bytes 589856 | tf_op jit(solution)/shard_map/ppermute | solution.py:24
  179.0 2.8 %last_sums.2 = (bf16[4,96,768]{2,1,0:T(8,128)(2,1)}, bf16[4,96,768]{2,1,0:T(8,128)(2,1)S(1)}) custom-call(s32[1]{0:T(128)} %constant.21.clone.1.refs_0_, bf16[4,8,96,768]{3,2,1,0:T(8,128)(2,1)} %get-tuple-element.94.refs_1_.refs_3_.refs_5_.refs_7_.refs_4_, bf16[8,96,768]{2,1,0:T(8,128)(2,1)} %copy-done.50, ...), custom_call_target="tpu_custom_call" | custom-call | tf_op jit(solution)/shard_map/last_sums/pallas_call | solution.py:639
  183.1 4.8 %all-to-all-start.4 = ((bf16[4,64,768]{2,1,0:T(8,128)(2,1)}), bf16[4,64,768]{2,1,0:T(8,128)(2,1)}, u32[]{:S(2)}, u32[]{:S(2)}) async-start(bf16[4,64,768]{2,1,0:T(8,128)(2,1)} %bitcast.12), calls=%async_computation.4 | async-start | bytes 786432 | tf_op jit(solution)/shard_map/all_to_all | solution.py:687
  188.9 5.4 %input_back.1.refs_0_ = bf16[4,80,768]{2,1,0:T(8,128)(2,1)} custom-call(s32[1]{0:T(128)} %bitcast.1.refs_0_, bf16[256,768]{1,0:T(8,128)(2,1)S(1)} %copy-done.49, f32[1,4608]{1,0:T(1,128)S(1)} %get-tuple-element.89.refs_2_, f32[256,768]{1,0:T(8,128)} %get-tuple-element.120.refs_3_, bf16[3,256,768]{2,1,0:T(8,128)(2,1)} %get-tuple-element.111.refs_7_.refs_4_, ...), custom_call_target="tpu_custom_call" | custom-call | flops 4000000000 | tf_op jit(solution)/shard_map/input_back/pallas_call | solution.py:639
  194.3 3.2 %collective-permute-done.33.refs_3_.refs_9_ = bf16[4,96,768]{2,1,0:T(8,128)(2,1)S(1)} collective-permute-done((bf16[4,96,768]{2,1,0:T(8,128)(2,1)}, bf16[4,96,768]{2,1,0:T(8,128)(2,1)S(1)}, u32[]{:S(2)}, u32[]{:S(2)}) %collective-permute-start.33) | collective-permute-done | bytes 589856 | tf_op jit(solution)/shard_map/ppermute | solution.py:24
  198.4 1.7 first_sums.3
  202.9 5.0 %all-to-all-start.5 = ((bf16[4,80,768]{2,1,0:T(8,128)(2,1)}), bf16[4,80,768]{2,1,0:T(8,128)(2,1)}, u32[]{:S(2)}, u32[]{:S(2)}) async-start(bf16[4,80,768]{2,1,0:T(8,128)(2,1)} %after.5), calls=%async_computation.5 | async-start | bytes 983040 | tf_op jit(solution)/shard_map/all_to_all | solution.py:893
  210.6 1.5 collective-permute-start.46
  212.1 3.2 %collect2.1 = (bf16[2,96,768]{2,1,0:T(8,128)(2,1)S(1)}, bf16[2,96,768]{2,1,0:T(8,128)(2,1)S(1)}, bf16[2,96,768]{2,1,0:T(8,128)(2,1)S(1)}, bf16[2,96,768]{2,1,0:T(8,128)(2,1)S(1)}) custom-call(s32[1]{0:T(128)} %bitcast.refs_0_, bf16[4,8,96,768]{3,2,1,0:T(8,128)(2,1)} %get-tuple-element.94.refs_1_.refs_3_.refs_5_.refs_7_.refs_4_, ...), custom_call_target="tpu_custom_call" | custom-call | tf_op jit(solution)/shard_map/collect2/pallas_call | solution.py:639
  215.2 2.6 collective-permute-done.43.refs_3_
  217.8 1.9 collective-permute-start.35
  219.8 2.4 collective-permute-start.36
  222.1 1.8 collective-permute-done.45.refs_8_.refs_4_
  223.9 3.8 %collective-permute-start.37 = (bf16[2,96,768]{2,1,0:T(8,128)(2,1)S(1)}, bf16[2,96,768]{2,1,0:T(8,128)(2,1)S(1)}, u32[]{:S(2)}, u32[]{:S(2)}) collective-permute-start(bf16[2,96,768]{2,1,0:T(8,128)(2,1)S(1)} %get-tuple-element.117), channel_id=1, source_target_pairs={{0,3},{1,2},{2,1},{3,0},{4,7},{5,6},{6,5},{7,4},{8,11},{9,10},{10,... | collective-permute-start | bytes 884744 | tf_op jit(solution)/shard_map/ppermute | solution.py:151
  228.5 2.1 last_sums.3
  232.2 1.5 collective-permute-start.48
  235.2 4.2 %all-to-all-start.6 = ((bf16[8,4,3072]{2,1,0:T(4,128)(2,1)}), bf16[8,4,3072]{2,1,0:T(4,128)(2,1)}, u32[]{:S(2)}, u32[]{:S(2)}) async-start(bf16[8,4,3072]{2,1,0:T(4,128)(2,1)} %broadcast_in_dim.14), calls=%async_computation.6 | async-start | bytes 393216 | tf_op jit(solution)/shard_map/all_to_all | solution.py:897
  239.4 3.6 %collective-permute-done.36.refs_3_.refs_8_ = bf16[2,96,768]{2,1,0:T(8,128)(2,1)S(1)} collective-permute-done((bf16[2,96,768]{2,1,0:T(8,128)(2,1)S(1)}, bf16[2,96,768]{2,1,0:T(8,128)(2,1)S(1)}, u32[]{:S(2)}, u32[]{:S(2)}) %collective-permute-start.36) | collective-permute-done | bytes 294944 | tf_op jit(solution)/shard_map/ppermute | solution.py:151
  244.8 2.4 collect1.1
  247.2 5.3 %collective-permute-start.49 = (bf16[96,768]{1,0:T(8,128)(2,1)S(1)}, bf16[96,768]{1,0:T(8,128)(2,1)S(1)}, u32[]{:S(2)}, u32[]{:S(2)}) collective-permute-start(bf16[96,768]{1,0:T(8,128)(2,1)S(1)} %get-tuple-element.145), channel_id=1, source_target_pairs={{0,1},{1,0},{2,3},{3,2},{4,5},{5,4},{6,7},{7,6},{8,9},{9,8},{10,11... | collective-permute-start | bytes 442376 | tf_op jit(solution)/shard_map/ppermute | solution.py:151
  253.5 1.5 collective-permute-start.51
  258.2 3.6 %all-to-all-start.7 = ((f32[32,4,96]{2,1,0:T(4,128)}), f32[32,4,96]{2,1,0:T(4,128)S(1)}, u32[]{:S(2)}, u32[]{:S(2)}) async-start(f32[32,4,96]{2,1,0:T(4,128)} %get-tuple-element.136.refs_7_), calls=%async_computation.7 | async-start | bytes 131072 | tf_op jit(solution)/shard_map/all_to_all | solution.py:909
  261.9 2.2 final2.1
  265.6 3.8 %all-to-all-done.7.refs_5_ = f32[32,4,96]{2,1,0:T(4,128)S(1)} async-done(((f32[32,4,96]{2,1,0:T(4,128)}), f32[32,4,96]{2,1,0:T(4,128)S(1)}, u32[]{:S(2)}, u32[]{:S(2)}) %all-to-all-start.7) | async-done | bytes 49184 | tf_op jit(solution)/shard_map/all_to_all | solution.py:909
  (258 shorter events, 60.6 us)
Async XLA Ops:
  5.2 16.1 %collective-permute-start.3 = (bf16[112,768]{1,0:T(8,128)(2,1)S(1)}, bf16[112,768]{1,0:T(8,128)(2,1)S(1)}, u32[]{:S(2)}, u32[]{:S(2)}) collective-permute-start(bf16[112,768]{1,0:T(8,128)(2,1)S(1)} %fusion.1.refs_1_), channel_id=1, source_target_pairs={{0,3},{1,2},{2,1},{3,0},{4,7},{5,6},{6,5},{7,4},{8,11},{9,10},{10,... | collective-permute-start | bytes 516104 | tf_op jit(solution)/shard_map/ppermute | solution.py:151
  10.3 14.6 %collective-permute-start.2 = (bf16[112,768]{1,0:T(8,128)(2,1)S(1)}, bf16[112,768]{1,0:T(8,128)(2,1)S(1)}, u32[]{:S(2)}, u32[]{:S(2)}) collective-permute-start(bf16[112,768]{1,0:T(8,128)(2,1)S(1)} %fusion.1.refs_1_), channel_id=1, source_target_pairs={{0,2},{1,3},{2,0},{3,1},{4,6},{5,7},{6,4},{7,5},{8,10},{9,11},{10,... | collective-permute-start | bytes 516104 | tf_op jit(solution)/shard_map/ppermute | solution.py:151
  10.3 14.6 %collective-permute-start.1 = (bf16[112,768]{1,0:T(8,128)(2,1)S(1)}, bf16[112,768]{1,0:T(8,128)(2,1)S(1)}, u32[]{:S(2)}, u32[]{:S(2)}) collective-permute-start(bf16[112,768]{1,0:T(8,128)(2,1)S(1)} %fusion.1.refs_1_), channel_id=1, source_target_pairs={{0,1},{1,0},{2,3},{3,2},{4,5},{5,4},{6,7},{7,6},{8,9},{9,8},{10,11... | collective-permute-start | bytes 516104 | tf_op jit(solution)/shard_map/ppermute | solution.py:151
  16.5 9.7 %all-to-all-start = ((bf16[4,8,96]{2,0,1:T(4,128)(2,1)}), bf16[4,8,96]{2,0,1:T(4,128)(2,1)S(1)}, u32[]{:S(2)}, u32[]{:S(2)}) async-start(bf16[4,8,96]{2,0,1:T(4,128)(2,1)} %copy.43), calls=%async_computation | async-start | bytes 16384 | tf_op jit(solution)/shard_map/all_to_all | solution.py:708
  26.2 15.4 %collective-permute-start.4 = (bf16[2,96,768]{2,1,0:T(8,128)(2,1)}, bf16[2,96,768]{2,1,0:T(8,128)(2,1)S(1)}, u32[]{:S(2)}, u32[]{:S(2)}) collective-permute-start(bf16[2,96,768]{2,1,0:T(8,128)(2,1)} %after.4.refs_1_), channel_id=1, source_target_pairs={{0,2},{1,3},{2,0},{3,1},{4,6},{5,7},{6,4},{7,5},{8,10},{9,11},{10,... | collective-permute-start | bytes 884744 | tf_op jit(solution)/shard_map/ppermute | solution.py:24
  40.5 15.2 %collective-permute-start.9 = (bf16[4,96,768]{2,1,0:T(8,128)(2,1)}, bf16[4,96,768]{2,1,0:T(8,128)(2,1)S(1)}, u32[]{:S(2)}, u32[]{:S(2)}) collective-permute-start(bf16[4,96,768]{2,1,0:T(8,128)(2,1)} %get-tuple-element.85.refs_4_.refs_16_.refs_11_), channel_id=1, source_target_pairs={{0,16},{4,20},{8,24},{12,28},{16,0},{20,4},{24,8},{28,12},{1,17},{... | collective-permute-start | bytes 1769480 | tf_op jit(solution)/shard_map/ppermute | solution.py:24
  41.0 14.8 %collective-permute-start.7 = (bf16[4,96,768]{2,1,0:T(8,128)(2,1)}, bf16[4,96,768]{2,1,0:T(8,128)(2,1)S(1)}, u32[]{:S(2)}, u32[]{:S(2)}) collective-permute-start(bf16[4,96,768]{2,1,0:T(8,128)(2,1)} %get-tuple-element.85.refs_4_.refs_16_.refs_11_), channel_id=1, source_target_pairs={{0,8},{4,12},{8,0},{12,4},{16,24},{20,28},{24,16},{28,20},{1,9},{5... | collective-permute-start | bytes 1769480 | tf_op jit(solution)/shard_map/ppermute | solution.py:24
  41.7 15.7 %collective-permute-start.5 = (bf16[2,2,96,768]{3,2,1,0:T(8,128)(2,1)S(1)}, bf16[2,2,96,768]{3,2,1,0:T(8,128)(2,1)S(1)}, u32[]{:S(2)}, u32[]{:S(2)}) collective-permute-start(bf16[2,2,96,768]{3,2,1,0:T(8,128)(2,1)S(1)} %pad_maximum_fusion), channel_id=1, source_target_pairs={{0,1},{1,0},{2,3},{3,2},{4,5},{5,4},{6,7},{7,6},{8,9},{9,8},{10,11... | collective-permute-start | bytes 1769480 | tf_op jit(solution)/shard_map/ppermute | solution.py:24
  63.9 15.7 %all-to-all-start.2 = ((bf16[4,80,768]{2,1,0:T(8,128)(2,1)}), bf16[4,80,768]{2,1,0:T(8,128)(2,1)S(1)}, u32[]{:S(2)}, u32[]{:S(2)}) async-start(bf16[4,80,768]{2,1,0:T(8,128)(2,1)} %copy-done.10), calls=%async_computation.2 | async-start | bytes 983040 | tf_op jit(solution)/shard_map/all_to_all | solution.py:684
  69.4 27.1 %collective-permute-start.18 = (bf16[8,96,768]{2,1,0:T(8,128)(2,1)}, bf16[8,96,768]{2,1,0:T(8,128)(2,1)}, u32[]{:S(2)}, u32[]{:S(2)}) collective-permute-start(bf16[8,96,768]{2,1,0:T(8,128)(2,1)} %spread2.1.refs_6_), channel_id=1, source_target_pairs={{0,16},{4,20},{8,24},{12,28},{16,0},{20,4},{24,8},{28,12},{1,17},{... | collective-permute-start | bytes 3538952 | tf_op jit(solution)/shard_map/ppermute | solution.py:24
  70.0 26.6 %collective-permute-start.16 = (bf16[8,96,768]{2,1,0:T(8,128)(2,1)}, bf16[8,96,768]{2,1,0:T(8,128)(2,1)}, u32[]{:S(2)}, u32[]{:S(2)}) collective-permute-start(bf16[8,96,768]{2,1,0:T(8,128)(2,1)} %spread2.1.refs_6_), channel_id=1, source_target_pairs={{0,8},{4,12},{8,0},{12,4},{16,24},{20,28},{24,16},{28,20},{1,9},{5... | collective-permute-start | bytes 3538952 | tf_op jit(solution)/shard_map/ppermute | solution.py:24
  71.3 13.8 %collective-permute-start.6 = (bf16[4,96,768]{2,1,0:T(8,128)(2,1)}, bf16[4,96,768]{2,1,0:T(8,128)(2,1)}, u32[]{:S(2)}, u32[]{:S(2)}) collective-permute-start(bf16[4,96,768]{2,1,0:T(8,128)(2,1)} %get-tuple-element.85.refs_4_.refs_16_.refs_11_), channel_id=1, source_target_pairs={{0,4},{4,0},{8,12},{12,8},{16,20},{20,16},{24,28},{28,24},{1,5},{5... | collective-permute-start | bytes 1769480 | tf_op jit(solution)/shard_map/ppermute | solution.py:24
  71.3 13.9 %collective-permute-start.10 = (bf16[4,96,768]{2,1,0:T(8,128)(2,1)S(1)}, bf16[4,96,768]{2,1,0:T(8,128)(2,1)}, u32[]{:S(2)}, u32[]{:S(2)}) collective-permute-start(bf16[4,96,768]{2,1,0:T(8,128)(2,1)S(1)} %collective-permute-done.9.refs_2_.refs_8_.refs_20_.refs_15_), channel_id=1, source_target_pairs={{0,4},{4,0},{8,12},{12,8},{16,20},{20,16},{24,28},{28,24},{1,5},{5... | collective-permute-start | bytes 1769480 | tf_op jit(solution)/shard_map/ppermute | solution.py:24
  71.8 13.9 %collective-permute-start.8 = (bf16[4,96,768]{2,1,0:T(8,128)(2,1)S(1)}, bf16[4,96,768]{2,1,0:T(8,128)(2,1)}, u32[]{:S(2)}, u32[]{:S(2)}) collective-permute-start(bf16[4,96,768]{2,1,0:T(8,128)(2,1)S(1)} %collective-permute-done.7.refs_1_.refs_6_.refs_18_.refs_13_), channel_id=1, source_target_pairs={{0,4},{4,0},{8,12},{12,8},{16,20},{20,16},{24,28},{28,24},{1,5},{5... | collective-permute-start | bytes 1769480 | tf_op jit(solution)/shard_map/ppermute | solution.py:24
  81.4 15.1 %all-to-all-start.3 = ((bf16[4,64,768]{2,1,0:T(8,128)(2,1)}), bf16[4,64,768]{2,1,0:T(8,128)(2,1)S(1)}, u32[]{:S(2)}, u32[]{:S(2)}) async-start(bf16[4,64,768]{2,1,0:T(8,128)(2,1)} %bitcast.10), calls=%async_computation.3 | async-start | bytes 786432 | tf_op jit(solution)/shard_map/all_to_all | solution.py:684
  85.7 28.9 %collective-permute-start.15 = (bf16[8,96,768]{2,1,0:T(8,128)(2,1)}, bf16[8,96,768]{2,1,0:T(8,128)(2,1)}, u32[]{:S(2)}, u32[]{:S(2)}) collective-permute-start(bf16[8,96,768]{2,1,0:T(8,128)(2,1)} %spread2.1.refs_6_), channel_id=1, source_target_pairs={{0,4},{4,0},{8,12},{12,8},{16,20},{20,16},{24,28},{28,24},{1,5},{5... | collective-permute-start | bytes 3538952 | tf_op jit(solution)/shard_map/ppermute | solution.py:24
  98.2 15.4 %collective-permute-start.20 = (bf16[4,96,768]{2,1,0:T(8,128)(2,1)S(1)}, bf16[4,96,768]{2,1,0:T(8,128)(2,1)S(1)}, u32[]{:S(2)}, u32[]{:S(2)}) collective-permute-start(bf16[4,96,768]{2,1,0:T(8,128)(2,1)S(1)} %get-tuple-element.92), channel_id=1, source_target_pairs={{0,16},{4,20},{8,24},{12,28},{16,0},{20,4},{24,8},{28,12},{1,17},{... | collective-permute-start | bytes 1769480 | tf_op jit(solution)/shard_map/ppermute | solution.py:24
  98.8 15.8 %collective-permute-start.19 = (bf16[8,96,768]{2,1,0:T(8,128)(2,1)}, bf16[8,96,768]{2,1,0:T(8,128)(2,1)S(1)}, u32[]{:S(2)}, u32[]{:S(2)}) collective-permute-start(bf16[8,96,768]{2,1,0:T(8,128)(2,1)} %collective-permute-done.18.refs_2_.refs_10_), channel_id=1, source_target_pairs={{0,4},{4,0},{8,12},{12,8},{16,20},{20,16},{24,28},{28,24},{1,5},{5... | collective-permute-start | bytes 3538952 | tf_op jit(solution)/shard_map/ppermute | solution.py:24
  98.8 15.8 %collective-permute-start.17 = (bf16[8,96,768]{2,1,0:T(8,128)(2,1)}, bf16[8,96,768]{2,1,0:T(8,128)(2,1)S(1)}, u32[]{:S(2)}, u32[]{:S(2)}) collective-permute-start(bf16[8,96,768]{2,1,0:T(8,128)(2,1)} %collective-permute-done.16.refs_1_.refs_8_), channel_id=1, source_target_pairs={{0,4},{4,0},{8,12},{12,8},{16,20},{20,16},{24,28},{28,24},{1,5},{5... | collective-permute-start | bytes 3538952 | tf_op jit(solution)/shard_map/ppermute | solution.py:24
  99.3 15.2 %collective-permute-start.22 = (bf16[4,96,768]{2,1,0:T(8,128)(2,1)S(1)}, bf16[4,96,768]{2,1,0:T(8,128)(2,1)S(1)}, u32[]{:S(2)}, u32[]{:S(2)}) collective-permute-start(bf16[4,96,768]{2,1,0:T(8,128)(2,1)S(1)} %get-tuple-element.93), channel_id=1, source_target_pairs={{0,8},{4,12},{8,0},{12,4},{16,24},{20,28},{24,16},{28,20},{1,9},{5... | collective-permute-start | bytes 1769480 | tf_op jit(solution)/shard_map/ppermute | solution.py:24
  148.8 16.7 %collective-permute-start.29 = (bf16[4,96,768]{2,1,0:T(8,128)(2,1)S(1)}, bf16[4,96,768]{2,1,0:T(8,128)(2,1)S(1)}, u32[]{:S(2)}, u32[]{:S(2)}) collective-permute-start(bf16[4,96,768]{2,1,0:T(8,128)(2,1)S(1)} %get-tuple-element.103.refs_6_), channel_id=1, source_target_pairs={{0,16},{4,20},{8,24},{12,28},{16,0},{20,4},{24,8},{28,12},{1,17},{... | collective-permute-start | bytes 1769480 | tf_op jit(solution)/shard_map/ppermute | solution.py:24
  150.2 16.2 %collective-permute-start.30 = (bf16[4,96,768]{2,1,0:T(8,128)(2,1)S(1)}, bf16[4,96,768]{2,1,0:T(8,128)(2,1)S(1)}, u32[]{:S(2)}, u32[]{:S(2)}) collective-permute-start(bf16[4,96,768]{2,1,0:T(8,128)(2,1)S(1)} %get-tuple-element.104.refs_7_), channel_id=1, source_target_pairs={{0,8},{4,12},{8,0},{12,4},{16,24},{20,28},{24,16},{28,20},{1,9},{5... | collective-permute-start | bytes 1769480 | tf_op jit(solution)/shard_map/ppermute | solution.py:24
  151.0 27.0 %collective-permute-start.31 = (bf16[4,96,768]{2,1,0:T(8,128)(2,1)}, bf16[4,96,768]{2,1,0:T(8,128)(2,1)S(1)}, u32[]{:S(2)}, u32[]{:S(2)}) collective-permute-start(bf16[4,96,768]{2,1,0:T(8,128)(2,1)} %get-tuple-element.109.refs_8_), channel_id=1, source_target_pairs={{0,8},{4,12},{8,0},{12,4},{16,24},{20,28},{24,16},{28,20},{1,9},{5... | collective-permute-start | bytes 1769480 | tf_op jit(solution)/shard_map/ppermute | solution.py:24
  152.3 25.7 %collective-permute-start.32 = (bf16[4,96,768]{2,1,0:T(8,128)(2,1)}, bf16[4,96,768]{2,1,0:T(8,128)(2,1)S(1)}, u32[]{:S(2)}, u32[]{:S(2)}) collective-permute-start(bf16[4,96,768]{2,1,0:T(8,128)(2,1)} %get-tuple-element.110.refs_9_), channel_id=1, source_target_pairs={{0,16},{4,20},{8,24},{12,28},{16,0},{20,4},{24,8},{28,12},{1,17},{... | collective-permute-start | bytes 1769480 | tf_op jit(solution)/shard_map/ppermute | solution.py:24
  165.4 16.4 %collective-permute-start.38 = (bf16[2,96,768]{2,1,0:T(8,128)(2,1)S(1)}, bf16[2,96,768]{2,1,0:T(8,128)(2,1)S(1)}, u32[]{:S(2)}, u32[]{:S(2)}) collective-permute-start(bf16[2,96,768]{2,1,0:T(8,128)(2,1)S(1)} %get-tuple-element.128), channel_id=1, source_target_pairs={{0,4},{4,0},{8,12},{12,8},{16,20},{20,16},{24,28},{28,24},{1,5},{5... | collective-permute-start | bytes 884744 | tf_op jit(solution)/shard_map/ppermute | solution.py:24
  165.5 17.0 %collective-permute-start.39 = (bf16[2,96,768]{2,1,0:T(8,128)(2,1)S(1)}, bf16[2,96,768]{2,1,0:T(8,128)(2,1)S(1)}, u32[]{:S(2)}, u32[]{:S(2)}) collective-permute-start(bf16[2,96,768]{2,1,0:T(8,128)(2,1)S(1)} %get-tuple-element.129), channel_id=1, source_target_pairs={{0,4},{4,0},{8,12},{12,8},{16,20},{20,16},{24,28},{28,24},{1,5},{5... | collective-permute-start | bytes 884744 | tf_op jit(solution)/shard_map/ppermute | solution.py:24
  166.5 44.1 %collective-permute-start.24 = (bf16[8,96,768]{2,1,0:T(8,128)(2,1)}, bf16[8,96,768]{2,1,0:T(8,128)(2,1)}, u32[]{:S(2)}, u32[]{:S(2)}) collective-permute-start(bf16[8,96,768]{2,1,0:T(8,128)(2,1)} %get-tuple-element.95), channel_id=1, source_target_pairs={{0,4},{4,0},{8,12},{12,8},{16,20},{20,16},{24,28},{28,24},{1,5},{5... | collective-permute-start | bytes 3538952 | tf_op jit(solution)/shard_map/ppermute | solution.py:24
  178.0 16.4 %collective-permute-start.40 = (bf16[4,96,768]{2,1,0:T(8,128)(2,1)}, bf16[4,96,768]{2,1,0:T(8,128)(2,1)}, u32[]{:S(2)}, u32[]{:S(2)}) collective-permute-start(bf16[4,96,768]{2,1,0:T(8,128)(2,1)} %get-tuple-element.130), channel_id=1, source_target_pairs={{0,4},{4,0},{8,12},{12,8},{16,20},{20,16},{24,28},{28,24},{1,5},{5... | collective-permute-start | bytes 1769480 | tf_op jit(solution)/shard_map/ppermute | solution.py:24
  178.0 16.3 %collective-permute-start.41 = (bf16[4,96,768]{2,1,0:T(8,128)(2,1)}, bf16[4,96,768]{2,1,0:T(8,128)(2,1)}, u32[]{:S(2)}, u32[]{:S(2)}) collective-permute-start(bf16[4,96,768]{2,1,0:T(8,128)(2,1)} %get-tuple-element.131), channel_id=1, source_target_pairs={{0,4},{4,0},{8,12},{12,8},{16,20},{20,16},{24,28},{28,24},{1,5},{5... | collective-permute-start | bytes 1769480 | tf_op jit(solution)/shard_map/ppermute | solution.py:24
  181.8 15.8 %collective-permute-start.33 = (bf16[4,96,768]{2,1,0:T(8,128)(2,1)}, bf16[4,96,768]{2,1,0:T(8,128)(2,1)S(1)}, u32[]{:S(2)}, u32[]{:S(2)}) collective-permute-start(bf16[4,96,768]{2,1,0:T(8,128)(2,1)} %get-tuple-element.112.refs_21_), channel_id=1, source_target_pairs={{0,8},{4,12},{8,0},{12,4},{16,24},{20,28},{24,16},{28,20},{1,9},{5... | collective-permute-start | bytes 1769480 | tf_op jit(solution)/shard_map/ppermute | solution.py:24
  182.5 15.4 %collective-permute-start.34 = (bf16[4,96,768]{2,1,0:T(8,128)(2,1)S(1)}, bf16[4,96,768]{2,1,0:T(8,128)(2,1)}, u32[]{:S(2)}, u32[]{:S(2)}) collective-permute-start(bf16[4,96,768]{2,1,0:T(8,128)(2,1)S(1)} %get-tuple-element.113.refs_22_), channel_id=1, source_target_pairs={{0,16},{4,20},{8,24},{12,28},{16,0},{20,4},{24,8},{28,12},{1,17},{... | collective-permute-start | bytes 1769480 | tf_op jit(solution)/shard_map/ppermute | solution.py:24
  183.1 19.8 %all-to-all-start.4 = ((bf16[4,64,768]{2,1,0:T(8,128)(2,1)}), bf16[4,64,768]{2,1,0:T(8,128)(2,1)}, u32[]{:S(2)}, u32[]{:S(2)}) async-start(bf16[4,64,768]{2,1,0:T(8,128)(2,1)} %bitcast.12), calls=%async_computation.4 | async-start | bytes 786432 | tf_op jit(solution)/shard_map/all_to_all | solution.py:687
  202.9 30.7 %all-to-all-start.5 = ((bf16[4,80,768]{2,1,0:T(8,128)(2,1)}), bf16[4,80,768]{2,1,0:T(8,128)(2,1)}, u32[]{:S(2)}, u32[]{:S(2)}) async-start(bf16[4,80,768]{2,1,0:T(8,128)(2,1)} %after.5), calls=%async_computation.5 | async-start | bytes 983040 | tf_op jit(solution)/shard_map/all_to_all | solution.py:893
  207.9 23.4 %collective-permute-start.42 = (bf16[4,96,768]{2,1,0:T(8,128)(2,1)}, bf16[4,96,768]{2,1,0:T(8,128)(2,1)S(1)}, u32[]{:S(2)}, u32[]{:S(2)}) collective-permute-start(bf16[4,96,768]{2,1,0:T(8,128)(2,1)} %get-tuple-element.141), channel_id=1, source_target_pairs={{0,4},{4,0},{8,12},{12,8},{16,20},{20,16},{24,28},{28,24},{1,5},{5... | collective-permute-start | bytes 1769480 | tf_op jit(solution)/shard_map/ppermute | solution.py:24
  207.9 9.9 %collective-permute-start.43 = (bf16[2,96,768]{2,1,0:T(8,128)(2,1)S(1)}, bf16[2,96,768]{2,1,0:T(8,128)(2,1)S(1)}, u32[]{:S(2)}, u32[]{:S(2)}) collective-permute-start(bf16[2,96,768]{2,1,0:T(8,128)(2,1)S(1)} %copy-done.43), channel_id=1, source_target_pairs={{0,16},{4,20},{8,24},{12,28},{16,0},{20,4},{24,8},{28,12},{1,17},{... | collective-permute-start | bytes 884744 | tf_op jit(solution)/shard_map/ppermute | solution.py:24
  208.5 11.2 %collective-permute-start.44 = (bf16[2,96,768]{2,1,0:T(8,128)(2,1)S(1)}, bf16[2,96,768]{2,1,0:T(8,128)(2,1)S(1)}, u32[]{:S(2)}, u32[]{:S(2)}) collective-permute-start(bf16[2,96,768]{2,1,0:T(8,128)(2,1)S(1)} %copy-done.41), channel_id=1, source_target_pairs={{0,8},{4,12},{8,0},{12,4},{16,24},{20,28},{24,16},{28,20},{1,9},{5... | collective-permute-start | bytes 884744 | tf_op jit(solution)/shard_map/ppermute | solution.py:24
  209.4 14.6 %collective-permute-start.45 = (bf16[2,96,768]{2,1,0:T(8,128)(2,1)S(1)}, bf16[2,96,768]{2,1,0:T(8,128)(2,1)S(1)}, u32[]{:S(2)}, u32[]{:S(2)}) collective-permute-start(bf16[2,96,768]{2,1,0:T(8,128)(2,1)S(1)} %copy-done.39), channel_id=1, source_target_pairs={{0,8},{4,12},{8,0},{12,4},{16,24},{20,28},{24,16},{28,20},{1,9},{5... | collective-permute-start | bytes 884744 | tf_op jit(solution)/shard_map/ppermute | solution.py:24
  210.6 17.2 %collective-permute-start.46 = (bf16[2,96,768]{2,1,0:T(8,128)(2,1)S(1)}, bf16[2,96,768]{2,1,0:T(8,128)(2,1)S(1)}, u32[]{:S(2)}, u32[]{:S(2)}) collective-permute-start(bf16[2,96,768]{2,1,0:T(8,128)(2,1)S(1)} %copy-done.37), channel_id=1, source_target_pairs={{0,16},{4,20},{8,24},{12,28},{16,0},{20,4},{24,8},{28,12},{1,17},{... | collective-permute-start | bytes 884744 | tf_op jit(solution)/shard_map/ppermute | solution.py:24
  217.8 21.6 %collective-permute-start.35 = (bf16[2,96,768]{2,1,0:T(8,128)(2,1)S(1)}, bf16[2,96,768]{2,1,0:T(8,128)(2,1)S(1)}, u32[]{:S(2)}, u32[]{:S(2)}) collective-permute-start(bf16[2,96,768]{2,1,0:T(8,128)(2,1)S(1)} %get-tuple-element.115), channel_id=1, source_target_pairs={{0,1},{1,0},{2,3},{3,2},{4,5},{5,4},{6,7},{7,6},{8,9},{9,8},{10,11... | collective-permute-start | bytes 884744 | tf_op jit(solution)/shard_map/ppermute | solution.py:151
  219.8 23.3 %collective-permute-start.36 = (bf16[2,96,768]{2,1,0:T(8,128)(2,1)S(1)}, bf16[2,96,768]{2,1,0:T(8,128)(2,1)S(1)}, u32[]{:S(2)}, u32[]{:S(2)}) collective-permute-start(bf16[2,96,768]{2,1,0:T(8,128)(2,1)S(1)} %get-tuple-element.116), channel_id=1, source_target_pairs={{0,2},{1,3},{2,0},{3,1},{4,6},{5,7},{6,4},{7,5},{8,10},{9,11},{10,... | collective-permute-start | bytes 884744 | tf_op jit(solution)/shard_map/ppermute | solution.py:151
  223.9 19.1 %collective-permute-start.37 = (bf16[2,96,768]{2,1,0:T(8,128)(2,1)S(1)}, bf16[2,96,768]{2,1,0:T(8,128)(2,1)S(1)}, u32[]{:S(2)}, u32[]{:S(2)}) collective-permute-start(bf16[2,96,768]{2,1,0:T(8,128)(2,1)S(1)} %get-tuple-element.117), channel_id=1, source_target_pairs={{0,3},{1,2},{2,1},{3,0},{4,7},{5,6},{6,5},{7,4},{8,11},{9,10},{10,... | collective-permute-start | bytes 884744 | tf_op jit(solution)/shard_map/ppermute | solution.py:151
  230.5 12.5 %collective-permute-start.47 = (bf16[2,96,768]{2,1,0:T(8,128)(2,1)}, bf16[2,96,768]{2,1,0:T(8,128)(2,1)S(1)}, u32[]{:S(2)}, u32[]{:S(2)}) collective-permute-start(bf16[2,96,768]{2,1,0:T(8,128)(2,1)} %get-tuple-element.142), channel_id=1, source_target_pairs={{0,8},{4,12},{8,0},{12,4},{16,24},{20,28},{24,16},{28,20},{1,9},{5... | collective-permute-start | bytes 884744 | tf_op jit(solution)/shard_map/ppermute | solution.py:24
  232.2 10.8 %collective-permute-start.48 = (bf16[2,96,768]{2,1,0:T(8,128)(2,1)S(1)}, bf16[2,96,768]{2,1,0:T(8,128)(2,1)S(1)}, u32[]{:S(2)}, u32[]{:S(2)}) collective-permute-start(bf16[2,96,768]{2,1,0:T(8,128)(2,1)S(1)} %get-tuple-element.143), channel_id=1, source_target_pairs={{0,16},{4,20},{8,24},{12,28},{16,0},{20,4},{24,8},{28,12},{1,17},{... | collective-permute-start | bytes 884744 | tf_op jit(solution)/shard_map/ppermute | solution.py:24
  235.2 19.7 %all-to-all-start.6 = ((bf16[8,4,3072]{2,1,0:T(4,128)(2,1)}), bf16[8,4,3072]{2,1,0:T(4,128)(2,1)}, u32[]{:S(2)}, u32[]{:S(2)}) async-start(bf16[8,4,3072]{2,1,0:T(4,128)(2,1)} %broadcast_in_dim.14), calls=%async_computation.6 | async-start | bytes 393216 | tf_op jit(solution)/shard_map/all_to_all | solution.py:897
  247.2 22.8 %collective-permute-start.49 = (bf16[96,768]{1,0:T(8,128)(2,1)S(1)}, bf16[96,768]{1,0:T(8,128)(2,1)S(1)}, u32[]{:S(2)}, u32[]{:S(2)}) collective-permute-start(bf16[96,768]{1,0:T(8,128)(2,1)S(1)} %get-tuple-element.145), channel_id=1, source_target_pairs={{0,1},{1,0},{2,3},{3,2},{4,5},{5,4},{6,7},{7,6},{8,9},{9,8},{10,11... | collective-permute-start | bytes 442376 | tf_op jit(solution)/shard_map/ppermute | solution.py:151
  252.5 17.6 %collective-permute-start.50 = (bf16[96,768]{1,0:T(8,128)(2,1)S(1)}, bf16[96,768]{1,0:T(8,128)(2,1)S(1)}, u32[]{:S(2)}, u32[]{:S(2)}) collective-permute-start(bf16[96,768]{1,0:T(8,128)(2,1)S(1)} %get-tuple-element.146), channel_id=1, source_target_pairs={{0,2},{1,3},{2,0},{3,1},{4,6},{5,7},{6,4},{7,5},{8,10},{9,11},{10,... | collective-permute-start | bytes 442376 | tf_op jit(solution)/shard_map/ppermute | solution.py:151
  253.5 16.6 %collective-permute-start.51 = (bf16[96,768]{1,0:T(8,128)(2,1)S(1)}, bf16[96,768]{1,0:T(8,128)(2,1)S(1)}, u32[]{:S(2)}, u32[]{:S(2)}) collective-permute-start(bf16[96,768]{1,0:T(8,128)(2,1)S(1)} %get-tuple-element.147), channel_id=1, source_target_pairs={{0,3},{1,2},{2,1},{3,0},{4,7},{5,6},{6,5},{7,4},{8,11},{9,10},{10,... | collective-permute-start | bytes 442376 | tf_op jit(solution)/shard_map/ppermute | solution.py:151
  258.2 11.1 %all-to-all-start.7 = ((f32[32,4,96]{2,1,0:T(4,128)}), f32[32,4,96]{2,1,0:T(4,128)S(1)}, u32[]{:S(2)}, u32[]{:S(2)}) async-start(f32[32,4,96]{2,1,0:T(4,128)} %get-tuple-element.136.refs_7_), calls=%async_computation.7 | async-start | bytes 131072 | tf_op jit(solution)/shard_map/all_to_all | solution.py:909
  (79 other events, 465.7 us)

commit v3 on v2

--- a/solution.py
+++ b/solution.py
@@ -127,6 +127,23 @@
         + [part(2, 1), (others[2], (1,), (middle,)), high_in],
         [], [half] * 2, [], [], "last_sums", first,
     )
+
+
+def whole_first(kept, others, first=()):
+    whole = jax.ShapeDtypeStruct(kept.shape[1:], BF)
+    return call(
+        whole_kernel, None, jnp.zeros((1,), jnp.int32),
+        [(kept, (3,), (1,)), others[3], others[4], (kept, (1,), (1,)), others[1]],
+        [], [whole, whole], [], [], "whole_sums", first,
+    )
+
+
+def whole_last(kept, others, corner_in, first=()):
+    whole = jax.ShapeDtypeStruct(kept.shape[1:], BF)
+    return call(
+        add_kernel, 3, jnp.zeros((1,), jnp.int32), [(kept, (2,), (1,)), others[2], corner_in],
+        [], [whole], [], [], "whole_last", first,
+    )[0]
 
 
 def cut(over_x, over_y, first=()):
@@ -442,7 +459,7 @@
 
 
 def input_back_kernel(spec, me_ref, tokens_ref, mod_ref, dmiddle_ref, dqkv_ref, sums_ref, gate_ref,
-                      qv_ref, proj_off_ref, up_off_ref, down_off_ref, *rest):
+                      qv_ref, proj_off_ref, up_off_ref, down_off_ref, result_ref, *rest):
     width, tok, chunk, pieces = spec
     refs, rest = rest[: len(pieces)], rest[len(pieces) :]
     packed_ref, weights, dmod, rows, sems = rest
@@ -471,7 +488,8 @@
         rows[2:3, :] = up_off_ref[:, seq * width : (seq + 1) * width]
         rows[3:4, :chunk] = proj_off_ref[:, own]
         rows[3:4, chunk : 2 * chunk] = down_off_ref[:, own]
-        packed_ref[seq, tok:] = rows[...].astype(BF)
+        packed_ref[seq, tok : tok + 16] = rows[...].astype(BF)
+        packed_ref[seq, tok + 16 :] = result_ref[seq * tok : (seq + 1) * tok]
 
 
 def mod_grad_kernel(spec, me_ref, small_ref, cond_ref, matrix_ref, grad_ref, sums_ref, dcond_ref):
@@ -535,6 +553,15 @@
             ]
 
 
+def whole_kernel(spec, me_ref, kept_corner, low_in, high_in, kept_x, other_x, corner, side):
+    middle = low_in.shape[0]
+    for unit in range(2 * middle):
+        source = low_in if unit < middle else high_in
+        value = kept_corner[0, unit].astype(F32) + source[unit % middle].astype(F32)
+        corner[unit] = value.astype(BF)
+        side[unit] = (kept_x[0, unit].astype(F32) + other_x[unit].astype(F32)).astype(BF)
+
+
 def add_kernel(spec, me_ref, *refs):
     outs = refs[len(refs) * spec // (spec + 1) :]
     for index, out in enumerate(outs):
@@ -603,9 +630,10 @@
 
 def final2_kernel(spec, me_ref, *refs):
     width, chunk, wide, n_seq = spec
-    result_in, packed_ref, up_ref, down_ref, result_ref, tokens_ref = refs[n_seq:]
-    result_ref[...] = result_in[...]
-    tokens_ref[...] = packed_ref[:, : tokens_ref.shape[1]]
+    packed_ref, up_ref, down_ref, result_ref, tokens_ref = refs[n_seq:]
+    tok = tokens_ref.shape[1]
+    result_ref[...] = packed_ref[:, tok + 16 :]
+    tokens_ref[...] = packed_ref[:, :tok]
     rows = up_ref.shape[0]
     for index in range(2):
         value = refs[0][index].astype(F32)
@@ -682,9 +710,6 @@
 
     def to_latents(values):
         return lax.all_to_all(values, "seq", 0, 0, tiled=True)
-
-    def to_tokens(values):
-        return lax.all_to_all(values.reshape(n_seq, tok, width), "seq", 0, 0, tiled=True)
 
     shaped = jax.ShapeDtypeStruct
     dma = pltpu.SemaphoreType.DMA
@@ -848,7 +873,6 @@
         first2 = scatter_first(kept2, others2, [datt])
         low2, high2 = swap(first2[0], "dp", 2), swap(first2[1], "dp", 1)
         x_high2, y_low2 = swap(first2[2], "dp", 1), swap(first2[3], "dp", 2)
-        result = to_tokens(result)
     *grads1, dqkv, qv_bias = call(
         attend_back_kernel,
         (width, factor, pairs),
@@ -863,16 +887,14 @@
     )
     if layout.direct:
         kept1, others1 = grads1[0], [swap(g, "dp", 0) for g in grads1[1:]]
-        last2 = scatter_last(kept2, others2, low2, high2, [dqkv, x_high2, y_low2])
-        x_low2, y_high2 = swap(last2[0], "dp", 1), swap(last2[1], "dp", 2)
     assert n_seq == 4 and wide == 4
     (packed,) = call(
         input_back_kernel,
         (width, tok, chunk, spec1),
         me,
-        [tokens, mod, dmiddle, dqkv, sums1, dgate2, qv_bias, proj_bias, up_bias, down_bias],
+        [tokens, mod, dmiddle, dqkv, sums1, dgate2, qv_bias, proj_bias, up_bias, down_bias, result],
         arrays1,
-        [shaped((n_seq, tok + 16, width), BF)],
+        [shaped((n_seq, 2 * tok + 16, width), BF)],
         [],
         [
             pltpu.VMEM((3, blocks, block_rows, width), BF),
@@ -881,17 +903,18 @@
             dma((n1,)),
         ],
         "input_back",
-        list(last2) if layout.direct else (),
+        (),
         4 * 10**9,
     )
 
     if layout.direct:
-        first1 = scatter_first(kept1, others1, [x_low2, y_high2])
-        low1, high1 = swap(first1[0], "dp", 2), swap(first1[1], "dp", 1)
-        x_high1, y_low1 = swap(first1[2], "dp", 1), swap(first1[3], "dp", 2)
-        (packed,) = after([packed], list(first1) + [result])
+        last2 = scatter_last(kept2, others2, low2, high2, [dqkv, x_high2, y_low2, packed])
+        x_low2, y_high2 = swap(last2[0], "dp", 1), swap(last2[1], "dp", 2)
     packed = lax.all_to_all(packed, "seq", 0, 0, tiled=True)
-    token_grad = packed[:, :tok]
+    if layout.direct:
+        first1 = whole_first(kept1, others1, [x_low2, y_high2])
+        corner1, over_x1 = swap(first1[0], "dp", 1), swap(first1[1], "dp", 1)
+    token_grad, result = packed[:, :tok], packed[:, tok + 16 :]
     small = packed[:, tok : tok + 4].reshape(n_seq, 4 * width)
     small = jnp.broadcast_to(small[None], (n_dp,) + small.shape)
     small = lax.all_to_all(small, "dp", 0, 0, tiled=True).reshape(n_dp * held, 4 * width)
@@ -915,12 +938,12 @@
             [pltpu.VMEM((n_seq, 2, rows, width), BF), dma((n_seq,))], "collect2",
         )
         over_z2 = swap_seq(blocks2[1:])
-        last1 = scatter_last(kept1, others1, low1, high1, [blocks2[0], x_high1, y_low1])
-        x_low1, y_high1 = swap(last1[0], "dp", 1), swap(last1[1], "dp", 2)
-    if layout.direct:
+        last1 = whole_last(kept1, others1, corner1, [blocks2[0]])
+        over_y1 = swap(last1, "dp", 2)
         blocks1 = call(
             collect1_kernel, spec_seq, here,
-            [(kept1, (0,), (1,)), others1[0], x_low1, x_high1, y_low1, y_high1], [], [],
+            [(kept1, (0,), (1,)), others1[0]]
+            + [(v, (half,), (2,)) for v in (over_x1, over_y1) for half in range(2)], [], [],
             [shaped((rows, width), BF)] * n_seq,
             [pltpu.VMEM((n_seq, rows, width), BF), dma((n_seq,))], "collect1", over_z2,
         )
@@ -928,7 +951,7 @@
 
     if layout.direct:
         up_out, down_out, result, token_grad = call(
-            final2_kernel, spec_seq, here, [blocks2[0]] + over_z2 + [result, packed], [],
+            final2_kernel, spec_seq, here, [blocks2[0]] + over_z2 + [packed], [],
             [shaped((rows, width), F32), shaped((wide * rows, chunk), F32)]
             + [shaped((held, tok, width), BF)] * 2, [], [], "final2", [dcond_part],
         )
@@ -947,7 +970,6 @@
         t3 = s_down.reshape(wide * rows, n_seq, chunk).transpose(1, 0, 2)
         r1, up_out, down_out = scatter_seq(t1), scatter_seq(t2), scatter_seq(t3)
         qkv_out, proj_out = r1[:, : 3 * chunk], r1[:, 3 * chunk :]
-        result = to_tokens(result)
     dcond = jnp.sum(dcond.reshape(n_dp, n_seq, held, rows), axis=1)
     dcond = dcond.transpose(1, 0, 2).reshape(held, width)
     dconds = jax.vjp(jax.nn.silu, cond_float)[1](dcond)[0].reshape(micro, lats, width)

time: 273 us -> 261 us (0.956)
  starting transfers between devices: 80.1 us -> 69.1 us
  local copies, waits for them, and re-layouts: 33.6 us -> 30.2 us
    ppermute x9, waiting for transfers between devices: 7.21 us -> 16.6 us  [swap_seq(): lax.ppermute(value, 'seq', [(i, i ^ mask + 1) for i in range(count)])]
    ppermute x43 -> x40, waiting for transfers between devices: 50.9 us -> 45.4 us  [swap(): return lax.ppermute(values, axis, [(i, i ^ 1 << bit) for i in range(count)])]
    ppermute x9, starting transfers between devices: 21.6 us -> 16.8 us  [swap_seq(): lax.ppermute(value, 'seq', [(i, i ^ mask + 1) for i in range(count)])]
    all_to_all x1 -> x0, starting transfers between devices: 4.82 us -> none  [to_tokens(): lax.all_to_all(values.reshape(n_seq, tok, width), 'seq', 0, 0, tiled=True)]
    unnamed x141 -> x115, local copies, waits for them, and re-layouts: 22.6 us -> 20.2 us
    ppermute x43 -> x40, starting transfers between devices: 26 us -> 24.9 us  [swap(): return lax.ppermute(values, axis, [(i, i ^ 1 << bit) for i in range(count)])]
  transfers between devices with their start and end apart: 60 -> 56, of which waited for: 21 -> 22; matrix products, arithmetic and copies ran while one was open for 5% -> 4% of each run, Pallas kernels for 20% -> 20%
where the time goes in v3:
time: 261 us; the launch traced here: 260 us
  waiting for transfers between devices  77.9 us (30%)
  Pallas kernels  77.2 us (30%)
  starting transfers between devices  69.1 us (26%)
  local copies, waits for them, and re-layouts  30.2 us (12%)
  other arithmetic  3.87 us (1%)
    pallas_call x20, Pallas kernels, call(): pl.pallas_call(run, grid=(1,), out_shape=far_outs + outs, in_specs=[pl.Bl...  77.2 us
    ppermute x40, waiting for transfers between devices, swap(): return lax.ppermute(values, axis, [(i, i ^ 1 << bit) for i in range(count)])  45.4 us
    ppermute x40, starting transfers between devices, swap(): return lax.ppermute(values, axis, [(i, i ^ 1 << bit) for i in range(count)])  24.9 us
    unnamed x115, local copies, waits for them, and re-layouts  20.2 us
    ppermute x9, starting transfers between devices, swap_seq(): lax.ppermute(value, 'seq', [(i, i ^ mask + 1) for i in range(count)])  16.8 us
    ppermute x9, waiting for transfers between devices, swap_seq(): lax.ppermute(value, 'seq', [(i, i ^ mask + 1) for i in range(count)])  16.6 us
    all_to_all x2, waiting for transfers between devices, to_latents(): return lax.all_to_all(values, 'seq', 0, 0, tiled=True)  7.79 us
    all_to_all x2, starting transfers between devices, to_latents(): return lax.all_to_all(values, 'seq', 0, 0, tiled=True)  7.24 us
  transfers between devices with their start and end apart: 56, of which 22 were waited for; matrix products, arithmetic and copies ran while one was open for 4% of the time, Pallas kernels for 20%

profile of v3, /device:TPU:0, one launch (start us, length us, event | category | flops | bytes accessed | tf_op | source)
XLA Modules:
  0.0 259.7 jit_solution(7783033983797578859)
XLA Ops:
  0.7 3.5 %concatenate.14 = bf16[1536]{0:T(1024)(128)(2,1)S(1)} concatenate(bf16[192]{0:T(256)(128)(2,1)} %param.19, bf16[192]{0:T(256)(128)(2,1)} %param.20, bf16[192]{0:T(256)(128)(2,1)} %param.22, bf16[192]{0:T(256)(128)(2,1)} %param.26, bf16[768]{0:T(1024)(128)(2,1)} %param.24), dimensions={0} | concatenate | bytes 6144 | tf_op jit(solution)/shard_map/concatenate | solution.py:718
  5.2 5.1 %collective-permute-start.3 = (bf16[112,768]{1,0:T(8,128)(2,1)S(1)}, bf16[112,768]{1,0:T(8,128)(2,1)S(1)}, u32[]{:S(2)}, u32[]{:S(2)}) collective-permute-start(bf16[112,768]{1,0:T(8,128)(2,1)S(1)} %fusion.1.refs_1_), channel_id=1, source_target_pairs={{0,3},{1,2},{2,1},{3,0},{4,7},{5,6},{6,5},{7,4},{8,11},{9,10},{10,... | collective-permute-start | bytes 516104 | tf_op jit(solution)/shard_map/ppermute | solution.py:168
  15.2 1.3 copy.42
  16.5 4.0 %all-to-all-start = ((bf16[4,8,96]{2,0,1:T(4,128)(2,1)}), bf16[4,8,96]{2,0,1:T(4,128)(2,1)S(1)}, u32[]{:S(2)}, u32[]{:S(2)}) async-start(bf16[4,8,96]{2,0,1:T(4,128)(2,1)} %copy.42), calls=%async_computation | async-start | bytes 16384 | tf_op jit(solution)/shard_map/all_to_all | solution.py:733
  21.3 3.6 %collective-permute-done.2.refs_2_.refs_3_ = bf16[112,768]{1,0:T(8,128)(2,1)S(1)} collective-permute-done((bf16[112,768]{1,0:T(8,128)(2,1)S(1)}, bf16[112,768]{1,0:T(8,128)(2,1)S(1)}, u32[]{:S(2)}, u32[]{:S(2)}) %collective-permute-start.2) | collective-permute-done | bytes 172064 | tf_op jit(solution)/shard_map/ppermute | solution.py:168
  27.1 3.7 %all-to-all-start.1 = ((f32[8,4,1152]{2,1,0:T(4,128)}), f32[8,4,1152]{2,1,0:T(4,128)S(1)}, u32[]{:S(2)}, u32[]{:S(2)}) async-start(f32[8,4,1152]{2,1,0:T(4,128)} %reshape.97), calls=%async_computation.1 | async-start | bytes 294912 | tf_op jit(solution)/shard_map/all_to_all | solution.py:736
  30.8 5.7 %all-to-all-done.1.refs_2_.refs_5_ = f32[8,4,1152]{2,1,0:T(4,128)S(1)} async-done(((f32[8,4,1152]{2,1,0:T(4,128)}), f32[8,4,1152]{2,1,0:T(4,128)S(1)}, u32[]{:S(2)}, u32[]{:S(2)}) %all-to-all-start.1) | async-done | bytes 147488 | tf_op jit(solution)/shard_map/all_to_all | solution.py:736
  42.9 3.1 %collective-permute-start.5 = (bf16[2,2,96,768]{3,2,1,0:T(8,128)(2,1)S(1)}, bf16[2,2,96,768]{3,2,1,0:T(8,128)(2,1)S(1)}, u32[]{:S(2)}, u32[]{:S(2)}) collective-permute-start(bf16[2,2,96,768]{3,2,1,0:T(8,128)(2,1)S(1)} %pad_maximum_fusion), channel_id=1, source_target_pairs={{0,1},{1,0},{2,3},{3,2},{4,5},{5,4},{6,7},{7,6},{8,9},{9,8},{10,11... | collective-permute-start | bytes 1769480 | tf_op jit(solution)/shard_map/ppermute | solution.py:24
  46.0 10.9 %collective-permute-done.9.refs_2_.refs_8_.refs_20_.refs_16_ = bf16[4,96,768]{2,1,0:T(8,128)(2,1)S(1)} collective-permute-done((bf16[4,96,768]{2,1,0:T(8,128)(2,1)}, bf16[4,96,768]{2,1,0:T(8,128)(2,1)S(1)}, u32[]{:S(2)}, u32[]{:S(2)}) %collective-permute-start.9) | collective-permute-done | bytes 589856 | tf_op jit(solution)/shard_map/ppermute | solution.py:24
  57.0 1.6 collective-permute-done.5.refs_3_
  60.3 1.5 collective-permute-start.11
  61.7 1.4 collective-permute-start.13
  65.0 3.6 %all-to-all-start.2 = ((bf16[4,80,768]{2,1,0:T(8,128)(2,1)}), bf16[4,80,768]{2,1,0:T(8,128)(2,1)S(1)}, u32[]{:S(2)}, u32[]{:S(2)}) async-start(bf16[4,80,768]{2,1,0:T(8,128)(2,1)} %copy-done.10), calls=%async_computation.2 | async-start | bytes 983040 | tf_op jit(solution)/shard_map/all_to_all | solution.py:712
  69.1 1.4 spread2.1.refs_6_
  71.0 1.3 collective-permute-start.16
  72.9 7.8 %all-to-all-done.2.refs_1_.refs_2_ = bf16[4,80,768]{2,1,0:T(8,128)(2,1)S(1)} async-done(((bf16[4,80,768]{2,1,0:T(8,128)(2,1)}), bf16[4,80,768]{2,1,0:T(8,128)(2,1)S(1)}, u32[]{:S(2)}, u32[]{:S(2)}) %all-to-all-start.2) | async-done | bytes 491552 | tf_op jit(solution)/shard_map/all_to_all | solution.py:712
  82.6 3.6 %all-to-all-start.3 = ((bf16[4,64,768]{2,1,0:T(8,128)(2,1)}), bf16[4,64,768]{2,1,0:T(8,128)(2,1)S(1)}, u32[]{:S(2)}, u32[]{:S(2)}) async-start(bf16[4,64,768]{2,1,0:T(8,128)(2,1)} %bitcast.10), calls=%async_computation.3 | async-start | bytes 786432 | tf_op jit(solution)/shard_map/all_to_all | solution.py:712
  89.0 7.9 %attention.1 = (bf16[256,768]{1,0:T(8,128)(2,1)S(1)}, bf16[3,256,768]{2,1,0:T(8,128)(2,1)}, bf16[256,768]{1,0:T(8,128)(2,1)S(1)}, f32[256,768]{1,0:T(8,128)}, f3...) custom-call(s32[1]{0:T(128)} %bitcast.1.refs_0_, bf16[4,80,768]{2,1,0:T(8,128)(2,1)} %copy-done.7, ...), custom_call_target="tpu_custom_call" | custom-call | tf_op jit(solution)/shard_map/attention/pallas_call | solution.py:667
  97.7 1.6 cut.3
  101.2 13.6 %collective-permute-done.20.refs_12_ = bf16[4,96,768]{2,1,0:T(8,128)(2,1)S(1)} collective-permute-done((bf16[4,96,768]{2,1,0:T(8,128)(2,1)S(1)}, bf16[4,96,768]{2,1,0:T(8,128)(2,1)S(1)}, u32[]{:S(2)}, u32[]{:S(2)}) %collective-permute-start.20) | collective-permute-done | bytes 589856 | tf_op jit(solution)/shard_map/ppermute | solution.py:24
  118.5 17.1 %mlp.1 = (bf16[4,8,96,768]{3,2,1,0:T(8,128)(2,1)}, bf16[8,96,768]{2,1,0:T(8,128)(2,1)}, bf16[8,96,768]{2,1,0:T(8,128)(2,1)}, bf16[8,96,768]{2,1,0:T(8,128)(2,1)}...) custom-call(s32[1]{0:T(128)} %bitcast.1.refs_0_, ...), custom_call_target="tpu_custom_call" | custom-call | tf_op jit(solution)/shard_map/mlp/pallas_call | solution.py:667
  136.7 7.7 %middle_back.1 = (f32[256,768]{1,0:T(8,128)}, bf16[256,768]{1,0:T(8,128)(2,1)S(1)}, bf16[256,768]{1,0:T(8,128)(2,1)S(1)}, f32[1,2304]{1,0:T(1,128)S(1)}, f32[1,768]{1,0:T(1,128)S(1)}) custom-call(s32[1]{0:T(128)} %bitcast.1.refs_0_, f32[256,768]{1,0:T(8,128)} %get-tuple-element.84.refs_3_.refs_1_, f32[1,4608]{1,0:T(1,128)S(1)} %get-tuple-element.85.refs_2_, ...), custom_call_target="tpu_custom_call" | custom-call | tf_op jit(solution)/shard_map/middle_back/pallas_call | solution.py:667
  146.3 3.6 %first_sums.1 = (bf16[4,96,768]{2,1,0:T(8,128)(2,1)S(1)}, bf16[4,96,768]{2,1,0:T(8,128)(2,1)S(1)}, bf16[4,96,768]{2,1,0:T(8,128)(2,1)}, bf16[4,96,768]{2,1,0:T(8,128)(2,1)}) custom-call(s32[1]{0:T(128)} %constant.21.clone.1.refs_0_, bf16[4,8,96,768]{3,2,1,0:T(8,128)(2,1)} %get-tuple-element.90.refs_1_.refs_3_.refs_5_.refs_7_.refs_4_, ...), custom_call_target="tpu_custom_call" | custom-call | tf_op jit(solution)/shard_map/first_sums/pallas_call | solution.py:667
  149.9 1.5 collective-permute-start.29
  152.1 1.3 collective-permute-start.31
  154.0 12.7 %attention_back.1 = (bf16[4,4,96,768]{3,2,1,0:T(8,128)(2,1)}, bf16[4,96,768]{2,1,0:T(8,128)(2,1)}, bf16[4,96,768]{2,1,0:T(8,128)(2,1)}, bf16[4,96,768]{2,1,0:T(8...) custom-call(s32[1]{0:T(128)} %bitcast.1.refs_0_, ...), custom_call_target="tpu_custom_call" | custom-call | tf_op jit(solution)/shard_map/attention_back/pallas_call | solution.py:667
  167.3 5.7 %input_back.1.refs_10_ = bf16[4,144,768]{2,1,0:T(8,128)(2,1)} custom-call(s32[1]{0:T(128)} %bitcast.1.refs_0_, bf16[256,768]{1,0:T(8,128)(2,1)S(1)} %copy-done.32, f32[1,4608]{1,0:T(1,128)S(1)} %get-tuple-element.85.refs_2_, f32[256,768]{1,0:T(8,128)} %get-tuple-element.109.refs_3_, bf16[3,256,768]{2,1,0:T(8,128)(2,1)} %get-tuple-element.107.refs_4_.refs_7_, ...), custom_call_target="tpu_custom_call" | custom-call | flops 4000000000 | tf_op jit(solution)/shard_map/input_back/pallas_call | solution.py:667
  173.1 5.0 %all-to-all-start.4 = ((bf16[4,144,768]{2,1,0:T(8,128)(2,1)}), bf16[4,144,768]{2,1,0:T(8,128)(2,1)}, u32[]{:S(2)}, u32[]{:S(2)}) async-start(bf16[4,144,768]{2,1,0:T(8,128)(2,1)} %input_back.1.refs_10_), calls=%async_computation.4 | async-start | bytes 1769472 | tf_op jit(solution)/shard_map/all_to_all | solution.py:913
  179.2 2.2 last_sums.1
  183.1 1.6 collective-permute-done.40.refs_3_
  184.8 11.8 %collective-permute-done.33.refs_3_.refs_6_ = bf16[4,96,768]{2,1,0:T(8,128)(2,1)S(1)} collective-permute-done((bf16[4,96,768]{2,1,0:T(8,128)(2,1)S(1)}, bf16[4,96,768]{2,1,0:T(8,128)(2,1)S(1)}, u32[]{:S(2)}, u32[]{:S(2)}) %collective-permute-start.33) | collective-permute-done | bytes 589856 | tf_op jit(solution)/shard_map/ppermute | solution.py:24
  197.9 2.4 whole_sums.1
  200.2 1.3 collective-permute-start.44
  203.6 3.8 %collect2.1 = (bf16[2,96,768]{2,1,0:T(8,128)(2,1)S(1)}, bf16[2,96,768]{2,1,0:T(8,128)(2,1)}, bf16[2,96,768]{2,1,0:T(8,128)(2,1)}, bf16[2,96,768]{2,1,0:T(8,128)(2,1)S(1)}) custom-call(s32[1]{0:T(128)} %bitcast.refs_0_, bf16[4,8,96,768]{3,2,1,0:T(8,128)(2,1)} %get-tuple-element.90.refs_1_.refs_3_.refs_5_.refs_7_.refs_4_, bf16[8,96,768]{2,1,0:T(8,128)(2,1)} %copy-done.46, ...), custom_call_target="tpu_custom_call" | custom-call | tf_op jit(solution)/shard_map/collect2/pallas_call | solution.py:667
  207.4 2.1 collective-permute-start.35
  209.5 2.4 collective-permute-start.36
  213.5 3.4 %all-to-all-start.5 = ((bf16[8,4,3072]{2,1,0:T(4,128)(2,1)}), bf16[8,4,3072]{2,1,0:T(4,128)(2,1)S(1)}, u32[]{:S(2)}, u32[]{:S(2)}) async-start(bf16[8,4,3072]{2,1,0:T(4,128)(2,1)} %broadcast_in_dim.14), calls=%async_computation.5 | async-start | bytes 393216 | tf_op jit(solution)/shard_map/all_to_all | solution.py:920
  217.3 1.7 collective-permute-start.42
  219.0 1.5 whole_last.1
  220.5 2.0 collective-permute-start.45
  224.7 4.1 %all-to-all-start.6 = ((f32[32,4,96]{2,1,0:T(4,128)}), f32[32,4,96]{2,1,0:T(4,128)S(1)}, u32[]{:S(2)}, u32[]{:S(2)}) async-start(f32[32,4,96]{2,1,0:T(4,128)} %get-tuple-element.123.refs_6_), calls=%async_computation.6 | async-start | bytes 131072 | tf_op jit(solution)/shard_map/all_to_all | solution.py:932
  228.8 4.4 %collective-permute-done.36.refs_3_.refs_8_ = bf16[2,96,768]{2,1,0:T(8,128)(2,1)S(1)} collective-permute-done((bf16[2,96,768]{2,1,0:T(8,128)(2,1)}, bf16[2,96,768]{2,1,0:T(8,128)(2,1)S(1)}, u32[]{:S(2)}, u32[]{:S(2)}) %collective-permute-start.36) | collective-permute-done | bytes 294944 | tf_op jit(solution)/shard_map/ppermute | solution.py:168
  233.2 2.2 final2.1
  238.2 1.4 all-to-all-done.6.refs_5_
  240.6 2.7 %collect1.1 = (bf16[96,768]{1,0:T(8,128)(2,1)S(1)}, bf16[96,768]{1,0:T(8,128)(2,1)S(1)}, bf16[96,768]{1,0:T(8,128)(2,1)S(1)}, bf16[96,768]{1,0:T(8,128)(2,1)S(1)}) custom-call(s32[1]{0:T(128)} %bitcast.refs_0_, bf16[4,4,96,768]{3,2,1,0:T(8,128)(2,1)} %get-tuple-element.128.refs_1_.refs_4_, bf16[4,96,768]{2,1,0:T(8,128)(2,1)} %collective-permute-done.38.refs_2_, ...), custom_call_target="tpu_custom_call" | custom-call | tf_op jit(solution)/shard_map/collect1/pallas_call | solution.py:667
  243.3 4.0 %collective-permute-start.46 = (bf16[96,768]{1,0:T(8,128)(2,1)S(1)}, bf16[96,768]{1,0:T(8,128)(2,1)S(1)}, u32[]{:S(2)}, u32[]{:S(2)}) collective-permute-start(bf16[96,768]{1,0:T(8,128)(2,1)S(1)} %get-tuple-element.137), channel_id=1, source_target_pairs={{0,1},{1,0},{2,3},{3,2},{4,5},{5,4},{6,7},{7,6},{8,9},{9,8},{10,11... | collective-permute-start | bytes 442376 | tf_op jit(solution)/shard_map/ppermute | solution.py:168
  248.3 1.5 collective-permute-start.48
  251.1 7.8 %collective-permute-done.47.refs_3_ = bf16[96,768]{1,0:T(8,128)(2,1)S(1)} collective-permute-done((bf16[96,768]{1,0:T(8,128)(2,1)S(1)}, bf16[96,768]{1,0:T(8,128)(2,1)S(1)}, u32[]{:S(2)}, u32[]{:S(2)}) %collective-permute-start.47) | collective-permute-done | bytes 147488 | tf_op jit(solution)/shard_map/ppermute | solution.py:168
  (223 shorter events, 53.7 us)
Async XLA Ops:
  5.2 16.1 %collective-permute-start.3 = (bf16[112,768]{1,0:T(8,128)(2,1)S(1)}, bf16[112,768]{1,0:T(8,128)(2,1)S(1)}, u32[]{:S(2)}, u32[]{:S(2)}) collective-permute-start(bf16[112,768]{1,0:T(8,128)(2,1)S(1)} %fusion.1.refs_1_), channel_id=1, source_target_pairs={{0,3},{1,2},{2,1},{3,0},{4,7},{5,6},{6,5},{7,4},{8,11},{9,10},{10,... | collective-permute-start | bytes 516104 | tf_op jit(solution)/shard_map/ppermute | solution.py:168
  10.3 14.6 %collective-permute-start.2 = (bf16[112,768]{1,0:T(8,128)(2,1)S(1)}, bf16[112,768]{1,0:T(8,128)(2,1)S(1)}, u32[]{:S(2)}, u32[]{:S(2)}) collective-permute-start(bf16[112,768]{1,0:T(8,128)(2,1)S(1)} %fusion.1.refs_1_), channel_id=1, source_target_pairs={{0,2},{1,3},{2,0},{3,1},{4,6},{5,7},{6,4},{7,5},{8,10},{9,11},{10,... | collective-permute-start | bytes 516104 | tf_op jit(solution)/shard_map/ppermute | solution.py:168
  10.3 14.6 %collective-permute-start.1 = (bf16[112,768]{1,0:T(8,128)(2,1)S(1)}, bf16[112,768]{1,0:T(8,128)(2,1)S(1)}, u32[]{:S(2)}, u32[]{:S(2)}) collective-permute-start(bf16[112,768]{1,0:T(8,128)(2,1)S(1)} %fusion.1.refs_1_), channel_id=1, source_target_pairs={{0,1},{1,0},{2,3},{3,2},{4,5},{5,4},{6,7},{7,6},{8,9},{9,8},{10,11... | collective-permute-start | bytes 516104 | tf_op jit(solution)/shard_map/ppermute | solution.py:168
  16.5 9.7 %all-to-all-start = ((bf16[4,8,96]{2,0,1:T(4,128)(2,1)}), bf16[4,8,96]{2,0,1:T(4,128)(2,1)S(1)}, u32[]{:S(2)}, u32[]{:S(2)}) async-start(bf16[4,8,96]{2,0,1:T(4,128)(2,1)} %copy.42), calls=%async_computation | async-start | bytes 16384 | tf_op jit(solution)/shard_map/all_to_all | solution.py:733
  26.2 16.6 %collective-permute-start.4 = (bf16[2,96,768]{2,1,0:T(8,128)(2,1)}, bf16[2,96,768]{2,1,0:T(8,128)(2,1)S(1)}, u32[]{:S(2)}, u32[]{:S(2)}) collective-permute-start(bf16[2,96,768]{2,1,0:T(8,128)(2,1)} %after.3.refs_1_), channel_id=1, source_target_pairs={{0,2},{1,3},{2,0},{3,1},{4,6},{5,7},{6,4},{7,5},{8,10},{9,11},{10,... | collective-permute-start | bytes 884744 | tf_op jit(solution)/shard_map/ppermute | solution.py:24
  27.1 9.4 %all-to-all-start.1 = ((f32[8,4,1152]{2,1,0:T(4,128)}), f32[8,4,1152]{2,1,0:T(4,128)S(1)}, u32[]{:S(2)}, u32[]{:S(2)}) async-start(f32[8,4,1152]{2,1,0:T(4,128)} %reshape.97), calls=%async_computation.1 | async-start | bytes 294912 | tf_op jit(solution)/shard_map/all_to_all | solution.py:736
  41.7 15.2 %collective-permute-start.9 = (bf16[4,96,768]{2,1,0:T(8,128)(2,1)}, bf16[4,96,768]{2,1,0:T(8,128)(2,1)S(1)}, u32[]{:S(2)}, u32[]{:S(2)}) collective-permute-start(bf16[4,96,768]{2,1,0:T(8,128)(2,1)} %get-tuple-element.81.refs_4_.refs_16_.refs_12_), channel_id=1, source_target_pairs={{0,16},{4,20},{8,24},{12,28},{16,0},{20,4},{24,8},{28,12},{1,17},{... | collective-permute-start | bytes 1769480 | tf_op jit(solution)/shard_map/ppermute | solution.py:24
  42.2 14.8 %collective-permute-start.7 = (bf16[4,96,768]{2,1,0:T(8,128)(2,1)}, bf16[4,96,768]{2,1,0:T(8,128)(2,1)S(1)}, u32[]{:S(2)}, u32[]{:S(2)}) collective-permute-start(bf16[4,96,768]{2,1,0:T(8,128)(2,1)} %get-tuple-element.81.refs_4_.refs_16_.refs_12_), channel_id=1, source_target_pairs={{0,8},{4,12},{8,0},{12,4},{16,24},{20,28},{24,16},{28,20},{1,9},{5... | collective-permute-start | bytes 1769480 | tf_op jit(solution)/shard_map/ppermute | solution.py:24
  42.9 15.7 %collective-permute-start.5 = (bf16[2,2,96,768]{3,2,1,0:T(8,128)(2,1)S(1)}, bf16[2,2,96,768]{3,2,1,0:T(8,128)(2,1)S(1)}, u32[]{:S(2)}, u32[]{:S(2)}) collective-permute-start(bf16[2,2,96,768]{3,2,1,0:T(8,128)(2,1)S(1)} %pad_maximum_fusion), channel_id=1, source_target_pairs={{0,1},{1,0},{2,3},{3,2},{4,5},{5,4},{6,7},{7,6},{8,9},{9,8},{10,11... | collective-permute-start | bytes 1769480 | tf_op jit(solution)/shard_map/ppermute | solution.py:24
  60.3 8.4 %collective-permute-start.11 = (bf16[2,96,768]{2,1,0:T(8,128)(2,1)}, bf16[2,96,768]{2,1,0:T(8,128)(2,1)S(1)}, u32[]{:S(2)}, u32[]{:S(2)}) collective-permute-start(bf16[2,96,768]{2,1,0:T(8,128)(2,1)} %get-tuple-element.82), channel_id=1, source_target_pairs={{0,16},{4,20},{8,24},{12,28},{16,0},{20,4},{24,8},{28,12},{1,17},{... | collective-permute-start | bytes 884744 | tf_op jit(solution)/shard_map/ppermute | solution.py:24
  61.7 7.4 %collective-permute-start.13 = (bf16[2,96,768]{2,1,0:T(8,128)(2,1)}, bf16[2,96,768]{2,1,0:T(8,128)(2,1)S(1)}, u32[]{:S(2)}, u32[]{:S(2)}) collective-permute-start(bf16[2,96,768]{2,1,0:T(8,128)(2,1)} %get-tuple-element.83), channel_id=1, source_target_pairs={{0,8},{4,12},{8,0},{12,4},{16,24},{20,28},{24,16},{28,20},{1,9},{5... | collective-permute-start | bytes 884744 | tf_op jit(solution)/shard_map/ppermute | solution.py:24
  65.0 15.7 %all-to-all-start.2 = ((bf16[4,80,768]{2,1,0:T(8,128)(2,1)}), bf16[4,80,768]{2,1,0:T(8,128)(2,1)S(1)}, u32[]{:S(2)}, u32[]{:S(2)}) async-start(bf16[4,80,768]{2,1,0:T(8,128)(2,1)} %copy-done.10), calls=%async_computation.2 | async-start | bytes 983040 | tf_op jit(solution)/shard_map/all_to_all | solution.py:712
  70.5 27.2 %collective-permute-start.18 = (bf16[8,96,768]{2,1,0:T(8,128)(2,1)}, bf16[8,96,768]{2,1,0:T(8,128)(2,1)}, u32[]{:S(2)}, u32[]{:S(2)}) collective-permute-start(bf16[8,96,768]{2,1,0:T(8,128)(2,1)} %spread2.1.refs_6_), channel_id=1, source_target_pairs={{0,16},{4,20},{8,24},{12,28},{16,0},{20,4},{24,8},{28,12},{1,17},{... | collective-permute-start | bytes 3538952 | tf_op jit(solution)/shard_map/ppermute | solution.py:24
  71.0 26.6 %collective-permute-start.16 = (bf16[8,96,768]{2,1,0:T(8,128)(2,1)}, bf16[8,96,768]{2,1,0:T(8,128)(2,1)}, u32[]{:S(2)}, u32[]{:S(2)}) collective-permute-start(bf16[8,96,768]{2,1,0:T(8,128)(2,1)} %spread2.1.refs_6_), channel_id=1, source_target_pairs={{0,8},{4,12},{8,0},{12,4},{16,24},{20,28},{24,16},{28,20},{1,9},{5... | collective-permute-start | bytes 3538952 | tf_op jit(solution)/shard_map/ppermute | solution.py:24
  72.3 13.9 %collective-permute-start.6 = (bf16[4,96,768]{2,1,0:T(8,128)(2,1)}, bf16[4,96,768]{2,1,0:T(8,128)(2,1)}, u32[]{:S(2)}, u32[]{:S(2)}) collective-permute-start(bf16[4,96,768]{2,1,0:T(8,128)(2,1)} %get-tuple-element.81.refs_4_.refs_16_.refs_12_), channel_id=1, source_target_pairs={{0,4},{4,0},{8,12},{12,8},{16,20},{20,16},{24,28},{28,24},{1,5},{5... | collective-permute-start | bytes 1769480 | tf_op jit(solution)/shard_map/ppermute | solution.py:24
  72.3 13.9 %collective-permute-start.10 = (bf16[4,96,768]{2,1,0:T(8,128)(2,1)S(1)}, bf16[4,96,768]{2,1,0:T(8,128)(2,1)}, u32[]{:S(2)}, u32[]{:S(2)}) collective-permute-start(bf16[4,96,768]{2,1,0:T(8,128)(2,1)S(1)} %collective-permute-done.9.refs_2_.refs_8_.refs_20_.refs_16_), channel_id=1, source_target_pairs={{0,4},{4,0},{8,12},{12,8},{16,20},{20,16},{24,28},{28,24},{1,5},{5... | collective-permute-start | bytes 1769480 | tf_op jit(solution)/shard_map/ppermute | solution.py:24
  72.9 13.9 %collective-permute-start.8 = (bf16[4,96,768]{2,1,0:T(8,128)(2,1)S(1)}, bf16[4,96,768]{2,1,0:T(8,128)(2,1)}, u32[]{:S(2)}, u32[]{:S(2)}) collective-permute-start(bf16[4,96,768]{2,1,0:T(8,128)(2,1)S(1)} %collective-permute-done.7.refs_1_.refs_6_.refs_18_.refs_14_), channel_id=1, source_target_pairs={{0,4},{4,0},{8,12},{12,8},{16,20},{20,16},{24,28},{28,24},{1,5},{5... | collective-permute-start | bytes 1769480 | tf_op jit(solution)/shard_map/ppermute | solution.py:24
  82.6 15.1 %all-to-all-start.3 = ((bf16[4,64,768]{2,1,0:T(8,128)(2,1)}), bf16[4,64,768]{2,1,0:T(8,128)(2,1)S(1)}, u32[]{:S(2)}, u32[]{:S(2)}) async-start(bf16[4,64,768]{2,1,0:T(8,128)(2,1)} %bitcast.10), calls=%async_computation.3 | async-start | bytes 786432 | tf_op jit(solution)/shard_map/all_to_all | solution.py:712
  86.8 28.9 %collective-permute-start.15 = (bf16[8,96,768]{2,1,0:T(8,128)(2,1)}, bf16[8,96,768]{2,1,0:T(8,128)(2,1)}, u32[]{:S(2)}, u32[]{:S(2)}) collective-permute-start(bf16[8,96,768]{2,1,0:T(8,128)(2,1)} %spread2.1.refs_6_), channel_id=1, source_target_pairs={{0,4},{4,0},{8,12},{12,8},{16,20},{20,16},{24,28},{28,24},{1,5},{5... | collective-permute-start | bytes 3538952 | tf_op jit(solution)/shard_map/ppermute | solution.py:24
  99.3 15.4 %collective-permute-start.20 = (bf16[4,96,768]{2,1,0:T(8,128)(2,1)S(1)}, bf16[4,96,768]{2,1,0:T(8,128)(2,1)S(1)}, u32[]{:S(2)}, u32[]{:S(2)}) collective-permute-start(bf16[4,96,768]{2,1,0:T(8,128)(2,1)S(1)} %get-tuple-element.88), channel_id=1, source_target_pairs={{0,16},{4,20},{8,24},{12,28},{16,0},{20,4},{24,8},{28,12},{1,17},{... | collective-permute-start | bytes 1769480 | tf_op jit(solution)/shard_map/ppermute | solution.py:24
  100.0 15.8 %collective-permute-start.19 = (bf16[8,96,768]{2,1,0:T(8,128)(2,1)}, bf16[8,96,768]{2,1,0:T(8,128)(2,1)S(1)}, u32[]{:S(2)}, u32[]{:S(2)}) collective-permute-start(bf16[8,96,768]{2,1,0:T(8,128)(2,1)} %collective-permute-done.18.refs_2_.refs_10_), channel_id=1, source_target_pairs={{0,4},{4,0},{8,12},{12,8},{16,20},{20,16},{24,28},{28,24},{1,5},{5... | collective-permute-start | bytes 3538952 | tf_op jit(solution)/shard_map/ppermute | solution.py:24
  100.0 15.8 %collective-permute-start.17 = (bf16[8,96,768]{2,1,0:T(8,128)(2,1)}, bf16[8,96,768]{2,1,0:T(8,128)(2,1)S(1)}, u32[]{:S(2)}, u32[]{:S(2)}) collective-permute-start(bf16[8,96,768]{2,1,0:T(8,128)(2,1)} %collective-permute-done.16.refs_1_.refs_8_), channel_id=1, source_target_pairs={{0,4},{4,0},{8,12},{12,8},{16,20},{20,16},{24,28},{28,24},{1,5},{5... | collective-permute-start | bytes 3538952 | tf_op jit(solution)/shard_map/ppermute | solution.py:24
  100.5 15.2 %collective-permute-start.22 = (bf16[4,96,768]{2,1,0:T(8,128)(2,1)S(1)}, bf16[4,96,768]{2,1,0:T(8,128)(2,1)S(1)}, u32[]{:S(2)}, u32[]{:S(2)}) collective-permute-start(bf16[4,96,768]{2,1,0:T(8,128)(2,1)S(1)} %get-tuple-element.89), channel_id=1, source_target_pairs={{0,8},{4,12},{8,0},{12,4},{16,24},{20,28},{24,16},{28,20},{1,9},{5... | collective-permute-start | bytes 1769480 | tf_op jit(solution)/shard_map/ppermute | solution.py:24
  135.6 8.9 %collective-permute-start.25 = (bf16[8,96,768]{2,1,0:T(8,128)(2,1)}, bf16[8,96,768]{2,1,0:T(8,128)(2,1)S(1)}, u32[]{:S(2)}, u32[]{:S(2)}) collective-permute-start(bf16[8,96,768]{2,1,0:T(8,128)(2,1)} %get-tuple-element.92), channel_id=1, source_target_pairs={{0,4},{4,0},{8,12},{12,8},{16,20},{20,16},{24,28},{28,24},{1,5},{5... | collective-permute-start | bytes 3538952 | tf_op jit(solution)/shard_map/ppermute | solution.py:24
  135.8 8.6 %collective-permute-start.28 = (bf16[8,96,768]{2,1,0:T(8,128)(2,1)}, bf16[8,96,768]{2,1,0:T(8,128)(2,1)S(1)}, u32[]{:S(2)}, u32[]{:S(2)}) collective-permute-start(bf16[8,96,768]{2,1,0:T(8,128)(2,1)} %get-tuple-element.95), channel_id=1, source_target_pairs={{0,4},{4,0},{8,12},{12,8},{16,20},{20,16},{24,28},{28,24},{1,5},{5... | collective-permute-start | bytes 3538952 | tf_op jit(solution)/shard_map/ppermute | solution.py:24
  136.2 8.2 %collective-permute-start.26 = (bf16[4,96,768]{2,1,0:T(8,128)(2,1)S(1)}, bf16[4,96,768]{2,1,0:T(8,128)(2,1)S(1)}, u32[]{:S(2)}, u32[]{:S(2)}) collective-permute-start(bf16[4,96,768]{2,1,0:T(8,128)(2,1)S(1)} %get-tuple-element.93), channel_id=1, source_target_pairs={{0,4},{4,0},{8,12},{12,8},{16,20},{20,16},{24,28},{28,24},{1,5},{5... | collective-permute-start | bytes 1769480 | tf_op jit(solution)/shard_map/ppermute | solution.py:24
  136.3 8.1 %collective-permute-start.27 = (bf16[4,96,768]{2,1,0:T(8,128)(2,1)S(1)}, bf16[4,96,768]{2,1,0:T(8,128)(2,1)S(1)}, u32[]{:S(2)}, u32[]{:S(2)}) collective-permute-start(bf16[4,96,768]{2,1,0:T(8,128)(2,1)S(1)} %get-tuple-element.94), channel_id=1, source_target_pairs={{0,4},{4,0},{8,12},{12,8},{16,20},{20,16},{24,28},{28,24},{1,5},{5... | collective-permute-start | bytes 1769480 | tf_op jit(solution)/shard_map/ppermute | solution.py:24
  149.9 28.2 %collective-permute-start.29 = (bf16[4,96,768]{2,1,0:T(8,128)(2,1)S(1)}, bf16[4,96,768]{2,1,0:T(8,128)(2,1)S(1)}, u32[]{:S(2)}, u32[]{:S(2)}) collective-permute-start(bf16[4,96,768]{2,1,0:T(8,128)(2,1)S(1)} %get-tuple-element.99.refs_6_), channel_id=1, source_target_pairs={{0,16},{4,20},{8,24},{12,28},{16,0},{20,4},{24,8},{28,12},{1,17},{... | collective-permute-start | bytes 1769480 | tf_op jit(solution)/shard_map/ppermute | solution.py:24
  151.4 27.2 %collective-permute-start.30 = (bf16[4,96,768]{2,1,0:T(8,128)(2,1)S(1)}, bf16[4,96,768]{2,1,0:T(8,128)(2,1)}, u32[]{:S(2)}, u32[]{:S(2)}) collective-permute-start(bf16[4,96,768]{2,1,0:T(8,128)(2,1)S(1)} %get-tuple-element.100.refs_7_), channel_id=1, source_target_pairs={{0,8},{4,12},{8,0},{12,4},{16,24},{20,28},{24,16},{28,20},{1,9},{5... | collective-permute-start | bytes 1769480 | tf_op jit(solution)/shard_map/ppermute | solution.py:24
  152.1 27.1 %collective-permute-start.31 = (bf16[4,96,768]{2,1,0:T(8,128)(2,1)}, bf16[4,96,768]{2,1,0:T(8,128)(2,1)}, u32[]{:S(2)}, u32[]{:S(2)}) collective-permute-start(bf16[4,96,768]{2,1,0:T(8,128)(2,1)} %get-tuple-element.105.refs_8_), channel_id=1, source_target_pairs={{0,8},{4,12},{8,0},{12,4},{16,24},{20,28},{24,16},{28,20},{1,9},{5... | collective-permute-start | bytes 1769480 | tf_op jit(solution)/shard_map/ppermute | solution.py:24
  153.4 25.8 %collective-permute-start.32 = (bf16[4,96,768]{2,1,0:T(8,128)(2,1)}, bf16[4,96,768]{2,1,0:T(8,128)(2,1)}, u32[]{:S(2)}, u32[]{:S(2)}) collective-permute-start(bf16[4,96,768]{2,1,0:T(8,128)(2,1)} %get-tuple-element.106.refs_9_), channel_id=1, source_target_pairs={{0,16},{4,20},{8,24},{12,28},{16,0},{20,4},{24,8},{28,12},{1,17},{... | collective-permute-start | bytes 1769480 | tf_op jit(solution)/shard_map/ppermute | solution.py:24
  173.1 38.9 %all-to-all-start.4 = ((bf16[4,144,768]{2,1,0:T(8,128)(2,1)}), bf16[4,144,768]{2,1,0:T(8,128)(2,1)}, u32[]{:S(2)}, u32[]{:S(2)}) async-start(bf16[4,144,768]{2,1,0:T(8,128)(2,1)} %input_back.1.refs_10_), calls=%async_computation.4 | async-start | bytes 1769472 | tf_op jit(solution)/shard_map/all_to_all | solution.py:913
  178.0 23.5 %collective-permute-start.24 = (bf16[8,96,768]{2,1,0:T(8,128)(2,1)}, bf16[8,96,768]{2,1,0:T(8,128)(2,1)S(1)}, u32[]{:S(2)}, u32[]{:S(2)}) collective-permute-start(bf16[8,96,768]{2,1,0:T(8,128)(2,1)} %get-tuple-element.91), channel_id=1, source_target_pairs={{0,4},{4,0},{8,12},{12,8},{16,20},{20,16},{24,28},{28,24},{1,5},{5... | collective-permute-start | bytes 3538952 | tf_op jit(solution)/shard_map/ppermute | solution.py:24
  181.4 15.2 %collective-permute-start.33 = (bf16[4,96,768]{2,1,0:T(8,128)(2,1)S(1)}, bf16[4,96,768]{2,1,0:T(8,128)(2,1)S(1)}, u32[]{:S(2)}, u32[]{:S(2)}) collective-permute-start(bf16[4,96,768]{2,1,0:T(8,128)(2,1)S(1)} %get-tuple-element.117), channel_id=1, source_target_pairs={{0,8},{4,12},{8,0},{12,4},{16,24},{20,28},{24,16},{28,20},{1,9},{5... | collective-permute-start | bytes 1769480 | tf_op jit(solution)/shard_map/ppermute | solution.py:24
  182.2 14.8 %collective-permute-start.34 = (bf16[4,96,768]{2,1,0:T(8,128)(2,1)S(1)}, bf16[4,96,768]{2,1,0:T(8,128)(2,1)S(1)}, u32[]{:S(2)}, u32[]{:S(2)}) collective-permute-start(bf16[4,96,768]{2,1,0:T(8,128)(2,1)S(1)} %get-tuple-element.118), channel_id=1, source_target_pairs={{0,16},{4,20},{8,24},{12,28},{16,0},{20,4},{24,8},{28,12},{1,17},{... | collective-permute-start | bytes 1769480 | tf_op jit(solution)/shard_map/ppermute | solution.py:24
  184.7 32.2 %collective-permute-start.43 = (bf16[4,96,768]{2,1,0:T(8,128)(2,1)}, bf16[4,96,768]{2,1,0:T(8,128)(2,1)S(1)}, u32[]{:S(2)}, u32[]{:S(2)}) collective-permute-start(bf16[4,96,768]{2,1,0:T(8,128)(2,1)} %get-tuple-element.134), channel_id=1, source_target_pairs={{0,4},{4,0},{8,12},{12,8},{16,20},{20,16},{24,28},{28,24},{1,5},{5... | collective-permute-start | bytes 1769480 | tf_op jit(solution)/shard_map/ppermute | solution.py:24
  200.2 17.1 %collective-permute-start.44 = (bf16[4,96,768]{2,1,0:T(8,128)(2,1)S(1)}, bf16[4,96,768]{2,1,0:T(8,128)(2,1)}, u32[]{:S(2)}, u32[]{:S(2)}) collective-permute-start(bf16[4,96,768]{2,1,0:T(8,128)(2,1)S(1)} %get-tuple-element.135), channel_id=1, source_target_pairs={{0,8},{4,12},{8,0},{12,4},{16,24},{20,28},{24,16},{28,20},{1,9},{5... | collective-permute-start | bytes 1769480 | tf_op jit(solution)/shard_map/ppermute | solution.py:24
  207.4 13.1 %collective-permute-start.35 = (bf16[2,96,768]{2,1,0:T(8,128)(2,1)}, bf16[2,96,768]{2,1,0:T(8,128)(2,1)S(1)}, u32[]{:S(2)}, u32[]{:S(2)}) collective-permute-start(bf16[2,96,768]{2,1,0:T(8,128)(2,1)} %get-tuple-element.120), channel_id=1, source_target_pairs={{0,1},{1,0},{2,3},{3,2},{4,5},{5,4},{6,7},{7,6},{8,9},{9,8},{10,11... | collective-permute-start | bytes 884744 | tf_op jit(solution)/shard_map/ppermute | solution.py:168
  209.5 23.7 %collective-permute-start.36 = (bf16[2,96,768]{2,1,0:T(8,128)(2,1)}, bf16[2,96,768]{2,1,0:T(8,128)(2,1)S(1)}, u32[]{:S(2)}, u32[]{:S(2)}) collective-permute-start(bf16[2,96,768]{2,1,0:T(8,128)(2,1)} %get-tuple-element.121), channel_id=1, source_target_pairs={{0,2},{1,3},{2,0},{3,1},{4,6},{5,7},{6,4},{7,5},{8,10},{9,11},{10,... | collective-permute-start | bytes 884744 | tf_op jit(solution)/shard_map/ppermute | solution.py:168
  211.9 21.3 %collective-permute-start.37 = (bf16[2,96,768]{2,1,0:T(8,128)(2,1)S(1)}, bf16[2,96,768]{2,1,0:T(8,128)(2,1)S(1)}, u32[]{:S(2)}, u32[]{:S(2)}) collective-permute-start(bf16[2,96,768]{2,1,0:T(8,128)(2,1)S(1)} %get-tuple-element.122), channel_id=1, source_target_pairs={{0,3},{1,2},{2,1},{3,0},{4,7},{5,6},{6,5},{7,4},{8,11},{9,10},{10,... | collective-permute-start | bytes 884744 | tf_op jit(solution)/shard_map/ppermute | solution.py:168
  213.5 10.0 %all-to-all-start.5 = ((bf16[8,4,3072]{2,1,0:T(4,128)(2,1)}), bf16[8,4,3072]{2,1,0:T(4,128)(2,1)S(1)}, u32[]{:S(2)}, u32[]{:S(2)}) async-start(bf16[8,4,3072]{2,1,0:T(4,128)(2,1)} %broadcast_in_dim.14), calls=%async_computation.5 | async-start | bytes 393216 | tf_op jit(solution)/shard_map/all_to_all | solution.py:920
  216.9 22.8 %collective-permute-start.38 = (bf16[4,96,768]{2,1,0:T(8,128)(2,1)}, bf16[4,96,768]{2,1,0:T(8,128)(2,1)}, u32[]{:S(2)}, u32[]{:S(2)}) collective-permute-start(bf16[4,96,768]{2,1,0:T(8,128)(2,1)} %get-tuple-element.129), channel_id=1, source_target_pairs={{0,4},{4,0},{8,12},{12,8},{16,20},{20,16},{24,28},{28,24},{1,5},{5... | collective-permute-start | bytes 1769480 | tf_op jit(solution)/shard_map/ppermute | solution.py:24
  217.3 22.4 %collective-permute-start.42 = (bf16[4,96,768]{2,1,0:T(8,128)(2,1)}, bf16[4,96,768]{2,1,0:T(8,128)(2,1)}, u32[]{:S(2)}, u32[]{:S(2)}) collective-permute-start(bf16[4,96,768]{2,1,0:T(8,128)(2,1)} %get-tuple-element.133), channel_id=1, source_target_pairs={{0,8},{4,12},{8,0},{12,4},{16,24},{20,28},{24,16},{28,20},{1,9},{5... | collective-permute-start | bytes 1769480 | tf_op jit(solution)/shard_map/ppermute | solution.py:24
  220.5 19.2 %collective-permute-start.45 = (bf16[4,96,768]{2,1,0:T(8,128)(2,1)S(1)}, bf16[4,96,768]{2,1,0:T(8,128)(2,1)S(1)}, u32[]{:S(2)}, u32[]{:S(2)}) collective-permute-start(bf16[4,96,768]{2,1,0:T(8,128)(2,1)S(1)} %whole_last.1), channel_id=1, source_target_pairs={{0,16},{4,20},{8,24},{12,28},{16,0},{20,4},{24,8},{28,12},{1,17},{... | collective-permute-start | bytes 1769480 | tf_op jit(solution)/shard_map/ppermute | solution.py:24
  224.7 14.9 %all-to-all-start.6 = ((f32[32,4,96]{2,1,0:T(4,128)}), f32[32,4,96]{2,1,0:T(4,128)S(1)}, u32[]{:S(2)}, u32[]{:S(2)}) async-start(f32[32,4,96]{2,1,0:T(4,128)} %get-tuple-element.123.refs_6_), calls=%async_computation.6 | async-start | bytes 131072 | tf_op jit(solution)/shard_map/all_to_all | solution.py:932
  243.3 7.8 %collective-permute-start.46 = (bf16[96,768]{1,0:T(8,128)(2,1)S(1)}, bf16[96,768]{1,0:T(8,128)(2,1)S(1)}, u32[]{:S(2)}, u32[]{:S(2)}) collective-permute-start(bf16[96,768]{1,0:T(8,128)(2,1)S(1)} %get-tuple-element.137), channel_id=1, source_target_pairs={{0,1},{1,0},{2,3},{3,2},{4,5},{5,4},{6,7},{7,6},{8,9},{9,8},{10,11... | collective-permute-start | bytes 442376 | tf_op jit(solution)/shard_map/ppermute | solution.py:168
  247.4 11.6 %collective-permute-start.47 = (bf16[96,768]{1,0:T(8,128)(2,1)S(1)}, bf16[96,768]{1,0:T(8,128)(2,1)S(1)}, u32[]{:S(2)}, u32[]{:S(2)}) collective-permute-start(bf16[96,768]{1,0:T(8,128)(2,1)S(1)} %get-tuple-element.138), channel_id=1, source_target_pairs={{0,2},{1,3},{2,0},{3,1},{4,6},{5,7},{6,4},{7,5},{8,10},{9,11},{10,... | collective-permute-start | bytes 442376 | tf_op jit(solution)/shard_map/ppermute | solution.py:168
  248.3 10.6 %collective-permute-start.48 = (bf16[96,768]{1,0:T(8,128)(2,1)S(1)}, bf16[96,768]{1,0:T(8,128)(2,1)S(1)}, u32[]{:S(2)}, u32[]{:S(2)}) collective-permute-start(bf16[96,768]{1,0:T(8,128)(2,1)S(1)} %get-tuple-element.139), channel_id=1, source_target_pairs={{0,3},{1,2},{2,1},{3,0},{4,7},{5,6},{6,5},{7,4},{8,11},{9,10},{10,... | collective-permute-start | bytes 442376 | tf_op jit(solution)/shard_map/ppermute | solution.py:168
  (62 other events, 310.9 us)
